TPU v7x, 32 devices: a whole 2x2x4 slice. The times are simulated.
32 devices in a mesh: chan: 16 (over z, x, core), win: 2 (over y).
Axes of the slice: x: 2, y: 2, z: 4, core: 2. Of those that a mesh axis runs over, the one named last changes fastest.
Arguments:
- records: bfloat16 [8, 8192, 512], P('win', 'chan'), may hold values from -6 to 6
- block_pairs: int32 [512, 2], P('chan'), may hold values from 0 to 63, as said below
- lag_low: int32 [512], P('chan'), may hold values from 0 to 31
- lag_high: int32 [512], P('chan'), may hold values from 97 to 128
- slot_count: int32 [16], P('chan'), may hold values from 1 to 32, as said below
Outputs:
- stacks: float32 [512, 128, 128], P(('chan', 'win'))
Inputs may be any that keep to these rules, and one draw needn't show every extreme that they name: `block_pairs`: slot p belongs to owner p // 32; for owner o both blocks of each slot lie within o * 4 - 16 to o * 4 + 19, and the two blocks differ by at most 16. Slots of owner o at or after slot_count[o] are unused; some owner uses all 32.
All inputs are finite; a program needn't handle non-finite values.
Results may differ from a plain program's by a relative error of at most 0.0015.
Values may be sent and summed in bfloat16 or wider, within the bound.
No kernel may reach another device: no remote copies, remote signals or barrier semaphores. Data moves between devices by JAX's collectives and lax.ppermute only.
A program may use at most 128 MiB of HBM per device.

v0:
```python
import math

import jax
import jax.numpy as jnp
from jax import lax
from jax.sharding import PartitionSpec as P

BLOCK = 128
F = 128
LAGS = 128
REACH = 16
B_DEV = 4


def shifted(block, axis, distance):
    devices = range(lax.axis_size(axis))
    route = [(i - distance, i) for i in devices if i - distance in devices]
    return lax.ppermute(block, axis, route)


def forward_table(length, bins):
    first = length // 32
    times = jnp.arange(length, dtype=jnp.int32)[:, None]
    freqs = (first + jnp.arange(bins, dtype=jnp.int32))[None, :]
    phase = 2.0 * math.pi / length * (times * freqs % length).astype(jnp.float32)
    return jnp.concatenate([jnp.cos(phase), -jnp.sin(phase)], axis=1).astype(jnp.bfloat16)


def inverse_table(length, bins, lag_total):
    first = length // 32
    freqs = (first + jnp.arange(bins, dtype=jnp.int32))[:, None]
    shifts = (jnp.arange(lag_total, dtype=jnp.int32) - lag_total // 2)[None, :]
    phase = 2.0 * math.pi / length * (freqs * shifts % length).astype(jnp.float32)
    return jnp.concatenate([jnp.cos(phase), -jnp.sin(phase)], axis=0)


def whiten(spectra, bins):
    real_part = spectra[..., :bins]
    imag_part = spectra[..., bins:]
    power = real_part * real_part + imag_part * imag_part
    level = jnp.mean(power, axis=-1, keepdims=True)
    factor = lax.rsqrt(power + 0.1 * level + 1e-06)
    return jnp.concatenate([real_part * factor, imag_part * factor], axis=-1).astype(jnp.bfloat16)


def pair_products(first, second, bins):
    first_re, first_im = (first[..., :bins], first[..., bins:])
    second_re, second_im = (second[..., :bins], second[..., bins:])
    form = "spbf,spbf->pbf"
    real_sum = jnp.einsum(
        form, first_re, second_re, preferred_element_type=jnp.float32
    ) + jnp.einsum(form, first_im, second_im, preferred_element_type=jnp.float32)
    imag_sum = jnp.einsum(
        form, first_re, second_im, preferred_element_type=jnp.float32
    ) - jnp.einsum(form, first_im, second_re, preferred_element_type=jnp.float32)
    return jnp.concatenate([real_sum, imag_sum], axis=-1)


def per_device(records, block_pairs, lag_low, lag_high, slot_count):
    seg_count, chan_count, length = records.shape
    forward = forward_table(length, F)
    spectra = jnp.dot(
        records.reshape(seg_count * chan_count, length), forward, preferred_element_type=jnp.float32
    )
    whitened = whiten(spectra.reshape(seg_count, chan_count, 2 * F), F)
    depth = REACH // B_DEV
    pieces = []
    for offset in range(-depth, depth + 1):
        if offset == 0:
            pieces.append(whitened)
        else:
            pieces.append(shifted(whitened, "chan", -offset))
    neighbourhood = jnp.concatenate(pieces, axis=1)
    blocks = neighbourhood.reshape(seg_count, neighbourhood.shape[1] // BLOCK, BLOCK, 2 * F)
    base = (lax.axis_index("chan") - depth) * B_DEV
    slot_total = block_pairs.shape[0]
    groups = 4
    local_pairs = (block_pairs - base).reshape(groups, slot_total // groups, 2)

    def one_group(pair_rows):
        first = jnp.take(blocks, pair_rows[:, 0], axis=1)
        second = jnp.take(blocks, pair_rows[:, 1], axis=1)
        return pair_products(first, second, F)

    spectrum = lax.map(one_group, local_pairs).reshape(slot_total, BLOCK, 2 * F)
    inverse = inverse_table(length, F, LAGS)
    factor = 1.0 / math.sqrt(F * seg_count * lax.axis_size("win"))
    lag_index = jnp.arange(LAGS, dtype=jnp.int32)
    summed = lax.psum_scatter(spectrum, "win", scatter_dimension=0, tiled=True)
    share = summed.shape[0]
    start = lax.axis_index("win") * share
    slot_index = start + jnp.arange(share, dtype=jnp.int32)
    low = lax.dynamic_slice_in_dim(lag_low, start, share)
    high = lax.dynamic_slice_in_dim(lag_high, start, share)
    stack = (
        jnp.einsum(
            "pbf,fl->pbl",
            summed,
            inverse,
            precision=lax.Precision.HIGHEST,
            preferred_element_type=jnp.float32,
        )
        * factor
    )
    used = slot_index < slot_count[0]
    keep = (
        (lag_index[None, :] >= low[:, None]) & (lag_index[None, :] < high[:, None]) & used[:, None]
    )
    return jnp.where(keep[:, None, :], stack, jnp.zeros_like(stack))


def solution(mesh):
    in_specs = (P("win", "chan", None), P("chan", None), P("chan"), P("chan"), P("chan"))
    out_specs = P(("chan", "win"), None, None)
    return jax.shard_map(
        per_device, mesh=mesh, in_specs=in_specs, out_specs=out_specs, check_vma=False
    )
```

profile of v0, /device:TPU:17, one launch (start us, length us, event | category | flops | bytes accessed | tf_op | source)
XLA Modules:
  0.0 286.4 jit_solution(5386617236624813043)
XLA Ops:
  6.5 1.1 cosine_convert_fusion
  8.1 2.1 convolution_bitcast_fusion
  10.3 3.6 %reshape.90 = f32[4,512,256]{1,0,2:T(4,128)} reshape(f32[2048,256]{0,1:T(8,128)} %convolution_bitcast_fusion) | data formatting | bytes 4194304 | tf_op jit(solution)/shard_map/reshape | solution.py:65
  13.9 2.1 fusion.25
  16.7 1.6 pad_maximum_fusion
  18.3 3.2 %collective-permute-start = (bf16[4,512,256]{1,0,2:T(4,128)(2,1)}, bf16[4,512,256]{1,0,2:T(4,128)(2,1)}, u32[]{:S(2)}, u32[]{:S(2)}) collective-permute-start(bf16[4,512,256]{1,0,2:T(4,128)(2,1)} %pad_maximum_fusion), channel_id=1, source_target_pairs={{0,8},{2,10},{4,12},{6,14},{8,16},{10,18},{12,20},{14,22},{16,24},... | collective-permute-start | bytes 3145736 | tf_op jit(solution)/shard_map/ppermute | solution.py:18
  21.5 1.9 collective-permute-start.1
  23.5 3.1 %collective-permute-start.2 = (bf16[4,512,256]{1,0,2:T(4,128)(2,1)}, bf16[4,512,256]{1,0,2:T(4,128)(2,1)}, u32[]{:S(2)}, u32[]{:S(2)}) collective-permute-start(bf16[4,512,256]{1,0,2:T(4,128)(2,1)} %pad_maximum_fusion), channel_id=1, source_target_pairs={{0,4},{2,6},{4,8},{6,10},{8,12},{10,14},{12,16},{14,18},{16,20},{1... | collective-permute-start | bytes 3145736 | tf_op jit(solution)/shard_map/ppermute | solution.py:18
  26.6 3.0 %collective-permute-start.3 = (bf16[4,512,256]{1,0,2:T(4,128)(2,1)}, bf16[4,512,256]{1,0,2:T(4,128)(2,1)}, u32[]{:S(2)}, u32[]{:S(2)}) collective-permute-start(bf16[4,512,256]{1,0,2:T(4,128)(2,1)} %pad_maximum_fusion), channel_id=1, source_target_pairs={{0,2},{2,4},{4,6},{6,8},{8,10},{10,12},{12,14},{14,16},{16,18},{18... | collective-permute-start | bytes 3145736 | tf_op jit(solution)/shard_map/ppermute | solution.py:18
  29.6 2.0 collective-permute-start.4
  31.7 12.9 %collective-permute-done = bf16[4,512,256]{1,0,2:T(4,128)(2,1)} collective-permute-done((bf16[4,512,256]{1,0,2:T(4,128)(2,1)}, bf16[4,512,256]{1,0,2:T(4,128)(2,1)}, u32[]{:S(2)}, u32[]{:S(2)}) %collective-permute-start) | collective-permute-done | bytes 1048608 | tf_op jit(solution)/shard_map/ppermute | solution.py:18
  44.6 3.0 %collective-permute-start.5 = (bf16[4,512,256]{1,0,2:T(4,128)(2,1)}, bf16[4,512,256]{1,0,2:T(4,128)(2,1)}, u32[]{:S(2)}, u32[]{:S(2)}) collective-permute-start(bf16[4,512,256]{1,0,2:T(4,128)(2,1)} %pad_maximum_fusion), channel_id=1, source_target_pairs={{4,0},{6,2},{8,4},{10,6},{12,8},{14,10},{16,12},{18,14},{20,16},{2... | collective-permute-start | bytes 3145736 | tf_op jit(solution)/shard_map/ppermute | solution.py:18
  47.6 22.5 %collective-permute-done.1 = bf16[4,512,256]{1,0,2:T(4,128)(2,1)} collective-permute-done((bf16[4,512,256]{1,0,2:T(4,128)(2,1)}, bf16[4,512,256]{1,0,2:T(4,128)(2,1)}, u32[]{:S(2)}, u32[]{:S(2)}) %collective-permute-start.1) | collective-permute-done | bytes 1048608 | tf_op jit(solution)/shard_map/ppermute | solution.py:18
  70.1 1.9 collective-permute-start.6
  72.1 22.0 %collective-permute-done.2 = bf16[4,512,256]{1,0,2:T(4,128)(2,1)} collective-permute-done((bf16[4,512,256]{1,0,2:T(4,128)(2,1)}, bf16[4,512,256]{1,0,2:T(4,128)(2,1)}, u32[]{:S(2)}, u32[]{:S(2)}) %collective-permute-start.2) | collective-permute-done | bytes 1048608 | tf_op jit(solution)/shard_map/ppermute | solution.py:18
  94.1 5.1 %collective-permute-start.7 = (bf16[4,512,256]{1,0,2:T(4,128)(2,1)}, bf16[4,512,256]{1,0,2:T(4,128)(2,1)S(1)}, u32[]{:S(2)}, u32[]{:S(2)}) collective-permute-start(bf16[4,512,256]{1,0,2:T(4,128)(2,1)} %pad_maximum_fusion), channel_id=1, source_target_pairs={{8,0},{10,2},{12,4},{14,6},{16,8},{18,10},{20,12},{22,14},{24,16},... | collective-permute-start | bytes 3145736 | tf_op jit(solution)/shard_map/ppermute | solution.py:18
  99.3 2.6 constant_dynamic-update-slice_fusion.8
  101.9 2.7 constant_dynamic-update-slice_fusion.7
  104.5 2.7 constant_dynamic-update-slice_fusion.6
  107.2 8.7 %collective-permute-done.3 = bf16[4,512,256]{1,0,2:T(4,128)(2,1)} collective-permute-done((bf16[4,512,256]{1,0,2:T(4,128)(2,1)}, bf16[4,512,256]{1,0,2:T(4,128)(2,1)}, u32[]{:S(2)}, u32[]{:S(2)}) %collective-permute-start.3) | collective-permute-done | bytes 1048608 | tf_op jit(solution)/shard_map/ppermute | solution.py:18
  115.9 2.6 constant_dynamic-update-slice_fusion.5
  118.5 1.6 constant_dynamic-update-slice_fusion.4
  120.1 2.7 constant_dynamic-update-slice_fusion.3
  122.8 2.6 constant_dynamic-update-slice_fusion.2
  125.4 2.8 constant_dynamic-update-slice_fusion.1
  128.2 1.4 constant_dynamic-update-slice_fusion
  129.6 15.3 %copy.6 = bf16[4,4608,256]{2,1,0:T(8,128)(2,1)} copy(bf16[4,4608,256]{1,0,2:T(4,128)(2,1)} %constant_dynamic-update-slice_fusion) | data formatting | bytes 18874368 | tf_op jit(solution)/shard_map/concatenate | solution.py:73
  144.9 64.9 %while.10 = (s32[]{:T(128)}, f32[4,8,128,256]{3,2,1,0:T(8,128)}, s32[4,8,2]{1,0,2:T(4,128)S(1)}, bf16[4,36,128,256]{3,2,1,0:T(8,128)(2,1)}, s32[]{:T(128)}) while((s32[]{:T(128)}, f32[4,8,128,256]{3,2,1,0:T(8,128)}, s32[4,8,2]{1,0,2:T(4,128)S(1)}, bf16[4,36,128,256]{3,2,1,0:T(8,128)(2,1)}, s32[]{:T(128)}) %tuple.44), condition=%wide.region_2.4_spmd, body=%wide.region_1.3_spmd.sunk | while | flops 8390754 | bytes 28320736 | solution.py:85
  144.9 5.7 %gather_fusion = bf16[8,4,128,256]{3,2,1,0:T(8,128)(2,1)} fusion(bf16[4,36,128,256]{3,2,1,0:T(8,128)(2,1)} %get-tuple-element.121, s32[1024]{0:T(1024)S(1)} %pad_clamp_fusion.4), kind=kCustom, calls=%fused_computation.1.clone.clone.1 | custom fusion | bytes 4194336 | tf_op jit(solution)/shard_map/while/body/eval_jaxpr/jit(_take)/gather | solution.py:82
  150.6 5.8 %gather_fusion.1 = bf16[8,4,128,256]{3,2,1,0:T(8,128)(2,1)} fusion(bf16[4,36,128,256]{3,2,1,0:T(8,128)(2,1)} %get-tuple-element.121, s32[1024]{0:T(1024)S(1)} %pad_clamp_fusion.5), kind=kCustom, calls=%fused_computation.clone.clone.1 | custom fusion | bytes 4194336 | tf_op jit(solution)/shard_map/while/body/eval_jaxpr/jit(_take)/gather | solution.py:81
  156.4 2.6 select_bitcast_fusion.3
  160.1 1.1 fusion.31
  161.1 5.7 %gather_fusion = bf16[8,4,128,256]{3,2,1,0:T(8,128)(2,1)} fusion(bf16[4,36,128,256]{3,2,1,0:T(8,128)(2,1)} %get-tuple-element.121, s32[1024]{0:T(1024)S(1)} %pad_clamp_fusion.4), kind=kCustom, calls=%fused_computation.1.clone.clone.1 | custom fusion | bytes 4194336 | tf_op jit(solution)/shard_map/while/body/eval_jaxpr/jit(_take)/gather | solution.py:82
  166.8 5.8 %gather_fusion.1 = bf16[8,4,128,256]{3,2,1,0:T(8,128)(2,1)} fusion(bf16[4,36,128,256]{3,2,1,0:T(8,128)(2,1)} %get-tuple-element.121, s32[1024]{0:T(1024)S(1)} %pad_clamp_fusion.5), kind=kCustom, calls=%fused_computation.clone.clone.1 | custom fusion | bytes 4194336 | tf_op jit(solution)/shard_map/while/body/eval_jaxpr/jit(_take)/gather | solution.py:81
  172.6 2.6 select_bitcast_fusion.3
  175.3 0.9 fusion.30
  176.3 1.1 fusion.31
  177.4 5.7 %gather_fusion = bf16[8,4,128,256]{3,2,1,0:T(8,128)(2,1)} fusion(bf16[4,36,128,256]{3,2,1,0:T(8,128)(2,1)} %get-tuple-element.121, s32[1024]{0:T(1024)S(1)} %pad_clamp_fusion.4), kind=kCustom, calls=%fused_computation.1.clone.clone.1 | custom fusion | bytes 4194336 | tf_op jit(solution)/shard_map/while/body/eval_jaxpr/jit(_take)/gather | solution.py:82
  183.1 5.8 %gather_fusion.1 = bf16[8,4,128,256]{3,2,1,0:T(8,128)(2,1)} fusion(bf16[4,36,128,256]{3,2,1,0:T(8,128)(2,1)} %get-tuple-element.121, s32[1024]{0:T(1024)S(1)} %pad_clamp_fusion.5), kind=kCustom, calls=%fused_computation.clone.clone.1 | custom fusion | bytes 4194336 | tf_op jit(solution)/shard_map/while/body/eval_jaxpr/jit(_take)/gather | solution.py:81
  188.8 2.6 select_bitcast_fusion.3
  191.5 0.9 fusion.30
  192.5 1.0 fusion.31
  193.6 5.7 %gather_fusion = bf16[8,4,128,256]{3,2,1,0:T(8,128)(2,1)} fusion(bf16[4,36,128,256]{3,2,1,0:T(8,128)(2,1)} %get-tuple-element.121, s32[1024]{0:T(1024)S(1)} %pad_clamp_fusion.4), kind=kCustom, calls=%fused_computation.1.clone.clone.1 | custom fusion | bytes 4194336 | tf_op jit(solution)/shard_map/while/body/eval_jaxpr/jit(_take)/gather | solution.py:82
  199.3 5.8 %gather_fusion.1 = bf16[8,4,128,256]{3,2,1,0:T(8,128)(2,1)} fusion(bf16[4,36,128,256]{3,2,1,0:T(8,128)(2,1)} %get-tuple-element.121, s32[1024]{0:T(1024)S(1)} %pad_clamp_fusion.5), kind=kCustom, calls=%fused_computation.clone.clone.1 | custom fusion | bytes 4194336 | tf_op jit(solution)/shard_map/while/body/eval_jaxpr/jit(_take)/gather | solution.py:81
  205.1 2.6 select_bitcast_fusion.3
  208.7 1.1 fusion.31
  211.7 63.5 %reduce-scatter.2.cloned.1.call-done = f32[16,128,256]{2,1,0:T(8,128)} async-done(((f32[32,128,256]{2,1,0:T(8,128)}), f32[16,128,256]{2,1,0:T(8,128)}) %reduce-scatter.2.cloned.1.call-update) | async-done | bytes 2097168 | tf_op jit(solution)/shard_map/reduce_scatter | solution.py:89
  275.2 4.4 %fusion.5 = f32[16,128,128]{2,1,0:T(8,128)} fusion(f32[16,128,256]{2,1,0:T(8,128)} %reduce-scatter.2.cloned.1.call-done, pred[16,128]{1,0:T(8,128)(4,1)S(1)} %fusion.22, f32[128,128]{1,0:T(8,128)S(1)} %get-tuple-element.58, f32[128,128]{1,0:T(8,128)S(1)} %get-tuple-element.57), kind=kOutput, calls=%fused_computation.27 | convolution fusion | flops 805863424 | bytes 3278848 | tf_op jit(solution)/shard_map/pbf,fl->pbl/dot_general | solution.py:96
  (53 shorter events, 4.8 us)
Async XLA Ops:
  6.5 1.6 copy-start
  6.5 268.7 %reduce-scatter.2.cloned.1.call-start = ((), (), s32[]{:S(2)}) async-start(), calls=%async_computation.1 | async-start | bytes 6291456 | tf_op jit(solution)/shard_map/reduce_scatter | solution.py:89
  13.9 2.2 copy-start.1
  16.7 55.3 %copy-start.2 = (s32[32,2]{0,1:T(2,128)S(1)}, s32[32,2]{0,1:T(2,128)}, u32[]{:S(2)}) copy-start(s32[32,2]{0,1:T(2,128)} %param.10) | copy-start | bytes 772
  18.3 26.2 %collective-permute-start = (bf16[4,512,256]{1,0,2:T(4,128)(2,1)}, bf16[4,512,256]{1,0,2:T(4,128)(2,1)}, u32[]{:S(2)}, u32[]{:S(2)}) collective-permute-start(bf16[4,512,256]{1,0,2:T(4,128)(2,1)} %pad_maximum_fusion), channel_id=1, source_target_pairs={{0,8},{2,10},{4,12},{6,14},{8,16},{10,18},{12,20},{14,22},{16,24},... | collective-permute-start | bytes 3145736 | tf_op jit(solution)/shard_map/ppermute | solution.py:18
  21.5 48.5 %collective-permute-start.1 = (bf16[4,512,256]{1,0,2:T(4,128)(2,1)}, bf16[4,512,256]{1,0,2:T(4,128)(2,1)}, u32[]{:S(2)}, u32[]{:S(2)}) collective-permute-start(bf16[4,512,256]{1,0,2:T(4,128)(2,1)} %pad_maximum_fusion), channel_id=1, source_target_pairs={{0,6},{2,8},{4,10},{6,12},{8,14},{10,16},{12,18},{14,20},{16,22},{... | collective-permute-start | bytes 3145736 | tf_op jit(solution)/shard_map/ppermute | solution.py:18
  23.5 70.6 %collective-permute-start.2 = (bf16[4,512,256]{1,0,2:T(4,128)(2,1)}, bf16[4,512,256]{1,0,2:T(4,128)(2,1)}, u32[]{:S(2)}, u32[]{:S(2)}) collective-permute-start(bf16[4,512,256]{1,0,2:T(4,128)(2,1)} %pad_maximum_fusion), channel_id=1, source_target_pairs={{0,4},{2,6},{4,8},{6,10},{8,12},{10,14},{12,16},{14,18},{16,20},{1... | collective-permute-start | bytes 3145736 | tf_op jit(solution)/shard_map/ppermute | solution.py:18
  26.6 89.3 %collective-permute-start.3 = (bf16[4,512,256]{1,0,2:T(4,128)(2,1)}, bf16[4,512,256]{1,0,2:T(4,128)(2,1)}, u32[]{:S(2)}, u32[]{:S(2)}) collective-permute-start(bf16[4,512,256]{1,0,2:T(4,128)(2,1)} %pad_maximum_fusion), channel_id=1, source_target_pairs={{0,2},{2,4},{4,6},{6,8},{8,10},{10,12},{12,14},{14,16},{16,18},{18... | collective-permute-start | bytes 3145736 | tf_op jit(solution)/shard_map/ppermute | solution.py:18
  29.6 90.5 %collective-permute-start.4 = (bf16[4,512,256]{1,0,2:T(4,128)(2,1)}, bf16[4,512,256]{1,0,2:T(4,128)(2,1)}, u32[]{:S(2)}, u32[]{:S(2)}) collective-permute-start(bf16[4,512,256]{1,0,2:T(4,128)(2,1)} %pad_maximum_fusion), channel_id=1, source_target_pairs={{2,0},{4,2},{6,4},{8,6},{10,8},{12,10},{14,12},{16,14},{18,16},{20... | collective-permute-start | bytes 3145736 | tf_op jit(solution)/shard_map/ppermute | solution.py:18
  44.6 78.2 %collective-permute-start.5 = (bf16[4,512,256]{1,0,2:T(4,128)(2,1)}, bf16[4,512,256]{1,0,2:T(4,128)(2,1)}, u32[]{:S(2)}, u32[]{:S(2)}) collective-permute-start(bf16[4,512,256]{1,0,2:T(4,128)(2,1)} %pad_maximum_fusion), channel_id=1, source_target_pairs={{4,0},{6,2},{8,4},{10,6},{12,8},{14,10},{16,12},{18,14},{20,16},{2... | collective-permute-start | bytes 3145736 | tf_op jit(solution)/shard_map/ppermute | solution.py:18
  70.1 55.3 %collective-permute-start.6 = (bf16[4,512,256]{1,0,2:T(4,128)(2,1)}, bf16[4,512,256]{1,0,2:T(4,128)(2,1)}, u32[]{:S(2)}, u32[]{:S(2)}) collective-permute-start(bf16[4,512,256]{1,0,2:T(4,128)(2,1)} %pad_maximum_fusion), channel_id=1, source_target_pairs={{6,0},{8,2},{10,4},{12,6},{14,8},{16,10},{18,12},{20,14},{22,16},{... | collective-permute-start | bytes 3145736 | tf_op jit(solution)/shard_map/ppermute | solution.py:18
  94.1 34.1 %collective-permute-start.7 = (bf16[4,512,256]{1,0,2:T(4,128)(2,1)}, bf16[4,512,256]{1,0,2:T(4,128)(2,1)S(1)}, u32[]{:S(2)}, u32[]{:S(2)}) collective-permute-start(bf16[4,512,256]{1,0,2:T(4,128)(2,1)} %pad_maximum_fusion), channel_id=1, source_target_pairs={{8,0},{10,2},{12,4},{14,6},{16,8},{18,10},{20,12},{22,14},{24,16},... | collective-permute-start | bytes 3145736 | tf_op jit(solution)/shard_map/ppermute | solution.py:18
  209.8 0.7 copy-start.3
  209.8 0.7 copy-start.4
Sparse Core Ops, SparseCore 0:
  210.0 65.2 reduce-scatter.1
where the time goes:
time: 289 us; the launch traced here: 286 us
  waiting for transfers between devices  130 us (45%)
  local copies, waits for them, and re-layouts  86.2 us (30%)
  other arithmetic  26.3 us (9%)
  starting transfers between devices  23.4 us (8%)
  between operations  14.2 us (5%)
  matrix products  6.49 us (2%)
    ppermute x8, waiting for transfers between devices, shifted(): return lax.ppermute(block, axis, route)  66.1 us
    reduce_scatter x1, waiting for transfers between devices, per_device(): summed = lax.psum_scatter(spectrum, 'win', scatter_dimension=0, tiled=True)  63.5 us
    ppermute x8, starting transfers between devices, shifted(): return lax.ppermute(block, axis, route)  23.4 us
    gather x4, local copies, waits for them, and re-layouts, one_group(): first = jnp.take(blocks, pair_rows[:, 0], axis=1)  23.1 us
    gather x4, local copies, waits for them, and re-layouts, one_group(): second = jnp.take(blocks, pair_rows[:, 1], axis=1)  22.7 us
    unnamed x17, local copies, waits for them, and re-layouts  19.8 us
    concatenate x2, local copies, waits for them, and re-layouts, per_device(): neighbourhood = jnp.concatenate(pieces, axis=1)  16.7 us
    select_n x4, other arithmetic, one_group(): second = jnp.take(blocks, pair_rows[:, 1], axis=1)  10.6 us
  transfers between devices with their start and end apart: 9, of which 5 were waited for; matrix products, arithmetic and copies ran while one was open for 7% of the time, Pallas kernels for 0%

commit v1 on v0

v1 whole, which is shorter than its diff:
```python
import functools
import math

import jax
import jax.numpy as jnp
import numpy as np
from jax import lax
from jax.experimental import pallas as pl
from jax.experimental.pallas import tpu as pltpu
from jax.sharding import PartitionSpec as P

BLOCK = 128
F = 128
LAGS = 128
REACH = 16
VMEM_LIMIT = 48 * 1024 * 1024


def forward_table(length):
    first = length // 32
    times = np.arange(length, dtype=np.int64)[:, None]
    freqs = (first + np.arange(F, dtype=np.int64))[None, :]
    phase = 2.0 * math.pi / length * (times * freqs % length)
    table = np.concatenate([np.cos(phase), -np.sin(phase)], axis=1)
    return jnp.asarray(table.astype(np.float32)).astype(jnp.bfloat16)


def inverse_tables(length, factor):
    first = length // 32
    freqs = (first + np.arange(F, dtype=np.int64))[:, None]
    shifts = (np.arange(LAGS, dtype=np.int64) - LAGS // 2)[None, :]
    phase = 2.0 * math.pi / length * (freqs * shifts % length)
    table = (np.concatenate([np.cos(phase), -np.sin(phase)], axis=0) * factor).astype(np.float32)
    high = table.astype(jnp.bfloat16)
    low = (table - high.astype(np.float32)).astype(jnp.bfloat16)
    return jnp.asarray(np.concatenate([high, low], axis=1))


def spectra_kernel(parts, records_ref, table_ref, out_ref):
    blocks = out_ref.shape[1]
    for block in range(blocks):
        rows = records_ref[0, pl.ds(block * BLOCK, BLOCK), :]
        spectra = jnp.dot(rows, table_ref[...], preferred_element_type=jnp.float32)
        real_part, imag_part = spectra[:, :F], spectra[:, F:]
        power = real_part * real_part + imag_part * imag_part
        level = jnp.mean(power, axis=-1, keepdims=True)
        scale = lax.rsqrt(power + 0.1 * level + 1e-06)
        whitened = jnp.concatenate([real_part * scale, imag_part * scale], axis=1)
        out_ref[:, block] = whitened.astype(jnp.bfloat16).reshape(parts, BLOCK // parts, 2 * F)


def whitened_parts(records, parts):
    segments, channels, length = records.shape
    blocks, width = channels // BLOCK, BLOCK // parts
    packed = width % 16 == 0
    cut = parts if packed else 1
    whitened = pl.pallas_call(
        functools.partial(spectra_kernel, cut),
        grid=(segments,),
        in_specs=[
            pl.BlockSpec((1, channels, length), lambda s: (s, 0, 0)),
            pl.BlockSpec((length, 2 * F), lambda s: (0, 0)),
        ],
        out_specs=pl.BlockSpec((cut, blocks, BLOCK // cut, 2 * F), lambda s: (0, 0, s, 0)),
        out_shape=jax.ShapeDtypeStruct(
            (cut, blocks, segments * BLOCK // cut, 2 * F), jnp.bfloat16
        ),
        compiler_params=pltpu.CompilerParams(vmem_limit_bytes=VMEM_LIMIT),
    )(records, forward_table(length))
    if packed:
        return whitened
    whitened = whitened.reshape(blocks, segments, parts, width, 2 * F)
    return whitened.transpose(2, 0, 1, 3, 4).reshape(parts, blocks, segments * width, 2 * F)


def pair_kernel(step, wins, pairs_ref, counts_ref, below, own, above, table_ref, out_ref, held, cross, sem):
    parts, blocks = own.shape[:2]
    copies = [pltpu.make_async_copy(ref, held.at[k], sem.at[k]) for k, ref in enumerate((below, own, above))]
    for copy in copies:
        copy.start()
    for copy in copies:
        copy.wait()
    slots = out_ref.shape[1] // step
    rows = own.shape[2]
    owned = parts // wins * blocks

    def place(block):
        group, rest = block // owned, block % owned
        return group, rest // blocks, rest % blocks

    def part_of(part, _):
        owner, win = part // wins, part % wins

        def one_pair(slot, _):
            pair = part * slots + slot
            ga, ja, ba = place(pairs_ref[2 * pair])
            gb, jb, bb = place(pairs_ref[2 * pair + 1])
            real_sum = jnp.zeros((step, F), jnp.float32)
            imag_sum = jnp.zeros((step, F), jnp.float32)
            for w in range(wins):
                for r in range(0, rows, step):
                    a = held[ga, ja * wins + w, ba, pl.ds(r, step), :].astype(jnp.float32)
                    b = held[gb, jb * wins + w, bb, pl.ds(r, step), :].astype(jnp.float32)
                    ar, ai, br, bi = a[:, :F], a[:, F:], b[:, :F], b[:, F:]
                    real_sum += ar * br + ai * bi
                    imag_sum += ar * bi - ai * br
            cross[pl.ds(pl.multiple_of(slot * step, step), step), pl.ds(0, F)] = real_sum
            cross[pl.ds(pl.multiple_of(slot * step, step), step), pl.ds(F, F)] = imag_sum
            return 0

        count = jnp.clip(counts_ref[owner] - win * slots, 0, slots)
        lax.fori_loop(0, count, one_pair, 0)
        spectrum = cross[...]
        high = spectrum.astype(jnp.bfloat16)
        low = (spectrum - high.astype(jnp.float32)).astype(jnp.bfloat16)
        first = jnp.dot(high, table_ref[...], preferred_element_type=jnp.float32)
        second = jnp.dot(low, table_ref[:, :LAGS], preferred_element_type=jnp.float32)
        out_ref[part] = first[:, :LAGS] + (first[:, LAGS:] + second)
        return 0

    lax.fori_loop(0, parts, part_of, 0)


def per_device(records, block_pairs, lag_low, lag_high, slot_count):
    segments, channels, length = records.shape
    blocks = channels // BLOCK
    chans, wins = lax.axis_size("chan"), lax.axis_size("win")
    near = REACH // blocks
    parts = near * wins
    width = BLOCK // parts
    slots = block_pairs.shape[0]
    share = slots // wins
    groups = [[q * parts + k for k in range(parts)] for q in range(chans // near)]
    exchange = functools.partial(
        lax.all_to_all,
        axis_name=("chan", "win"),
        split_axis=0,
        concat_axis=0,
        axis_index_groups=groups,
        tiled=True,
    )

    own = exchange(whitened_parts(records, parts))
    win = lax.axis_index("win")
    base = (lax.axis_index("chan") // near - 1) * REACH
    local = jnp.clip(block_pairs - base, 0, 3 * REACH - 1)
    mine = lax.dynamic_slice_in_dim(local, win * share, share).reshape(2 * share)
    note = jnp.concatenate([mine, slot_count, jnp.zeros(128 - 2 * share - 1, jnp.int32)])
    notes = exchange(jnp.broadcast_to(note, (parts, 128)))
    pairs = notes[:, : 2 * share].reshape(parts * 2 * share)
    counts = notes[:: wins, 2 * share]

    up = [(i, i + near) for i in range(chans - near)]
    below = lax.ppermute(own, "chan", up)
    above = lax.ppermute(own, "chan", [(b, a) for a, b in up])

    step = max(width, 16)
    factor = 1.0 / math.sqrt(F * segments * wins)
    hbm = pl.BlockSpec(memory_space=pl.ANY)
    smem = pl.BlockSpec(memory_space=pltpu.SMEM)
    vmem = pl.BlockSpec(memory_space=pltpu.VMEM)
    lagged = pl.pallas_call(
        functools.partial(pair_kernel, step, wins),
        in_specs=[smem, smem, hbm, hbm, hbm, vmem],
        out_specs=vmem,
        out_shape=jax.ShapeDtypeStruct((parts, share * step, LAGS), jnp.float32),
        scratch_shapes=[
            pltpu.VMEM((3,) + own.shape, jnp.bfloat16),
            pltpu.VMEM((share * step, 2 * F), jnp.float32),
            pltpu.SemaphoreType.DMA((3,)),
        ],
        compiler_params=pltpu.CompilerParams(vmem_limit_bytes=VMEM_LIMIT),
    )(pairs, counts, below, own, above, inverse_tables(length, factor))

    if step > width:
        lagged = lagged.reshape(parts, share, step // width, width, LAGS).sum(axis=2)
    stack = exchange(lagged).reshape(parts, share, width, LAGS)
    stack = stack.transpose(1, 0, 2, 3).reshape(share, BLOCK, LAGS)
    start = win * share
    low = lax.dynamic_slice_in_dim(lag_low, start, share)
    high = lax.dynamic_slice_in_dim(lag_high, start, share)
    lag_index = jnp.arange(LAGS, dtype=jnp.int32)[None, :]
    used = start + jnp.arange(share, dtype=jnp.int32) < slot_count[0]
    keep = (lag_index >= low[:, None]) & (lag_index < high[:, None]) & used[:, None]
    return jnp.where(keep[:, None, :], stack, jnp.zeros_like(stack))


def solution(mesh):
    in_specs = (P("win", "chan", None), P("chan", None), P("chan"), P("chan"), P("chan"))
    out_specs = P(("chan", "win"), None, None)
    return jax.shard_map(
        per_device, mesh=mesh, in_specs=in_specs, out_specs=out_specs, check_vma=False
    )
```

time: 289 us -> 82.6 us (0.29)
  the two profiles are of different devices: /device:TPU:17 before, /device:TPU:0 now
where the time goes in v1:
time: 82.6 us; the launch traced here: 82.9 us
  waiting for transfers between devices  31.5 us (38%)
  blocking collectives  26.6 us (32%)
  Pallas kernels  11.1 us (13%)
  starting transfers between devices  8.41 us (10%)
  local copies, waits for them, and re-layouts  3.24 us (4%)
  other arithmetic  1.37 us (2%)
    all_to_all x1, blocking collectives, per_device(): own = exchange(whitened_parts(records, parts))  19.4 us
    all_to_all x1, waiting for transfers between devices, per_device(): stack = exchange(lagged).reshape(parts, share, width, LAGS)  14.2 us
    ppermute x1, waiting for transfers between devices, per_device(): below = lax.ppermute(own, 'chan', up)  13.1 us
    pallas_call x1, Pallas kernels, per_device(): pl.pallas_call(functools.partial(pair_kernel, step, wins), in_specs=[smem...  9.35 us
    all_to_all x1, blocking collectives, per_device(): notes = exchange(jnp.broadcast_to(note, (parts, 128)))  7.16 us
    ppermute x1, waiting for transfers between devices, per_device(): above = lax.ppermute(own, 'chan', [(b, a) for a, b in up])  4.18 us
    all_to_all x1, starting transfers between devices, per_device(): stack = exchange(lagged).reshape(parts, share, width, LAGS)  3.57 us
    ppermute x1, starting transfers between devices, per_device(): below = lax.ppermute(own, 'chan', up)  3.55 us
  transfers between devices with their start and end apart: 3, of which 3 were waited for; matrix products, arithmetic and copies ran while one was open for 1% of the time, Pallas kernels for 0%

profile of v1, /device:TPU:0, one launch (start us, length us, event | category | flops | bytes accessed | tf_op | source)
XLA Modules:
  0.0 82.9 jit_solution(10257297407805214676)
XLA Ops:
  0.0 0.0 copy-start
  0.0 1.6 %copy-done = bf16[4,512,512]{2,1,0:T(8,128)(2,1)S(1)} copy-done((bf16[4,512,512]{2,1,0:T(8,128)(2,1)S(1)}, bf16[4,512,512]{2,1,0:T(8,128)(2,1)}, u32[]{:S(2)}) %copy-start) | copy-done | bytes 2097176
  1.6 0.0 copy-start.1
  1.6 0.9 %copy-done.1 = bf16[512,256]{1,0:T(8,128)(2,1)S(1)} copy-done((bf16[512,256]{1,0:T(8,128)(2,1)S(1)}, bf16[512,256]{1,0:T(8,128)(2,1)}, u32[]{:S(2)}) %copy-start.1) | copy-done | bytes 262168
  2.5 0.0 copy-start.3
  2.5 0.0 copy-start.2
  2.5 1.7 %shard_map.73 = bf16[8,4,64,256]{3,2,1,0:T(8,128)(2,1)S(1)} custom-call(bf16[4,512,512]{2,1,0:T(8,128)(2,1)S(1)} %copy-done, bf16[512,256]{1,0:T(8,128)(2,1)S(1)} %copy-done.1), custom_call_target="tpu_custom_call" | custom-call | tf_op jit(solution)/shard_map/pallas_call | solution.py:57
  4.3 19.4 %all_to_all.19.own = bf16[8,4,64,256]{3,2,1,0:T(8,128)(2,1)S(1)} all-to-all(bf16[8,4,64,256]{3,2,1,0:T(8,128)(2,1)S(1)} %shard_map.73), channel_id=1, replica_groups={{0,1,2,3,4,5,6,7},{8,9,10,11,12,13,14,15},{16,17,18,19,20,21,22,23},{24..., dimensions={0} | all-to-all | bytes 2097152 | tf_op jit(solution)/shard_map/all_to_all | solution.py:143
  23.7 3.5 %collective-permute-start = (bf16[8,4,64,256]{3,2,1,0:T(8,128)(2,1)S(1)}, bf16[8,4,64,256]{3,2,1,0:T(8,128)(2,1)S(1)}, u32[]{:S(2)}, u32[]{:S(2)}) collective-permute-start(bf16[8,4,64,256]{3,2,1,0:T(8,128)(2,1)S(1)} %all_to_all.19.own), channel_id=1, source_target_pairs={{0,8},{2,10},{4,12},{6,14},{8,16},{10,18},{12,20},{14,22},{16,24},... | collective-permute-start | bytes 3145736 | tf_op jit(solution)/shard_map/ppermute | solution.py:154
  27.2 1.3 %collective-permute-start.1 = (bf16[8,4,64,256]{3,2,1,0:T(8,128)(2,1)S(1)}, bf16[8,4,64,256]{3,2,1,0:T(8,128)(2,1)S(1)}, u32[]{:S(2)}, u32[]{:S(2)}) collective-permute-start(bf16[8,4,64,256]{3,2,1,0:T(8,128)(2,1)S(1)} %all_to_all.19.own), channel_id=1, source_target_pairs={{8,0},{10,2},{12,4},{14,6},{16,8},{18,10},{20,12},{22,14},{24,16},... | collective-permute-start | bytes 3145736 | tf_op jit(solution)/shard_map/ppermute | solution.py:155
  28.6 0.0 copy-done.3
  28.6 0.1 constant_dynamic-slice_fusion
  28.7 0.1 copy.15
  28.7 0.1 reshape.68
  29.5 0.1 pad_add_fusion
  29.6 7.2 %all_to_all.20 = s32[8,1,128]{2,1,0:T(1,128)S(1)} all-to-all(s32[8,1,128]{2,1,0:T(1,128)S(1)} %broadcast_in_dim.24), channel_id=1, replica_groups={{0,1,2,3,4,5,6,7},{8,9,10,11,12,13,14,15},{16,17,18,19,20,21,22,23},{24..., dimensions={0} | all-to-all | bytes 8192 | tf_op jit(solution)/shard_map/all_to_all | solution.py:149
  36.7 0.1 slice.7
  36.8 0.1 reduce.counts_ref
  36.9 0.1 reshape.69.pairs_ref
  37.0 0.0 copy-start.4
  37.0 13.1 %collective-permute-done.below = bf16[8,4,64,256]{3,2,1,0:T(8,128)(2,1)S(1)} collective-permute-done((bf16[8,4,64,256]{3,2,1,0:T(8,128)(2,1)S(1)}, bf16[8,4,64,256]{3,2,1,0:T(8,128)(2,1)S(1)}, u32[]{:S(2)}, u32[]{:S(2)}) %collective-permute-start) | collective-permute-done | bytes 1048608 | tf_op jit(solution)/shard_map/ppermute | solution.py:154
  50.1 4.2 %collective-permute-done.1.above = bf16[8,4,64,256]{3,2,1,0:T(8,128)(2,1)S(1)} collective-permute-done((bf16[8,4,64,256]{3,2,1,0:T(8,128)(2,1)S(1)}, bf16[8,4,64,256]{3,2,1,0:T(8,128)(2,1)S(1)}, u32[]{:S(2)}, u32[]{:S(2)}) %collective-permute-start.1) | collective-permute-done | bytes 1048608 | tf_op jit(solution)/shard_map/ppermute | solution.py:155
  54.3 0.0 copy-done.2
  54.3 9.3 %shard_map.74 = f32[8,256,128]{2,1,0:T(8,128)} custom-call(s32[256]{0:T(256)S(1)} %reshape.69.pairs_ref, s32[4]{0:T(128)S(1)} %reduce.counts_ref, bf16[8,4,64,256]{3,2,1,0:T(8,128)(2,1)S(1)} %collective-permute-done.below, bf16[8,4,64,256]{3,2,1,0:T(8,128)(2,1)S(1)} %all_to_all.19.own, bf16[8,4,64,256]{3,2,1,0:T(8,128)(2,1)S(1)} %collective-permute-done.1.above, ...), custom_call_target="tpu_custom_call" | custom-call | tf_op jit(solution)/shard_map/pallas_call | solution.py:162
  63.6 0.0 copy-start.5
  63.6 3.6 %all-to-all-start.2 = ((f32[8,256,128]{2,1,0:T(8,128)}), f32[8,256,128]{2,1,0:T(8,128)S(1)}, u32[]{:S(2)}, u32[]{:S(2)}) async-start(f32[8,256,128]{2,1,0:T(8,128)} %shard_map.74), calls=%async_computation.2 | async-start | bytes 2097152 | tf_op jit(solution)/shard_map/all_to_all | solution.py:177
  67.2 0.0 copy-done.4
  67.2 0.1 dynamic_slice.10
  67.3 0.0 copy-done.5
  67.3 0.1 dynamic_slice.9
  67.4 0.1 fusion.1
  67.5 14.2 %all-to-all-done.2 = f32[8,256,128]{2,1,0:T(8,128)S(1)} async-done(((f32[8,256,128]{2,1,0:T(8,128)}), f32[8,256,128]{2,1,0:T(8,128)S(1)}, u32[]{:S(2)}, u32[]{:S(2)}) %all-to-all-start.2) | async-done | bytes 1048608 | tf_op jit(solution)/shard_map/all_to_all | solution.py:177
  81.7 0.1 copy.16
  81.8 1.1 %bitcast_select_fusion = f32[16,128,128]{2,1,0:T(8,128)} fusion(f32[16,8,16,128]{3,2,1,0:T(8,128)S(1)} %copy.16, pred[16,128]{1,0:T(8,128)(4,1)S(1)} %fusion.1), kind=kLoop, calls=%fused_computation | loop fusion | flops 262144 | bytes 2099200 | tf_op jit(solution)/shard_map/jit(_where)/select_n | solution.py:185
  (4 shorter events, 0.0 us)
Async XLA Ops:
  0.0 1.6 %copy-start = (bf16[4,512,512]{2,1,0:T(8,128)(2,1)S(1)}, bf16[4,512,512]{2,1,0:T(8,128)(2,1)}, u32[]{:S(2)}) copy-start(bf16[4,512,512]{2,1,0:T(8,128)(2,1)} %records_ref.1) | copy-start | bytes 6291460
  1.6 0.9 %copy-start.1 = (bf16[512,256]{1,0:T(8,128)(2,1)S(1)}, bf16[512,256]{1,0:T(8,128)(2,1)}, u32[]{:S(2)}) copy-start(bf16[512,256]{1,0:T(8,128)(2,1)} %constant.43.table_ref) | copy-start | bytes 786436
  2.5 26.0 %copy-start.3 = (s32[32,2]{0,1:T(2,128)S(1)}, s32[32,2]{0,1:T(2,128)}, u32[]{:S(2)}) copy-start(s32[32,2]{0,1:T(2,128)} %param.8) | copy-start | bytes 772
  2.5 51.7 %copy-start.2 = (bf16[256,256]{1,0:T(8,128)(2,1)S(1)}, bf16[256,256]{1,0:T(8,128)(2,1)}, u32[]{:S(2)}) copy-start(bf16[256,256]{1,0:T(8,128)(2,1)} %constant.41.clone.table_ref) | copy-start | bytes 393220
  23.7 26.4 %collective-permute-start = (bf16[8,4,64,256]{3,2,1,0:T(8,128)(2,1)S(1)}, bf16[8,4,64,256]{3,2,1,0:T(8,128)(2,1)S(1)}, u32[]{:S(2)}, u32[]{:S(2)}) collective-permute-start(bf16[8,4,64,256]{3,2,1,0:T(8,128)(2,1)S(1)} %all_to_all.19.own), channel_id=1, source_target_pairs={{0,8},{2,10},{4,12},{6,14},{8,16},{10,18},{12,20},{14,22},{16,24},... | collective-permute-start | bytes 3145736 | tf_op jit(solution)/shard_map/ppermute | solution.py:154
  27.2 27.0 %collective-permute-start.1 = (bf16[8,4,64,256]{3,2,1,0:T(8,128)(2,1)S(1)}, bf16[8,4,64,256]{3,2,1,0:T(8,128)(2,1)S(1)}, u32[]{:S(2)}, u32[]{:S(2)}) collective-permute-start(bf16[8,4,64,256]{3,2,1,0:T(8,128)(2,1)S(1)} %all_to_all.19.own), channel_id=1, source_target_pairs={{8,0},{10,2},{12,4},{14,6},{16,8},{18,10},{20,12},{22,14},{24,16},... | collective-permute-start | bytes 3145736 | tf_op jit(solution)/shard_map/ppermute | solution.py:155
  37.0 30.2 %copy-start.4 = (s32[32]{0:T(128)S(1)}, s32[32]{0:T(128)}, u32[]{:S(2)}) copy-start(s32[32]{0:T(128)} %param.10) | copy-start | bytes 388
  63.6 3.7 %copy-start.5 = (s32[32]{0:T(128)S(1)}, s32[32]{0:T(128)}, u32[]{:S(2)}) copy-start(s32[32]{0:T(128)} %param.9) | copy-start | bytes 388
  63.6 18.0 %all-to-all-start.2 = ((f32[8,256,128]{2,1,0:T(8,128)}), f32[8,256,128]{2,1,0:T(8,128)S(1)}, u32[]{:S(2)}, u32[]{:S(2)}) async-start(f32[8,256,128]{2,1,0:T(8,128)} %shard_map.74), calls=%async_computation.2 | async-start | bytes 2097152 | tf_op jit(solution)/shard_map/all_to_all | solution.py:177

commit v2 on v1

v2 whole, which is shorter than its diff:
```python
import functools
import math

import jax
import jax.numpy as jnp
import numpy as np
from jax import lax
from jax.experimental import pallas as pl
from jax.experimental.pallas import tpu as pltpu
from jax.sharding import PartitionSpec as P

BLOCK = 128
F = 128
LAGS = 128
REACH = 16
NOTE_ROWS = 16
VMEM_LIMIT = 48 * 1024 * 1024


def forward_table(length):
    first = length // 32
    times = np.arange(length, dtype=np.int64)[:, None]
    freqs = (first + np.arange(F, dtype=np.int64))[None, :]
    phase = 2.0 * math.pi / length * (times * freqs % length)
    table = np.concatenate([np.cos(phase), -np.sin(phase)], axis=1)
    return jnp.asarray(table.astype(np.float32)).astype(jnp.bfloat16)


def inverse_tables(length, factor):
    first = length // 32
    freqs = (first + np.arange(F, dtype=np.int64))[:, None]
    shifts = (np.arange(LAGS, dtype=np.int64) - LAGS // 2)[None, :]
    phase = 2.0 * math.pi / length * (freqs * shifts % length)
    table = (np.concatenate([np.cos(phase), -np.sin(phase)], axis=0) * factor).astype(np.float32)
    high = table.astype(jnp.bfloat16)
    low = (table - high.astype(np.float32)).astype(jnp.bfloat16)
    return jnp.asarray(np.concatenate([high, low], axis=1))


def encode(values):
    values = values * jnp.abs(values)
    return (values * jnp.abs(values)).astype(jnp.bfloat16)


def decode(code, scale):
    code = code.astype(jnp.float32)
    root = jnp.sqrt(jnp.sqrt(jnp.abs(code))) * scale
    return jnp.where(code < 0, -root, root)


def spectra_kernel(near, wins, records, pairs_ref, count_ref, table_ref, out_ref, held, note, sem):
    segments, channels, _ = records.shape
    cut, blocks = out_ref.shape[0], channels // BLOCK
    width = BLOCK // cut
    chan = lax.axis_index("chan")
    mine = lax.rem(chan, near) * wins + lax.axis_index("win")
    copies = [
        pltpu.make_async_copy(records.at[s], held.at[s], sem.at[s]) for s in range(segments)
    ]
    for copy in copies:
        copy.start()
    base = (lax.div(chan, near) - 1) * REACH
    slots = pairs_ref.shape[1]
    note[...] = jnp.zeros_like(note)
    note[0:2, 0:slots] = jnp.clip(pairs_ref[...] - base, 0, 3 * REACH - 1).astype(jnp.float32)
    note[2:3, :] = jnp.full((1, note.shape[1]), count_ref[0], jnp.int32).astype(jnp.float32)
    notes = note[...].astype(jnp.bfloat16)
    for part in range(cut):
        out_ref[part, pl.ds(out_ref.shape[1] - NOTE_ROWS, NOTE_ROWS), :] = notes
    for s in range(segments):
        copies[s].wait()
        for block in range(blocks):
            rows = held[s, pl.ds(block * BLOCK, BLOCK), :]
            spectra = jnp.dot(rows, table_ref[...], preferred_element_type=jnp.float32)
            real_part, imag_part = spectra[:, :F], spectra[:, F:]
            power = real_part * real_part + imag_part * imag_part
            level = jnp.mean(power, axis=-1, keepdims=True)
            scale = lax.rsqrt(power + 0.1 * level + 1e-06)
            whitened = jnp.concatenate([real_part * scale, imag_part * scale], axis=1)
            whitened = whitened.astype(jnp.bfloat16)
            spot = pl.ds((block * segments + s) * width, width)
            if cut == 1:
                out_ref[0, spot, :] = whitened
            else:
                for part in range(cut):
                    piece = whitened[part * width : (part + 1) * width]
                    out_ref[jnp.bitwise_xor(mine, part), spot, :] = piece


def whitened_parts(records, block_pairs, slot_count, near, wins):
    segments, channels, length = records.shape
    blocks, parts = channels // BLOCK, near * wins
    width = BLOCK // parts
    packed = width % 16 == 0
    cut = parts if packed else 1
    rows = blocks * segments * BLOCK // cut
    hbm = pl.BlockSpec(memory_space=pl.ANY)
    vmem = pl.BlockSpec(memory_space=pltpu.VMEM)
    smem = pl.BlockSpec(memory_space=pltpu.SMEM)
    out = pl.pallas_call(
        functools.partial(spectra_kernel, near, wins),
        in_specs=[hbm, vmem, smem, vmem],
        out_specs=vmem,
        out_shape=jax.ShapeDtypeStruct((cut, rows + NOTE_ROWS, 2 * F), jnp.bfloat16),
        scratch_shapes=[
            pltpu.VMEM(records.shape, jnp.bfloat16),
            pltpu.VMEM((NOTE_ROWS, 2 * F), jnp.float32),
            pltpu.SemaphoreType.DMA((segments,)),
        ],
        compiler_params=pltpu.CompilerParams(vmem_limit_bytes=VMEM_LIMIT),
    )(records, block_pairs.T, slot_count, forward_table(length))
    if packed:
        return out
    mine = lax.axis_index("chan") % near * wins + lax.axis_index("win")
    split = out[0, :rows].reshape(blocks, segments, parts, width, 2 * F)
    split = split.transpose(2, 0, 1, 3, 4).reshape(parts, blocks * segments * width, 2 * F)
    split = jnp.take(split, jnp.bitwise_xor(mine, jnp.arange(parts)), axis=0)
    notes = jnp.broadcast_to(out[0, rows:], (parts, NOTE_ROWS, 2 * F))
    return jnp.concatenate([split, notes], axis=1)


def pair_kernel(near, wins, fold, firsts, seconds, counts, table_ref, *refs):
    chips = near // 2 * wins
    pieces, (out_ref, held, cross, sem) = refs[: 3 * chips], refs[3 * chips :]
    size = held.shape[0] // (3 * chips)
    copies = [
        pltpu.make_async_copy(
            piece.at[pl.ds(0, size)], held.at[pl.ds(k * size, size)], sem.at[k]
        )
        for k, piece in enumerate(pieces)
    ]
    for copy in copies:
        copy.start()
    for copy in copies:
        copy.wait()
    slots = cross.shape[0] // fold
    together = min(4, slots)
    plane = near // 2 * size
    rows = plane // REACH
    mine = lax.rem(lax.axis_index("chan"), near)

    def one_pair(owner, win, slot):
        index = owner * (slots * wins) + win * slots + slot
        first, second = firsts[index], seconds[index]
        real_sum = jnp.zeros((16, F), jnp.float32)
        imag_sum = jnp.zeros((16, F), jnp.float32)
        for w in range(wins):
            for r in range(0, rows, 16):
                a = held[pl.ds(pl.multiple_of(first + (w * plane + r), 16), 16), :]
                b = held[pl.ds(pl.multiple_of(second + (w * plane + r), 16), 16), :]
                a, b = a.astype(jnp.float32), b.astype(jnp.float32)
                ar, ai, br, bi = a[:, :F], a[:, F:], b[:, :F], b[:, F:]
                real_sum += ar * br + ai * bi
                imag_sum += ar * bi - ai * br
        spot = pl.ds(pl.multiple_of(slot * fold, fold), fold)
        cross[spot, pl.ds(0, F)] = real_sum
        cross[spot, pl.ds(F, F)] = imag_sum

    def part_of(part, _):
        owner, win = lax.div(part, wins), lax.rem(part, wins)

        def some_pairs(step, _):
            for k in range(together):
                one_pair(owner, win, step * together + k)
            return 0

        count = jnp.clip(counts[owner] - win * slots, 0, slots)
        lax.fori_loop(0, lax.div(count + (together - 1), together), some_pairs, 0)
        spectrum = cross[...]
        high = spectrum.astype(jnp.bfloat16)
        low = (spectrum - high.astype(jnp.float32)).astype(jnp.bfloat16)
        left = jnp.dot(high, table_ref[...], preferred_element_type=jnp.float32)
        right = jnp.dot(low, table_ref[:, :LAGS], preferred_element_type=jnp.float32)
        lagged = left[:, :LAGS] + (left[:, LAGS:] + right)
        member = jnp.bitwise_xor(owner, mine) * wins + win
        out_ref[member] = lagged if out_ref.dtype == jnp.float32 else encode(lagged)
        return 0

    lax.fori_loop(0, near * wins, part_of, 0)


def per_device(records, block_pairs, lag_low, lag_high, slot_count):
    segments, channels, length = records.shape
    blocks = channels // BLOCK
    chans, wins = lax.axis_size("chan"), lax.axis_size("win")
    both = ("chan", "win")
    near = REACH // blocks
    parts, chips, halves = near * wins, near // 2 * wins, near // 2
    width = BLOCK // parts
    rows = blocks * segments * width
    slots = block_pairs.shape[0]
    share = slots // wins
    group_total = chans // near
    group, member = lax.axis_index("chan") // near, lax.axis_index("chan") % near

    def partner(block, distance):
        return lax.ppermute(block, both, [(i, i ^ distance) for i in range(chans * wins)])

    def along(block, to):
        route = [(q * near + j, to(q) * near + j) for q in range(group_total) for j in range(near)]
        return lax.ppermute(block, "chan", [r for r in route if 0 <= r[1] < chans])

    split = whitened_parts(records, block_pairs, slot_count, near, wins)
    split = split.reshape(halves, 2, wins, rows + NOTE_ROWS, 2 * F)
    other = partner(split[:, 1], wins)
    keep = split[:, 0]

    planes, notes = [[], [], []], []
    for w in range(wins):
        for h in range(halves):
            piece = [keep[h, w, :rows], other[h, w, :rows]]
            if w == 0:
                piece += [keep[h, w, rows:], other[h, w, rows:]]
            piece = jnp.concatenate(piece, axis=0)
            if w or h:
                piece = partner(piece, h * 2 * wins + w)
            if w == 0:
                notes.append(piece[2 * rows :].reshape(2, NOTE_ROWS, 2 * F)[:, :3, :slots])
            sent = piece[: 2 * rows]
            planes[0].append(along(sent, lambda q: q ^ 1))
            planes[1].append(piece)
            planes[2].append(along(sent, lambda q: ((q + 1) ^ 1) - 1))

    notes = jnp.concatenate(notes, axis=0).astype(jnp.int32)
    level, rest = notes[:, :2] // REACH, notes[:, :2] % REACH
    level = jnp.where(group % 2 == 0, 2 - level, level)
    place = jnp.bitwise_xor(rest // blocks, member) * blocks + rest % blocks
    place = (level * (wins * REACH) + place) * (segments * width)
    firsts, seconds = place[:, 0].reshape(near * slots), place[:, 1].reshape(near * slots)
    counts = notes[:, 2, 0]

    fold = max(width, 16)
    scale = 2.0 ** math.floor(31 - 0.5 * math.log2(F * segments * wins))
    table = inverse_tables(length, scale / math.sqrt(F * segments * wins))
    hbm = pl.BlockSpec(memory_space=pl.ANY)
    smem = pl.BlockSpec(memory_space=pltpu.SMEM)
    vmem = pl.BlockSpec(memory_space=pltpu.VMEM)
    lagged = pl.pallas_call(
        functools.partial(pair_kernel, near, wins, fold),
        in_specs=[smem, smem, smem, vmem] + [hbm] * (3 * chips),
        out_specs=vmem,
        out_shape=jax.ShapeDtypeStruct(
            (parts, share * fold, LAGS), jnp.bfloat16 if fold == width else jnp.float32
        ),
        scratch_shapes=[
            pltpu.VMEM((3 * chips * 2 * rows, 2 * F), jnp.bfloat16),
            pltpu.VMEM((share * fold, 2 * F), jnp.float32),
            pltpu.SemaphoreType.DMA((3 * chips,)),
        ],
        compiler_params=pltpu.CompilerParams(vmem_limit_bytes=VMEM_LIMIT),
    )(firsts, seconds, counts, table, *planes[0], *planes[1], *planes[2])
    if fold > width:
        lagged = encode(lagged.reshape(parts, share, fold // width, width, LAGS).sum(axis=2))
        lagged = lagged.reshape(parts, share * width, LAGS)

    groups = [[q * parts + k for k in range(parts)] for q in range(group_total)]
    stack = lax.all_to_all(lagged, both, 0, 0, axis_index_groups=groups, tiled=True)
    stack = decode(stack.reshape(parts, share, width, LAGS), 1.0 / scale)
    stack = stack.transpose(1, 0, 2, 3).reshape(share, BLOCK, LAGS)
    start = lax.axis_index("win") * share
    low = lax.dynamic_slice_in_dim(lag_low, start, share)
    high = lax.dynamic_slice_in_dim(lag_high, start, share)
    lag_index = jnp.arange(LAGS, dtype=jnp.int32)[None, :]
    used = start + jnp.arange(share, dtype=jnp.int32) < slot_count[0]
    keep = (lag_index >= low[:, None]) & (lag_index < high[:, None]) & used[:, None]
    return jnp.where(keep[:, None, :], stack, jnp.zeros_like(stack))


def solution(mesh):
    in_specs = (P("win", "chan", None), P("chan", None), P("chan"), P("chan"), P("chan"))
    out_specs = P(("chan", "win"), None, None)
    return jax.shard_map(
        per_device, mesh=mesh, in_specs=in_specs, out_specs=out_specs, check_vma=False
    )
```

time: 82.6 us -> 65 us (0.79); the launches traced: 82.9 us -> 64 us
  blocking collectives: 26.6 us -> 0 us
  starting transfers between devices: 8.41 us -> 20.1 us
  Pallas kernels: 11.1 us -> 7.38 us
  waiting for transfers between devices: 31.5 us -> 28.8 us
  local copies, waits for them, and re-layouts: 3.24 us -> 4.54 us
  other arithmetic: 1.37 us -> 2.32 us
    all_to_all x2 -> x0, blocking collectives: 26.6 us -> none  [the longest x1 19.4 us: per_device(): own = exchange(whitened_parts(records, parts))]
    ppermute x2 -> x12, starting transfers between devices: 4.84 us -> 16.2 us  [the longest x8 11.1 us: along(): return lax.ppermute(block, 'chan', [r for r in route if 0 <= r[1] < chans])]
    all_to_all x1, waiting for transfers between devices: 14.2 us -> 8.6 us  [per_device(): lax.all_to_all(lagged, both, 0, 0, axis_index_groups=groups, tiled=True)]
    pallas_call x2, Pallas kernels: 11.1 us -> 7.38 us  [the longest x1 5.54 us: per_device(): pl.pallas_call(functools.partial(pair_kernel, near, wins, fold), in_specs...]
    ppermute x2 -> x12, waiting for transfers between devices: 17.2 us -> 20.2 us  [the longest x8 10.7 us: along(): return lax.ppermute(block, 'chan', [r for r in route if 0 <= r[1] < chans])]
    unnamed x12 -> x14, local copies, waits for them, and re-layouts: 2.56 us -> 3.24 us
  transfers between devices with their start and end apart: 3 -> 13, of which waited for: 3 -> 6; matrix products, arithmetic and copies ran while one was open for 1% -> 2% of each run, Pallas kernels for 0% -> 0%
where the time goes in v2:
time: 65 us; the launch traced here: 64 us
  waiting for transfers between devices  28.8 us (44%)
  starting transfers between devices  20.1 us (31%)
  Pallas kernels  7.38 us (11%)
  local copies, waits for them, and re-layouts  4.54 us (7%)
  other arithmetic  2.32 us (4%)
  between operations  0.89 us (1%)
    ppermute x8, starting transfers between devices, along(): return lax.ppermute(block, 'chan', [r for r in route if 0 <= r[1] < chans])  11.1 us
    ppermute x8, waiting for transfers between devices, along(): return lax.ppermute(block, 'chan', [r for r in route if 0 <= r[1] < chans])  10.7 us
    ppermute x4, waiting for transfers between devices, partner(): lax.ppermute(block, both, [(i, i ^ distance) for i in range(chans * wins)])  9.48 us
    all_to_all x1, waiting for transfers between devices, per_device(): lax.all_to_all(lagged, both, 0, 0, axis_index_groups=groups, tiled=True)  8.6 us
    pallas_call x1, Pallas kernels, per_device(): pl.pallas_call(functools.partial(pair_kernel, near, wins, fold), in_specs...  5.54 us
    ppermute x4, starting transfers between devices, partner(): lax.ppermute(block, both, [(i, i ^ distance) for i in range(chans * wins)])  5.13 us
    all_to_all x1, starting transfers between devices, per_device(): lax.all_to_all(lagged, both, 0, 0, axis_index_groups=groups, tiled=True)  3.91 us
    unnamed x14, local copies, waits for them, and re-layouts  3.24 us
  transfers between devices with their start and end apart: 13, of which 6 were waited for; matrix products, arithmetic and copies ran while one was open for 2% of the time, Pallas kernels for 0%

profile of v2, /device:TPU:0, one launch (start us, length us, event | category | flops | bytes accessed | tf_op | source)
XLA Modules:
  0.0 64.0 jit_solution(7353494070100884172)
XLA Ops:
  0.7 0.0 copy-start
  0.7 1.6 %copy-done = bf16[4,512,512]{2,1,0:T(8,128)(2,1)S(1)} copy-done((bf16[4,512,512]{2,1,0:T(8,128)(2,1)S(1)}, bf16[4,512,512]{2,1,0:T(8,128)(2,1)}, u32[]{:S(2)}) %copy-start) | copy-done | bytes 2097176
  2.2 0.9 %copy-done.1 = bf16[512,256]{1,0:T(8,128)(2,1)S(1)} copy-done((bf16[512,256]{1,0:T(8,128)(2,1)S(1)}, bf16[512,256]{1,0:T(8,128)(2,1)}, u32[]{:S(2)}) %copy-start.1) | copy-done | bytes 262168
  3.2 0.7 %copy-done.3 = s32[32,2]{0,1:T(2,128)S(1)} copy-done((s32[32,2]{0,1:T(2,128)S(1)}, s32[32,2]{0,1:T(2,128)}, u32[]{:S(2)}) %copy-start.3) | copy-done | bytes 280
  3.9 1.8 %shard_map.73 = bf16[8,272,256]{2,1,0:T(8,128)(2,1)S(1)} custom-call(bf16[4,512,512]{2,1,0:T(8,128)(2,1)S(1)} %copy-done, s32[2,32]{1,0:T(2,128)S(1)} %bitcast.49, s32[1]{0:T(128)} %copy.34.count_ref, bf16[512,256]{1,0:T(8,128)(2,1)S(1)} %copy-done.1), custom_call_target="tpu_custom_call" | custom-call | tf_op jit(solution)/shard_map/pallas_call | solution.py:100
  5.7 0.1 slice_bitcast_fusion.1
  5.8 0.5 collective-permute-start
  6.4 1.5 %collective-permute-done = bf16[2,2,272,256]{3,2,1,0:T(8,128)(2,1)S(1)} collective-permute-done((bf16[2,2,272,256]{3,2,1,0:T(8,128)(2,1)S(1)}, bf16[2,2,272,256]{3,2,1,0:T(8,128)(2,1)S(1)}, u32[]{:S(2)}, u32[]{:S(2)}) %collective-permute-start) | collective-permute-done | bytes 557088 | tf_op jit(solution)/shard_map/ppermute | solution.py:197
  8.0 3.9 %collective-permute-start.6 = (bf16[512,256]{1,0:T(8,128)(2,1)S(1)}, bf16[512,256]{1,0:T(8,128)(2,1)S(1)}, u32[]{:S(2)}, u32[]{:S(2)}) collective-permute-start(bf16[512,256]{1,0:T(8,128)(2,1)S(1)} %pad_maximum_fusion.4), channel_id=1, source_target_pairs={{0,5},{1,4},{2,7},{3,6},{4,1},{5,0},{6,3},{7,2},{8,13},{9,12},{10,... | collective-permute-start | bytes 786440 | tf_op jit(solution)/shard_map/ppermute | solution.py:197
  11.9 0.6 collective-permute-start.1
  12.5 0.1 collective-permute-start.4
  12.7 2.1 %collective-permute-start.2 = (bf16[512,256]{1,0:T(8,128)(2,1)S(1)}, bf16[512,256]{1,0:T(8,128)(2,1)S(1)}, u32[]{:S(2)}, u32[]{:S(2)}) collective-permute-start(bf16[512,256]{1,0:T(8,128)(2,1)S(1)} %pad_maximum_fusion.2), channel_id=1, source_target_pairs={{0,8},{2,10},{4,12},{6,14},{8,0},{10,2},{12,4},{14,6},{16,24},{18,... | collective-permute-start | bytes 786440 | tf_op jit(solution)/shard_map/ppermute | solution.py:201
  14.7 0.7 %collective-permute-start.8 = (bf16[512,256]{1,0:T(8,128)(2,1)S(1)}, bf16[512,256]{1,0:T(8,128)(2,1)S(1)}, u32[]{:S(2)}, u32[]{:S(2)}) collective-permute-start(bf16[512,256]{1,0:T(8,128)(2,1)S(1)} %pad_maximum_fusion.2), channel_id=1, source_target_pairs={{8,16},{10,18},{12,20},{14,22},{16,8},{18,10},{20,12},{22,14},{9,1... | collective-permute-start | bytes 786440 | tf_op jit(solution)/shard_map/ppermute | solution.py:201
  15.4 3.6 %collective-permute-done.6.refs_7_ = bf16[512,256]{1,0:T(8,128)(2,1)S(1)} collective-permute-done((bf16[512,256]{1,0:T(8,128)(2,1)S(1)}, bf16[512,256]{1,0:T(8,128)(2,1)S(1)}, u32[]{:S(2)}, u32[]{:S(2)}) %collective-permute-start.6) | collective-permute-done | bytes 262176 | tf_op jit(solution)/shard_map/ppermute | solution.py:197
  19.0 0.7 %collective-permute-start.11 = (bf16[512,256]{1,0:T(8,128)(2,1)S(1)}, bf16[512,256]{1,0:T(8,128)(2,1)S(1)}, u32[]{:S(2)}, u32[]{:S(2)}) collective-permute-start(bf16[512,256]{1,0:T(8,128)(2,1)S(1)} %collective-permute-done.6.refs_7_), channel_id=1, source_target_pairs={{8,16},{10,18},{12,20},{14,22},{16,8},{18,10},{20,12},{22,14},{9,1... | collective-permute-start | bytes 786440 | tf_op jit(solution)/shard_map/ppermute | solution.py:201
  19.7 4.4 %collective-permute-done.4.refs_6_ = bf16[512,256]{1,0:T(8,128)(2,1)S(1)} collective-permute-done((bf16[512,256]{1,0:T(8,128)(2,1)S(1)}, bf16[512,256]{1,0:T(8,128)(2,1)S(1)}, u32[]{:S(2)}, u32[]{:S(2)}) %collective-permute-start.4) | collective-permute-done | bytes 262176 | tf_op jit(solution)/shard_map/ppermute | solution.py:197
  24.1 1.8 %collective-permute-start.7 = (bf16[512,256]{1,0:T(8,128)(2,1)S(1)}, bf16[512,256]{1,0:T(8,128)(2,1)S(1)}, u32[]{:S(2)}, u32[]{:S(2)}) collective-permute-start(bf16[512,256]{1,0:T(8,128)(2,1)S(1)} %collective-permute-done.6.refs_7_), channel_id=1, source_target_pairs={{0,8},{2,10},{4,12},{6,14},{8,0},{10,2},{12,4},{14,6},{16,24},{18,... | collective-permute-start | bytes 786440 | tf_op jit(solution)/shard_map/ppermute | solution.py:201
  25.9 0.0 collective-permute-done.1.refs_5_
  25.9 0.7 %collective-permute-start.10 = (bf16[512,256]{1,0:T(8,128)(2,1)S(1)}, bf16[512,256]{1,0:T(8,128)(2,1)S(1)}, u32[]{:S(2)}, u32[]{:S(2)}) collective-permute-start(bf16[512,256]{1,0:T(8,128)(2,1)S(1)} %collective-permute-done.4.refs_6_), channel_id=1, source_target_pairs={{8,16},{10,18},{12,20},{14,22},{16,8},{18,10},{20,12},{22,14},{9,1... | collective-permute-start | bytes 786440 | tf_op jit(solution)/shard_map/ppermute | solution.py:201
  26.6 0.7 %slice.109 = bf16[512,256]{1,0:T(8,128)(2,1)} slice(bf16[544,256]{1,0:T(8,128)(2,1)S(1)} %collective-permute-done.1.refs_5_), slice={[0:512], [0:256]} | slice | bytes 524288 | tf_op jit(solution)/shard_map/slice | solution.py:219
  27.3 0.0 collective-permute-done.2.refs_0_
  27.3 4.4 %collective-permute-start.5 = (bf16[512,256]{1,0:T(8,128)(2,1)S(1)}, bf16[512,256]{1,0:T(8,128)(2,1)S(1)}, u32[]{:S(2)}, u32[]{:S(2)}) collective-permute-start(bf16[512,256]{1,0:T(8,128)(2,1)S(1)} %collective-permute-done.4.refs_6_), channel_id=1, source_target_pairs={{0,8},{2,10},{4,12},{6,14},{8,0},{10,2},{12,4},{14,6},{16,24},{18,... | collective-permute-start | bytes 786440 | tf_op jit(solution)/shard_map/ppermute | solution.py:201
  31.8 0.0 collective-permute-done.8.refs_8_
  31.8 0.1 collective-permute-start.3
  31.9 0.0 collective-permute-done.11.refs_11_
  31.9 0.7 %collective-permute-start.9 = (bf16[512,256]{1,0:T(8,128)(2,1)}, bf16[512,256]{1,0:T(8,128)(2,1)S(1)}, u32[]{:S(2)}, u32[]{:S(2)}) collective-permute-start(bf16[512,256]{1,0:T(8,128)(2,1)} %slice.109), channel_id=1, source_target_pairs={{8,16},{10,18},{12,20},{14,22},{16,8},{18,10},{20,12},{22,14},{9,1... | collective-permute-start | bytes 786440 | tf_op jit(solution)/shard_map/ppermute | solution.py:201
  32.6 0.1 reshape_squeeze.6.firsts
  32.7 0.1 reshape_squeeze.7.seconds
  32.7 0.1 convert_reduce_fusion.counts
  32.9 0.0 copy-start.5
  32.9 0.0 collective-permute-done.7.refs_3_
  32.9 0.0 collective-permute-done.10.refs_10_
  32.9 6.0 %collective-permute-done.5.refs_2_ = bf16[512,256]{1,0:T(8,128)(2,1)S(1)} collective-permute-done((bf16[512,256]{1,0:T(8,128)(2,1)S(1)}, bf16[512,256]{1,0:T(8,128)(2,1)S(1)}, u32[]{:S(2)}, u32[]{:S(2)}) %collective-permute-start.5) | collective-permute-done | bytes 262176 | tf_op jit(solution)/shard_map/ppermute | solution.py:201
  39.0 4.6 %collective-permute-done.3.refs_1_ = bf16[512,256]{1,0:T(8,128)(2,1)S(1)} collective-permute-done((bf16[512,256]{1,0:T(8,128)(2,1)}, bf16[512,256]{1,0:T(8,128)(2,1)S(1)}, u32[]{:S(2)}, u32[]{:S(2)}) %collective-permute-start.3) | collective-permute-done | bytes 262176 | tf_op jit(solution)/shard_map/ppermute | solution.py:201
  43.6 0.0 collective-permute-done.9.refs_9_
  43.6 0.0 copy-done.2
  43.6 5.5 %shard_map.74 = bf16[8,256,128]{2,1,0:T(8,128)(2,1)} custom-call(s32[128]{0:T(128)S(1)} %reshape_squeeze.6.firsts, s32[128]{0:T(128)S(1)} %reshape_squeeze.7.seconds, s32[4]{0:T(128)S(1)} %convert_reduce_fusion.counts, bf16[256,256]{1,0:T(8,128)(2,1)S(1)} %copy-done.2, bf16[512,256]{1,0:T(8,128)(2,1)S(1)} %collective-permute-done.2.refs_0_, ...), custom_call_target="tpu_custom_call" | custom-call | tf_op jit(solution)/shard_map/pallas_call | solution.py:238
  49.1 3.9 %all-to-all-start = ((bf16[8,256,128]{2,1,0:T(8,128)(2,1)}), bf16[8,256,128]{2,1,0:T(8,128)(2,1)S(1)}, u32[]{:S(2)}, u32[]{:S(2)}) async-start(bf16[8,256,128]{2,1,0:T(8,128)(2,1)} %shard_map.74), calls=%async_computation | async-start | bytes 1048576 | tf_op jit(solution)/shard_map/all_to_all | solution.py:257
  53.0 0.0 copy-done.4
  53.0 0.1 dynamic_slice.6
  53.1 0.1 dynamic_slice.7
  53.2 0.1 fusion.5
  53.3 8.6 %all-to-all-done = bf16[8,256,128]{2,1,0:T(8,128)(2,1)S(1)} async-done(((bf16[8,256,128]{2,1,0:T(8,128)(2,1)}), bf16[8,256,128]{2,1,0:T(8,128)(2,1)S(1)}, u32[]{:S(2)}, u32[]{:S(2)}) %all-to-all-start) | async-done | bytes 524320 | tf_op jit(solution)/shard_map/all_to_all | solution.py:257
  61.9 0.6 fusion.2
  62.5 0.2 convert_compare_fusion
  62.7 0.1 fusion.3
  62.8 0.1 copy.29
  62.9 1.1 %bitcast_select_fusion = f32[16,128,128]{2,1,0:T(8,128)} fusion(f32[16,8,16,128]{3,2,1,0:T(8,128)S(1)} %copy.29, pred[16,128]{1,0:T(8,128)(4,1)S(1)} %fusion.5), kind=kLoop, calls=%fused_computation.7 | loop fusion | flops 262144 | bytes 2099200 | tf_op jit(solution)/shard_map/jit(_where)/select_n | solution.py:266
  (24 shorter events, 0.3 us)
Async XLA Ops:
  0.7 1.6 %copy-start = (bf16[4,512,512]{2,1,0:T(8,128)(2,1)S(1)}, bf16[4,512,512]{2,1,0:T(8,128)(2,1)}, u32[]{:S(2)}) copy-start(bf16[4,512,512]{2,1,0:T(8,128)(2,1)} %records.1) | copy-start | bytes 6291460
  2.2 0.9 %copy-start.1 = (bf16[512,256]{1,0:T(8,128)(2,1)S(1)}, bf16[512,256]{1,0:T(8,128)(2,1)}, u32[]{:S(2)}) copy-start(bf16[512,256]{1,0:T(8,128)(2,1)} %constant.98.table_ref) | copy-start | bytes 786436
  3.2 0.7 %copy-start.3 = (s32[32,2]{0,1:T(2,128)S(1)}, s32[32,2]{0,1:T(2,128)}, u32[]{:S(2)}) copy-start(s32[32,2]{0,1:T(2,128)} %param.8) | copy-start | bytes 772
  5.8 2.1 %collective-permute-start = (bf16[2,2,272,256]{3,2,1,0:T(8,128)(2,1)S(1)}, bf16[2,2,272,256]{3,2,1,0:T(8,128)(2,1)S(1)}, u32[]{:S(2)}, u32[]{:S(2)}) collective-permute-start(bf16[2,2,272,256]{3,2,1,0:T(8,128)(2,1)S(1)} %get-tuple-element.6), channel_id=1, source_target_pairs={{0,2},{1,3},{2,0},{3,1},{4,6},{5,7},{6,4},{7,5},{8,10},{9,11},{10,... | collective-permute-start | bytes 1671176 | tf_op jit(solution)/shard_map/ppermute | solution.py:197
  8.0 11.0 %collective-permute-start.6 = (bf16[512,256]{1,0:T(8,128)(2,1)S(1)}, bf16[512,256]{1,0:T(8,128)(2,1)S(1)}, u32[]{:S(2)}, u32[]{:S(2)}) collective-permute-start(bf16[512,256]{1,0:T(8,128)(2,1)S(1)} %pad_maximum_fusion.4), channel_id=1, source_target_pairs={{0,5},{1,4},{2,7},{3,6},{4,1},{5,0},{6,3},{7,2},{8,13},{9,12},{10,... | collective-permute-start | bytes 786440 | tf_op jit(solution)/shard_map/ppermute | solution.py:197
  11.9 14.0 %collective-permute-start.1 = (bf16[544,256]{1,0:T(8,128)(2,1)S(1)}, bf16[544,256]{1,0:T(8,128)(2,1)S(1)}, u32[]{:S(2)}, u32[]{:S(2)}) collective-permute-start(bf16[544,256]{1,0:T(8,128)(2,1)S(1)} %pad_maximum_fusion), channel_id=1, source_target_pairs={{0,4},{1,5},{2,6},{3,7},{4,0},{5,1},{6,2},{7,3},{8,12},{9,13},{10,... | collective-permute-start | bytes 835592 | tf_op jit(solution)/shard_map/ppermute | solution.py:197
  12.5 31.1 %copy-start.2 = (bf16[256,256]{1,0:T(8,128)(2,1)S(1)}, bf16[256,256]{1,0:T(8,128)(2,1)}, u32[]{:S(2)}) copy-start(bf16[256,256]{1,0:T(8,128)(2,1)} %constant.96.clone.table_ref) | copy-start | bytes 393220
  12.5 11.6 %collective-permute-start.4 = (bf16[512,256]{1,0:T(8,128)(2,1)S(1)}, bf16[512,256]{1,0:T(8,128)(2,1)S(1)}, u32[]{:S(2)}, u32[]{:S(2)}) collective-permute-start(bf16[512,256]{1,0:T(8,128)(2,1)S(1)} %pad_maximum_fusion.3), channel_id=1, source_target_pairs={{0,1},{1,0},{2,3},{3,2},{4,5},{5,4},{6,7},{7,6},{8,9},{9,8},{10,11... | collective-permute-start | bytes 786440 | tf_op jit(solution)/shard_map/ppermute | solution.py:197
  12.7 14.6 %collective-permute-start.2 = (bf16[512,256]{1,0:T(8,128)(2,1)S(1)}, bf16[512,256]{1,0:T(8,128)(2,1)S(1)}, u32[]{:S(2)}, u32[]{:S(2)}) collective-permute-start(bf16[512,256]{1,0:T(8,128)(2,1)S(1)} %pad_maximum_fusion.2), channel_id=1, source_target_pairs={{0,8},{2,10},{4,12},{6,14},{8,0},{10,2},{12,4},{14,6},{16,24},{18,... | collective-permute-start | bytes 786440 | tf_op jit(solution)/shard_map/ppermute | solution.py:201
  14.7 17.0 %collective-permute-start.8 = (bf16[512,256]{1,0:T(8,128)(2,1)S(1)}, bf16[512,256]{1,0:T(8,128)(2,1)S(1)}, u32[]{:S(2)}, u32[]{:S(2)}) collective-permute-start(bf16[512,256]{1,0:T(8,128)(2,1)S(1)} %pad_maximum_fusion.2), channel_id=1, source_target_pairs={{8,16},{10,18},{12,20},{14,22},{16,8},{18,10},{20,12},{22,14},{9,1... | collective-permute-start | bytes 786440 | tf_op jit(solution)/shard_map/ppermute | solution.py:201
  19.0 12.9 %collective-permute-start.11 = (bf16[512,256]{1,0:T(8,128)(2,1)S(1)}, bf16[512,256]{1,0:T(8,128)(2,1)S(1)}, u32[]{:S(2)}, u32[]{:S(2)}) collective-permute-start(bf16[512,256]{1,0:T(8,128)(2,1)S(1)} %collective-permute-done.6.refs_7_), channel_id=1, source_target_pairs={{8,16},{10,18},{12,20},{14,22},{16,8},{18,10},{20,12},{22,14},{9,1... | collective-permute-start | bytes 786440 | tf_op jit(solution)/shard_map/ppermute | solution.py:201
  24.1 8.8 %collective-permute-start.7 = (bf16[512,256]{1,0:T(8,128)(2,1)S(1)}, bf16[512,256]{1,0:T(8,128)(2,1)S(1)}, u32[]{:S(2)}, u32[]{:S(2)}) collective-permute-start(bf16[512,256]{1,0:T(8,128)(2,1)S(1)} %collective-permute-done.6.refs_7_), channel_id=1, source_target_pairs={{0,8},{2,10},{4,12},{6,14},{8,0},{10,2},{12,4},{14,6},{16,24},{18,... | collective-permute-start | bytes 786440 | tf_op jit(solution)/shard_map/ppermute | solution.py:201
  25.9 7.0 %collective-permute-start.10 = (bf16[512,256]{1,0:T(8,128)(2,1)S(1)}, bf16[512,256]{1,0:T(8,128)(2,1)S(1)}, u32[]{:S(2)}, u32[]{:S(2)}) collective-permute-start(bf16[512,256]{1,0:T(8,128)(2,1)S(1)} %collective-permute-done.4.refs_6_), channel_id=1, source_target_pairs={{8,16},{10,18},{12,20},{14,22},{16,8},{18,10},{20,12},{22,14},{9,1... | collective-permute-start | bytes 786440 | tf_op jit(solution)/shard_map/ppermute | solution.py:201
  27.3 11.6 %collective-permute-start.5 = (bf16[512,256]{1,0:T(8,128)(2,1)S(1)}, bf16[512,256]{1,0:T(8,128)(2,1)S(1)}, u32[]{:S(2)}, u32[]{:S(2)}) collective-permute-start(bf16[512,256]{1,0:T(8,128)(2,1)S(1)} %collective-permute-done.4.refs_6_), channel_id=1, source_target_pairs={{0,8},{2,10},{4,12},{6,14},{8,0},{10,2},{12,4},{14,6},{16,24},{18,... | collective-permute-start | bytes 786440 | tf_op jit(solution)/shard_map/ppermute | solution.py:201
  31.8 11.8 %collective-permute-start.3 = (bf16[512,256]{1,0:T(8,128)(2,1)}, bf16[512,256]{1,0:T(8,128)(2,1)S(1)}, u32[]{:S(2)}, u32[]{:S(2)}) collective-permute-start(bf16[512,256]{1,0:T(8,128)(2,1)} %slice.109), channel_id=1, source_target_pairs={{0,8},{2,10},{4,12},{6,14},{8,0},{10,2},{12,4},{14,6},{16,24},{18,... | collective-permute-start | bytes 786440 | tf_op jit(solution)/shard_map/ppermute | solution.py:201
  31.9 11.7 %collective-permute-start.9 = (bf16[512,256]{1,0:T(8,128)(2,1)}, bf16[512,256]{1,0:T(8,128)(2,1)S(1)}, u32[]{:S(2)}, u32[]{:S(2)}) collective-permute-start(bf16[512,256]{1,0:T(8,128)(2,1)} %slice.109), channel_id=1, source_target_pairs={{8,16},{10,18},{12,20},{14,22},{16,8},{18,10},{20,12},{22,14},{9,1... | collective-permute-start | bytes 786440 | tf_op jit(solution)/shard_map/ppermute | solution.py:201
  32.9 20.2 %copy-start.4 = (s32[32]{0:T(128)S(1)}, s32[32]{0:T(128)}, u32[]{:S(2)}) copy-start(s32[32]{0:T(128)} %param.9) | copy-start | bytes 388
  32.9 20.3 %copy-start.5 = (s32[32]{0:T(128)S(1)}, s32[32]{0:T(128)}, u32[]{:S(2)}) copy-start(s32[32]{0:T(128)} %param.10) | copy-start | bytes 388
  49.1 12.8 %all-to-all-start = ((bf16[8,256,128]{2,1,0:T(8,128)(2,1)}), bf16[8,256,128]{2,1,0:T(8,128)(2,1)S(1)}, u32[]{:S(2)}, u32[]{:S(2)}) async-start(bf16[8,256,128]{2,1,0:T(8,128)(2,1)} %shard_map.74), calls=%async_computation | async-start | bytes 1048576 | tf_op jit(solution)/shard_map/all_to_all | solution.py:257

commit v3 on v2

v3 whole, which is shorter than its diff:
```python
import functools
import math

import jax
import jax.numpy as jnp
import numpy as np
from jax import lax
from jax.experimental import pallas as pl
from jax.experimental.pallas import tpu as pltpu
from jax.sharding import PartitionSpec as P

BLOCK = 128
F = 128
LAGS = 128
REACH = 16
NOTE_ROWS = 16
VMEM_LIMIT = 48 * 1024 * 1024
SPECTRA_VMEM = VMEM_LIMIT


def forward_table(length):
    first = length // 32
    times = np.arange(length, dtype=np.int64)[:, None]
    freqs = (first + np.arange(F, dtype=np.int64))[None, :]
    phase = 2.0 * math.pi / length * (times * freqs % length)
    table = np.concatenate([np.cos(phase), -np.sin(phase)], axis=1)
    return jnp.asarray(table.astype(np.float32)).astype(jnp.bfloat16)


def inverse_tables(length, factor):
    first = length // 32
    freqs = (first + np.arange(F, dtype=np.int64))[:, None]
    shifts = (np.arange(LAGS, dtype=np.int64) - LAGS // 2)[None, :]
    phase = 2.0 * math.pi / length * (freqs * shifts % length)
    table = (np.concatenate([np.cos(phase), -np.sin(phase)], axis=0) * factor).astype(np.float32)
    high = table.astype(jnp.bfloat16)
    low = (table - high.astype(np.float32)).astype(jnp.bfloat16)
    return jnp.asarray(np.concatenate([high, low], axis=1))


def encode(values):
    values = values * jnp.abs(values)
    return (values * jnp.abs(values)).astype(jnp.bfloat16)


def spectra_kernel(near, wins, records, pairs, count_ref, table, out_ref, held, pairs_held, table_held, note, sem):
    segments, channels, _ = records.shape
    cut, blocks = out_ref.shape[0], channels // BLOCK
    width = BLOCK // cut
    chan = lax.axis_index("chan")
    mine = lax.rem(chan, near) * wins + lax.axis_index("win")
    copies = [
        pltpu.make_async_copy(records.at[s], held.at[s], sem.at[s]) for s in range(segments)
    ]
    table_copy = pltpu.make_async_copy(table, table_held, sem.at[segments])
    pairs_copy = pltpu.make_async_copy(pairs, pairs_held, sem.at[segments + 1])
    table_copy.start()
    for copy in copies:
        copy.start()
    pairs_copy.start()
    table_copy.wait()
    for s in range(segments):
        copies[s].wait()
        for block in range(blocks):
            rows = held[s, pl.ds(block * BLOCK, BLOCK), :]
            spectra = jnp.dot(rows, table_held[...], preferred_element_type=jnp.float32)
            real_part, imag_part = spectra[:, :F], spectra[:, F:]
            power = real_part * real_part + imag_part * imag_part
            level = jnp.mean(power, axis=-1, keepdims=True)
            scale = lax.rsqrt(power + 0.1 * level + 1e-06)
            whitened = jnp.concatenate([real_part * scale, imag_part * scale], axis=1)
            whitened = whitened.astype(jnp.bfloat16)
            spot = pl.ds((block * segments + s) * width, width)
            if cut == 1:
                out_ref[0, spot, :] = whitened
            else:
                for part in range(cut):
                    piece = whitened[part * width : (part + 1) * width]
                    out_ref[jnp.bitwise_xor(mine, part), spot, :] = piece
    pairs_copy.wait()
    base = (lax.div(chan, near) - 1) * REACH
    slots = pairs.shape[1]
    note[...] = jnp.zeros_like(note)
    note[0:2, 0:slots] = jnp.clip(pairs_held[...] - base, 0, 3 * REACH - 1).astype(jnp.float32)
    note[2:3, :] = jnp.full((1, note.shape[1]), count_ref[0], jnp.int32).astype(jnp.float32)
    notes = note[...].astype(jnp.bfloat16)
    for part in range(cut):
        out_ref[part, pl.ds(out_ref.shape[1] - NOTE_ROWS, NOTE_ROWS), :] = notes


def whitened_parts(records, block_pairs, slot_count, near, wins):
    segments, channels, length = records.shape
    blocks, parts = channels // BLOCK, near * wins
    width = BLOCK // parts
    packed = width % 16 == 0
    cut = parts if packed else 1
    rows = blocks * segments * BLOCK // cut
    hbm = pl.BlockSpec(memory_space=pl.ANY)
    vmem = pl.BlockSpec(memory_space=pltpu.VMEM)
    smem = pl.BlockSpec(memory_space=pltpu.SMEM)
    out = pl.pallas_call(
        functools.partial(spectra_kernel, near, wins),
        in_specs=[hbm, hbm, smem, hbm],
        out_specs=vmem,
        out_shape=jax.ShapeDtypeStruct((cut, rows + NOTE_ROWS, 2 * F), jnp.bfloat16),
        scratch_shapes=[
            pltpu.VMEM(records.shape, jnp.bfloat16),
            pltpu.VMEM(block_pairs.shape[::-1], jnp.int32),
            pltpu.VMEM((length, 2 * F), jnp.bfloat16),
            pltpu.VMEM((NOTE_ROWS, 2 * F), jnp.float32),
            pltpu.SemaphoreType.DMA((segments + 2,)),
        ],
        compiler_params=pltpu.CompilerParams(vmem_limit_bytes=SPECTRA_VMEM),
    )(records, block_pairs.T, slot_count, forward_table(length))
    if packed:
        return out
    mine = lax.axis_index("chan") % near * wins + lax.axis_index("win")
    split = out[0, :rows].reshape(blocks, segments, parts, width, 2 * F)
    split = split.transpose(2, 0, 1, 3, 4).reshape(parts, blocks * segments * width, 2 * F)
    split = jnp.take(split, jnp.bitwise_xor(mine, jnp.arange(parts)), axis=0)
    notes = jnp.broadcast_to(out[0, rows:], (parts, NOTE_ROWS, 2 * F))
    return jnp.concatenate([split, notes], axis=1)


def gather_pieces(pieces, held, sem):
    size = held.shape[0] // len(pieces)
    copies = [
        pltpu.make_async_copy(
            piece.at[pl.ds(0, size)], held.at[pl.ds(k * size, size)], sem.at[k]
        )
        for k, piece in enumerate(pieces)
    ]
    for copy in copies:
        copy.start()
    for copy in copies:
        copy.wait()


def add_pairs(near, wins, windows, fold, firsts, seconds, counts, held, before, cross):
    plane = held.shape[0] // (3 * windows)
    rows = plane // REACH
    slots = cross.shape[0] // (near * wins * fold)
    together = min(4, slots)

    def one_pair(index):
        first, second = firsts[index], seconds[index]
        spot = pl.ds(pl.multiple_of(index * fold, fold), fold)
        if before is None:
            real_sum = jnp.zeros((fold, F), jnp.float32)
            imag_sum = jnp.zeros((fold, F), jnp.float32)
        else:
            real_sum = before[spot, pl.ds(0, F)]
            imag_sum = before[spot, pl.ds(F, F)]
        for w in range(windows):
            for r in range(0, rows, 16):
                a = held[pl.ds(pl.multiple_of(first + (w * plane + r), 16), 16), :]
                b = held[pl.ds(pl.multiple_of(second + (w * plane + r), 16), 16), :]
                a, b = a.astype(jnp.float32), b.astype(jnp.float32)
                ar, ai, br, bi = a[:, :F], a[:, F:], b[:, :F], b[:, F:]
                real_sum += ar * br + ai * bi
                imag_sum += ar * bi - ai * br
        cross[spot, pl.ds(0, F)] = real_sum
        cross[spot, pl.ds(F, F)] = imag_sum

    def owner_of(owner, _):
        def some_pairs(step, _):
            for k in range(together):
                one_pair(owner * (slots * wins) + step * together + k)
            return 0

        count = jnp.clip(counts[owner], 0, slots * wins)
        lax.fori_loop(0, lax.div(count + (together - 1), together), some_pairs, 0)
        return 0

    lax.fori_loop(0, near, owner_of, 0)


def first_kernel(near, wins, fold, firsts, seconds, counts, *refs):
    pieces, (cross, held, sem) = refs[:-3], refs[-3:]
    gather_pieces(pieces, held, sem)
    add_pairs(near, wins, 1, fold, firsts, seconds, counts, held, None, cross)


def last_kernel(near, wins, fold, firsts, seconds, counts, before, table_ref, *refs):
    pieces, (out_ref, held, cross, sem) = refs[:-4], refs[-4:]
    gather_pieces(pieces, held, sem)
    add_pairs(near, wins, wins - 1, fold, firsts, seconds, counts, held, before, cross)
    mine = lax.rem(lax.axis_index("chan"), near)
    span = cross.shape[0] // near
    for owner in range(near):
        spectrum = cross[pl.ds(owner * span, span), :]
        high = spectrum.astype(jnp.bfloat16)
        low = (spectrum - high.astype(jnp.float32)).astype(jnp.bfloat16)
        left = jnp.dot(high, table_ref[...], preferred_element_type=jnp.float32)
        right = jnp.dot(low, table_ref[:, :LAGS], preferred_element_type=jnp.float32)
        lagged = left[:, :LAGS] + (left[:, LAGS:] + right)
        lagged = lagged if out_ref.dtype == jnp.float32 else encode(lagged)
        out_ref[jnp.bitwise_xor(owner, mine)] = lagged


def stack_kernel(share, scale, code, low_ref, high_ref, count_ref, out, held, sem):
    parts, width = code.shape[0], code.shape[1] // share
    start = lax.axis_index("win") * share
    lag_index = lax.broadcasted_iota(jnp.int32, (parts, width, LAGS), 2)
    together = min(4, share)
    copies = []
    for slot in range(share):
        values = code[:, pl.ds(slot * width, width), :].astype(jnp.float32)
        root = lax.rsqrt(lax.rsqrt(jnp.abs(values))) * scale
        root = jnp.where(values < 0, -root, root)
        used = start + slot < count_ref[0]
        high = jnp.where(used, high_ref[start + slot], 0)
        keep = (lag_index >= low_ref[start + slot]) & (lag_index < high)
        held[slot] = jnp.where(keep, root, 0.0).reshape(BLOCK, LAGS)
        if slot % together == together - 1:
            spot = pl.ds(slot + 1 - together, together)
            copies.append(pltpu.make_async_copy(held.at[spot], out.at[spot], sem.at[len(copies)]))
            copies[-1].start()
    for copy in copies:
        copy.wait()


def per_device(records, block_pairs, lag_low, lag_high, slot_count):
    segments, channels, length = records.shape
    blocks = channels // BLOCK
    chans, wins = lax.axis_size("chan"), lax.axis_size("win")
    both = ("chan", "win")
    near = REACH // blocks
    parts, chips, halves = near * wins, near // 2 * wins, near // 2
    width = BLOCK // parts
    rows = blocks * segments * width
    slots = block_pairs.shape[0]
    share = slots // wins
    group_total = chans // near
    group, member = lax.axis_index("chan") // near, lax.axis_index("chan") % near

    def partner(block, distance):
        return lax.ppermute(block, both, [(i, i ^ distance) for i in range(chans * wins)])

    def along(block, to):
        route = [(q * near + j, to(q) * near + j) for q in range(group_total) for j in range(near)]
        return lax.ppermute(block, "chan", [r for r in route if 0 <= r[1] < chans])

    split = whitened_parts(records, block_pairs, slot_count, near, wins)
    split = split.reshape(halves, 2, wins, rows + NOTE_ROWS, 2 * F)
    other = partner(split[:, 1], wins)
    keep = split[:, 0]

    planes, notes = [[], [], []], []
    for w in range(wins):
        for h in range(halves):
            piece = [keep[h, w, :rows], other[h, w, :rows]]
            if w == 0:
                piece += [keep[h, w, rows:], other[h, w, rows:]]
            piece = jnp.concatenate(piece, axis=0)
            if len(planes[1]) >= 3:
                piece = lax.optimization_barrier((piece, planes[1][-2]))[0]
            if w or h:
                piece = partner(piece, h * 2 * wins + w)
            if w == 0:
                notes.append(piece[2 * rows :].reshape(2, NOTE_ROWS, 2 * F)[:, :3, :slots])
            sent = piece[: 2 * rows]
            if len(planes[0]) >= 2:
                sent = lax.optimization_barrier((sent, planes[0][-2], planes[2][-2]))[0]
            planes[0].append(along(sent, lambda q: q ^ 1))
            planes[1].append(piece)
            planes[2].append(along(sent, lambda q: ((q + 1) ^ 1) - 1))

    notes = jnp.concatenate(notes, axis=0).astype(jnp.int32)
    level, rest = notes[:, :2] // REACH, notes[:, :2] % REACH
    level = jnp.where(group % 2 == 0, 2 - level, level)
    place = jnp.bitwise_xor(rest // blocks, member) * blocks + rest % blocks
    def first_row(windows):
        row = (level * (windows * REACH) + place) * (segments * width)
        return row[:, 0].reshape(near * slots), row[:, 1].reshape(near * slots), counts

    counts = notes[:, 2, 0]
    fold = max(width, 16)
    scale = 2.0 ** math.floor(31 - 0.5 * math.log2(F * segments * wins))
    table = inverse_tables(length, scale / math.sqrt(F * segments * wins))
    hbm = pl.BlockSpec(memory_space=pl.ANY)
    smem = pl.BlockSpec(memory_space=pltpu.SMEM)
    vmem = pl.BlockSpec(memory_space=pltpu.VMEM)
    params = pltpu.CompilerParams(vmem_limit_bytes=VMEM_LIMIT)
    cross = jax.ShapeDtypeStruct((near * slots * fold, 2 * F), jnp.float32)
    first = [plane[:halves] for plane in planes]
    first = first[0] + first[1] + first[2]
    before = pl.pallas_call(
        functools.partial(first_kernel, near, wins, fold),
        in_specs=[smem, smem, smem] + [hbm] * len(first),
        out_specs=vmem,
        out_shape=cross,
        scratch_shapes=[
            pltpu.VMEM((len(first) * 2 * rows, 2 * F), jnp.bfloat16),
            pltpu.SemaphoreType.DMA((len(first),)),
        ],
        compiler_params=params,
    )(*first_row(1), *first)
    last = [plane[halves:] for plane in planes]
    last = last[0] + last[1] + last[2]
    lagged = pl.pallas_call(
        functools.partial(last_kernel, near, wins, fold),
        in_specs=[smem, smem, smem, vmem, vmem] + [hbm] * len(last),
        out_specs=vmem,
        out_shape=jax.ShapeDtypeStruct(
            (near, slots * fold, LAGS), jnp.bfloat16 if fold == width else jnp.float32
        ),
        scratch_shapes=[
            pltpu.VMEM((len(last) * 2 * rows, 2 * F), jnp.bfloat16),
            pltpu.VMEM(cross.shape, jnp.float32),
            pltpu.SemaphoreType.DMA((len(last),)),
        ],
        compiler_params=params,
    )(*first_row(wins - 1), before, table, *last)
    if fold > width:
        lagged = encode(lagged.reshape(near, slots, fold // width, width, LAGS).sum(axis=2))
    lagged = lagged.reshape(parts, share * width, LAGS)

    groups = [[q * parts + k for k in range(parts)] for q in range(group_total)]
    stack = lax.all_to_all(lagged, both, 0, 0, axis_index_groups=groups, tiled=True)
    return pl.pallas_call(
        functools.partial(stack_kernel, share, 1.0 / scale),
        in_specs=[vmem, smem, smem, smem],
        out_specs=hbm,
        out_shape=jax.ShapeDtypeStruct((share, BLOCK, LAGS), jnp.float32),
        scratch_shapes=[
            pltpu.VMEM((share, BLOCK, LAGS), jnp.float32),
            pltpu.SemaphoreType.DMA((max(1, share // 4),)),
        ],
        compiler_params=params,
    )(stack, lag_low, lag_high, slot_count)


def solution(mesh):
    in_specs = (P("win", "chan", None), P("chan", None), P("chan"), P("chan"), P("chan"))
    out_specs = P(("chan", "win"), None, None)
    return jax.shard_map(
        per_device, mesh=mesh, in_specs=in_specs, out_specs=out_specs, check_vma=False
    )
```

time: 65 us -> 57.8 us (0.89)
  waiting for transfers between devices: 28.8 us -> 6.72 us
  blocking collectives: 0 us -> 12.8 us
  starting transfers between devices: 20.1 us -> 24.6 us
  other arithmetic: 2.32 us -> 0.26 us
  Pallas kernels: 7.38 us -> 8.5 us
  local copies, waits for them, and re-layouts: 4.54 us -> 3.6 us
    all_to_all x0 -> x1, blocking collectives: none -> 12.8 us  [per_device(): lax.all_to_all(lagged, both, 0, 0, axis_index_groups=groups, tiled=True)]
    all_to_all x1 -> x0, waiting for transfers between devices: 8.6 us -> none  [per_device(): lax.all_to_all(lagged, both, 0, 0, axis_index_groups=groups, tiled=True)]
    ppermute x8, waiting for transfers between devices: 10.7 us -> 2.19 us  [along(): return lax.ppermute(block, 'chan', [r for r in route if 0 <= r[1] < chans])]
    ppermute x8, starting transfers between devices: 11.1 us -> 17.1 us  [along(): return lax.ppermute(block, 'chan', [r for r in route if 0 <= r[1] < chans])]
    ppermute x4, waiting for transfers between devices: 9.48 us -> 4.54 us  [partner(): lax.ppermute(block, both, [(i, i ^ distance) for i in range(chans * wins)])]
    all_to_all x1 -> x0, starting transfers between devices: 3.91 us -> none  [per_device(): lax.all_to_all(lagged, both, 0, 0, axis_index_groups=groups, tiled=True)]
    ppermute x4, starting transfers between devices: 5.13 us -> 7.53 us  [partner(): lax.ppermute(block, both, [(i, i ^ distance) for i in range(chans * wins)])]
    select_n x1 -> x0, other arithmetic: 1.08 us -> none  [per_device(): return jnp.where(keep[:, None, :], stack, jnp.zeros_like(stack))]
  transfers between devices with their start and end apart: 13 -> 12, of which waited for: 6 -> 3; matrix products, arithmetic and copies ran while one was open for 2% -> 1% of each run, Pallas kernels for 0% -> 4%
where the time goes in v3:
time: 57.8 us; the launch traced here: 57.3 us
  starting transfers between devices  24.6 us (43%)
  blocking collectives  12.8 us (22%)
  Pallas kernels  8.5 us (15%)
  waiting for transfers between devices  6.72 us (12%)
  local copies, waits for them, and re-layouts  3.6 us (6%)
  between operations  0.89 us (2%)
    ppermute x8, starting transfers between devices, along(): return lax.ppermute(block, 'chan', [r for r in route if 0 <= r[1] < chans])  17.1 us
    all_to_all x1, blocking collectives, per_device(): lax.all_to_all(lagged, both, 0, 0, axis_index_groups=groups, tiled=True)  12.8 us
    ppermute x4, starting transfers between devices, partner(): lax.ppermute(block, both, [(i, i ^ distance) for i in range(chans * wins)])  7.53 us
    ppermute x4, waiting for transfers between devices, partner(): lax.ppermute(block, both, [(i, i ^ distance) for i in range(chans * wins)])  4.54 us
    unnamed x14, local copies, waits for them, and re-layouts  3.24 us
    pallas_call x1, Pallas kernels, per_device(): pl.pallas_call(functools.partial(last_kernel, near, wins, fold), in_specs...  2.88 us
    ppermute x8, waiting for transfers between devices, along(): return lax.ppermute(block, 'chan', [r for r in route if 0 <= r[1] < chans])  2.19 us
    pallas_call x1, Pallas kernels, per_device(): pl.pallas_call(functools.partial(first_kernel, near, wins, fold), in_spec...  2.11 us
  transfers between devices with their start and end apart: 12, of which 3 were waited for; matrix products, arithmetic and copies ran while one was open for 1% of the time, Pallas kernels for 4%

profile of v3, /device:TPU:0, one launch (start us, length us, event | category | flops | bytes accessed | tf_op | source)
XLA Modules:
  0.0 57.3 jit_solution(6994555231329268074)
XLA Ops:
  0.7 0.0 copy-start
  0.7 1.6 %copy-done = bf16[4,512,512]{2,1,0:T(8,128)(2,1)S(1)} copy-done((bf16[4,512,512]{2,1,0:T(8,128)(2,1)S(1)}, bf16[4,512,512]{2,1,0:T(8,128)(2,1)}, u32[]{:S(2)}) %copy-start) | copy-done | bytes 2097176
  2.2 0.0 copy-start.1
  2.2 0.9 %copy-done.1 = bf16[512,256]{1,0:T(8,128)(2,1)S(1)} copy-done((bf16[512,256]{1,0:T(8,128)(2,1)S(1)}, bf16[512,256]{1,0:T(8,128)(2,1)}, u32[]{:S(2)}) %copy-start.1) | copy-done | bytes 262168
  3.2 0.0 copy-start.3
  3.2 0.7 %copy-done.3 = s32[32,2]{0,1:T(2,128)S(1)} copy-done((s32[32,2]{0,1:T(2,128)S(1)}, s32[32,2]{0,1:T(2,128)}, u32[]{:S(2)}) %copy-start.3) | copy-done | bytes 280
  3.9 1.9 %shard_map.73 = bf16[8,272,256]{2,1,0:T(8,128)(2,1)S(1)} custom-call(bf16[4,512,512]{2,1,0:T(8,128)(2,1)S(1)} %copy-done, s32[2,32]{1,0:T(2,128)S(1)} %bitcast.43, s32[1]{0:T(128)S(6)} %copy.30.count_ref, bf16[512,256]{1,0:T(8,128)(2,1)S(1)} %copy-done.1), custom_call_target="tpu_custom_call" | custom-call | tf_op jit(solution)/shard_map/pallas_call | solution.py:101
  5.8 0.1 slice_bitcast_fusion.1
  5.9 0.5 collective-permute-start
  6.4 1.5 %collective-permute-done = bf16[2,2,272,256]{3,2,1,0:T(8,128)(2,1)S(1)} collective-permute-done((bf16[2,2,272,256]{3,2,1,0:T(8,128)(2,1)S(1)}, bf16[2,2,272,256]{3,2,1,0:T(8,128)(2,1)S(1)}, u32[]{:S(2)}, u32[]{:S(2)}) %collective-permute-start) | collective-permute-done | bytes 557088 | tf_op jit(solution)/shard_map/ppermute | solution.py:238
  8.0 2.9 %collective-permute-start.1 = (bf16[544,256]{1,0:T(8,128)(2,1)S(1)}, bf16[544,256]{1,0:T(8,128)(2,1)S(1)}, u32[]{:S(2)}, u32[]{:S(2)}) collective-permute-start(bf16[544,256]{1,0:T(8,128)(2,1)S(1)} %pad_maximum_fusion), channel_id=1, source_target_pairs={{0,4},{1,5},{2,6},{3,7},{4,0},{5,1},{6,2},{7,3},{8,12},{9,13},{10,... | collective-permute-start | bytes 835592 | tf_op jit(solution)/shard_map/ppermute | solution.py:238
  11.0 1.6 %collective-permute-start.2 = (bf16[512,256]{1,0:T(8,128)(2,1)S(1)}, bf16[512,256]{1,0:T(8,128)(2,1)S(1)}, u32[]{:S(2)}, u32[]{:S(2)}) collective-permute-start(bf16[512,256]{1,0:T(8,128)(2,1)S(1)} %pad_maximum_fusion.2), channel_id=1, source_target_pairs={{0,8},{2,10},{4,12},{6,14},{8,0},{10,2},{12,4},{14,6},{16,24},{18,... | collective-permute-start | bytes 786440 | tf_op jit(solution)/shard_map/ppermute | solution.py:242
  12.6 0.7 %collective-permute-start.4 = (bf16[512,256]{1,0:T(8,128)(2,1)S(1)}, bf16[512,256]{1,0:T(8,128)(2,1)S(1)}, u32[]{:S(2)}, u32[]{:S(2)}) collective-permute-start(bf16[512,256]{1,0:T(8,128)(2,1)S(1)} %pad_maximum_fusion.2), channel_id=1, source_target_pairs={{8,16},{10,18},{12,20},{14,22},{16,8},{18,10},{20,12},{22,14},{9,1... | collective-permute-start | bytes 786440 | tf_op jit(solution)/shard_map/ppermute | solution.py:242
  13.3 1.6 %collective-permute-start.6 = (bf16[512,256]{1,0:T(8,128)(2,1)S(1)}, bf16[512,256]{1,0:T(8,128)(2,1)S(1)}, u32[]{:S(2)}, u32[]{:S(2)}) collective-permute-start(bf16[512,256]{1,0:T(8,128)(2,1)S(1)} %pad_maximum_fusion.3), channel_id=1, source_target_pairs={{0,1},{1,0},{2,3},{3,2},{4,5},{5,4},{6,7},{7,6},{8,9},{9,8},{10,11... | collective-permute-start | bytes 786440 | tf_op jit(solution)/shard_map/ppermute | solution.py:238
  14.9 3.0 %collective-permute-done.1.refs_3_ = bf16[544,256]{1,0:T(8,128)(2,1)S(1)} collective-permute-done((bf16[544,256]{1,0:T(8,128)(2,1)S(1)}, bf16[544,256]{1,0:T(8,128)(2,1)S(1)}, u32[]{:S(2)}, u32[]{:S(2)}) %collective-permute-start.1) | collective-permute-done | bytes 278560 | tf_op jit(solution)/shard_map/ppermute | solution.py:238
  17.9 1.9 %collective-permute-start.3 = (bf16[512,256]{1,0:T(8,128)(2,1)S(1)}, bf16[512,256]{1,0:T(8,128)(2,1)S(1)}, u32[]{:S(2)}, u32[]{:S(2)}) collective-permute-start(bf16[512,256]{1,0:T(8,128)(2,1)S(1)} %slice.111), channel_id=1, source_target_pairs={{0,8},{2,10},{4,12},{6,14},{8,0},{10,2},{12,4},{14,6},{16,24},{18,... | collective-permute-start | bytes 786440 | tf_op jit(solution)/shard_map/ppermute | solution.py:242
  19.8 0.7 %collective-permute-start.5 = (bf16[512,256]{1,0:T(8,128)(2,1)S(1)}, bf16[512,256]{1,0:T(8,128)(2,1)S(1)}, u32[]{:S(2)}, u32[]{:S(2)}) collective-permute-start(bf16[512,256]{1,0:T(8,128)(2,1)S(1)} %slice.111), channel_id=1, source_target_pairs={{8,16},{10,18},{12,20},{14,22},{16,8},{18,10},{20,12},{22,14},{9,1... | collective-permute-start | bytes 786440 | tf_op jit(solution)/shard_map/ppermute | solution.py:242
  20.5 0.0 collective-permute-done.2.refs_0_
  20.5 2.5 %collective-permute-start.8 = (bf16[512,256]{1,0:T(8,128)(2,1)S(1)}, bf16[512,256]{1,0:T(8,128)(2,1)S(1)}, u32[]{:S(2)}, u32[]{:S(2)}) collective-permute-start(bf16[512,256]{1,0:T(8,128)(2,1)S(1)} %pad_maximum_fusion.4), channel_id=1, source_target_pairs={{0,5},{1,4},{2,7},{3,6},{4,1},{5,0},{6,3},{7,2},{8,13},{9,12},{10,... | collective-permute-start | bytes 786440 | tf_op jit(solution)/shard_map/ppermute | solution.py:238
  23.0 0.0 copy-start.2
  23.1 0.0 collective-permute-done.4.refs_4_
  23.1 0.0 collective-permute-done.6.refs_2_
  23.1 0.7 %collective-permute-start.10 = (bf16[512,256]{1,0:T(8,128)(2,1)S(1)}, bf16[512,256]{1,0:T(8,128)(2,1)S(1)}, u32[]{:S(2)}, u32[]{:S(2)}) collective-permute-start(bf16[512,256]{1,0:T(8,128)(2,1)S(1)} %collective-permute-done.6.refs_2_), channel_id=1, source_target_pairs={{8,16},{10,18},{12,20},{14,22},{16,8},{18,10},{20,12},{22,14},{9,1... | collective-permute-start | bytes 786440 | tf_op jit(solution)/shard_map/ppermute | solution.py:242
  23.8 5.7 %collective-permute-start.7 = (bf16[512,256]{1,0:T(8,128)(2,1)S(1)}, bf16[512,256]{1,0:T(8,128)(2,1)S(1)}, u32[]{:S(2)}, u32[]{:S(2)}) collective-permute-start(bf16[512,256]{1,0:T(8,128)(2,1)S(1)} %collective-permute-done.6.refs_2_), channel_id=1, source_target_pairs={{0,8},{2,10},{4,12},{6,14},{8,0},{10,2},{12,4},{14,6},{16,24},{18,... | collective-permute-start | bytes 786440 | tf_op jit(solution)/shard_map/ppermute | solution.py:242
  29.5 0.0 collective-permute-done.3.refs_1_
  29.5 0.0 collective-permute-done.5.refs_5_
  29.5 0.0 collective-permute-done.8.refs_3_
  29.5 0.7 %collective-permute-start.11 = (bf16[512,256]{1,0:T(8,128)(2,1)S(1)}, bf16[512,256]{1,0:T(8,128)(2,1)S(1)}, u32[]{:S(2)}, u32[]{:S(2)}) collective-permute-start(bf16[512,256]{1,0:T(8,128)(2,1)S(1)} %collective-permute-done.8.refs_3_), channel_id=1, source_target_pairs={{8,16},{10,18},{12,20},{14,22},{16,8},{18,10},{20,12},{22,14},{9,1... | collective-permute-start | bytes 786440 | tf_op jit(solution)/shard_map/ppermute | solution.py:242
  30.2 5.1 %collective-permute-start.9 = (bf16[512,256]{1,0:T(8,128)(2,1)S(1)}, bf16[512,256]{1,0:T(8,128)(2,1)S(1)}, u32[]{:S(2)}, u32[]{:S(2)}) collective-permute-start(bf16[512,256]{1,0:T(8,128)(2,1)S(1)} %collective-permute-done.8.refs_3_), channel_id=1, source_target_pairs={{0,8},{2,10},{4,12},{6,14},{8,0},{10,2},{12,4},{14,6},{16,24},{18,... | collective-permute-start | bytes 786440 | tf_op jit(solution)/shard_map/ppermute | solution.py:242
  35.4 0.1 reshape_squeeze.8.firsts
  35.5 0.1 reshape_squeeze.9.seconds
  35.6 0.1 convert_reduce_fusion.counts
  35.7 2.1 %shard_map.74.before = f32[2048,256]{1,0:T(8,128)S(1)} custom-call(s32[128]{0:T(128)S(1)} %reshape_squeeze.8.firsts, s32[128]{0:T(128)S(1)} %reshape_squeeze.9.seconds, s32[4]{0:T(128)S(1)} %convert_reduce_fusion.counts, bf16[512,256]{1,0:T(8,128)(2,1)S(1)} %collective-permute-done.2.refs_0_, bf16[512,256]{1,0:T(8,128)(2,1)S(1)} %collective-permute-done.3.refs_1_, ...), custom_call_target="tpu_custom_call" | custom-call | tf_op jit(solution)/shard_map/pallas_call | solution.py:288
  37.8 0.0 copy-start.4
  37.8 0.0 copy-start.5
  37.8 0.0 collective-permute-done.10.refs_4_
  37.9 0.0 collective-permute-done.7.refs_0_
  37.9 0.0 collective-permute-done.11.refs_5_
  37.9 2.2 %collective-permute-done.9.refs_1_ = bf16[512,256]{1,0:T(8,128)(2,1)S(1)} collective-permute-done((bf16[512,256]{1,0:T(8,128)(2,1)S(1)}, bf16[512,256]{1,0:T(8,128)(2,1)S(1)}, u32[]{:S(2)}, u32[]{:S(2)}) %collective-permute-start.9) | collective-permute-done | bytes 262176 | tf_op jit(solution)/shard_map/ppermute | solution.py:242
  40.0 0.0 copy-done.2
  40.0 2.9 %shard_map.75 = bf16[4,512,128]{2,1,0:T(8,128)(2,1)S(1)} custom-call(s32[128]{0:T(128)S(1)} %reshape_squeeze.8.firsts, s32[128]{0:T(128)S(1)} %reshape_squeeze.9.seconds, s32[4]{0:T(128)S(1)} %convert_reduce_fusion.counts, f32[2048,256]{1,0:T(8,128)S(1)} %shard_map.74.before, bf16[256,256]{1,0:T(8,128)(2,1)S(1)} %copy-done.2, ...), custom_call_target="tpu_custom_call" | custom-call | tf_op jit(solution)/shard_map/pallas_call | solution.py:301
  42.9 12.8 %all_to_all.5.code = bf16[8,256,128]{2,1,0:T(8,128)(2,1)S(1)} all-to-all(bf16[8,256,128]{2,1,0:T(8,128)(2,1)S(1)} %bitcast.42), channel_id=1, replica_groups={{0,1,2,3,4,5,6,7},{8,9,10,11,12,13,14,15},{16,17,18,19,20,21,22,23},{24..., dimensions={0} | all-to-all | bytes 1048576 | tf_op jit(solution)/shard_map/all_to_all | solution.py:320
  55.7 0.0 copy-done.4
  55.7 0.0 copy-done.5
  55.7 1.6 %shard_map.76 = f32[16,128,128]{2,1,0:T(8,128)} custom-call(bf16[8,256,128]{2,1,0:T(8,128)(2,1)S(1)} %all_to_all.5.code, s32[32]{0:T(128)S(1)} %copy-done.4, s32[32]{0:T(128)S(1)} %copy-done.5, s32[1]{0:T(128)S(6)} %copy.30.count_ref), custom_call_target="tpu_custom_call" | custom-call | tf_op jit(solution)/shard_map/pallas_call | solution.py:321
  (19 shorter events, 0.3 us)
Async XLA Ops:
  0.7 1.6 %copy-start = (bf16[4,512,512]{2,1,0:T(8,128)(2,1)S(1)}, bf16[4,512,512]{2,1,0:T(8,128)(2,1)}, u32[]{:S(2)}) copy-start(bf16[4,512,512]{2,1,0:T(8,128)(2,1)} %records.1) | copy-start | bytes 6291460
  2.2 0.9 %copy-start.1 = (bf16[512,256]{1,0:T(8,128)(2,1)S(1)}, bf16[512,256]{1,0:T(8,128)(2,1)}, u32[]{:S(2)}) copy-start(bf16[512,256]{1,0:T(8,128)(2,1)} %constant.89.table) | copy-start | bytes 786436
  3.2 0.7 %copy-start.3 = (s32[32,2]{0,1:T(2,128)S(1)}, s32[32,2]{0,1:T(2,128)}, u32[]{:S(2)}) copy-start(s32[32,2]{0,1:T(2,128)} %param.8) | copy-start | bytes 772
  5.9 2.1 %collective-permute-start = (bf16[2,2,272,256]{3,2,1,0:T(8,128)(2,1)S(1)}, bf16[2,2,272,256]{3,2,1,0:T(8,128)(2,1)S(1)}, u32[]{:S(2)}, u32[]{:S(2)}) collective-permute-start(bf16[2,2,272,256]{3,2,1,0:T(8,128)(2,1)S(1)} %get-tuple-element.12), channel_id=1, source_target_pairs={{0,2},{1,3},{2,0},{3,1},{4,6},{5,7},{6,4},{7,5},{8,10},{9,11},{10,... | collective-permute-start | bytes 1671176 | tf_op jit(solution)/shard_map/ppermute | solution.py:238
  8.0 9.9 %collective-permute-start.1 = (bf16[544,256]{1,0:T(8,128)(2,1)S(1)}, bf16[544,256]{1,0:T(8,128)(2,1)S(1)}, u32[]{:S(2)}, u32[]{:S(2)}) collective-permute-start(bf16[544,256]{1,0:T(8,128)(2,1)S(1)} %pad_maximum_fusion), channel_id=1, source_target_pairs={{0,4},{1,5},{2,6},{3,7},{4,0},{5,1},{6,2},{7,3},{8,12},{9,13},{10,... | collective-permute-start | bytes 835592 | tf_op jit(solution)/shard_map/ppermute | solution.py:238
  11.0 9.5 %collective-permute-start.2 = (bf16[512,256]{1,0:T(8,128)(2,1)S(1)}, bf16[512,256]{1,0:T(8,128)(2,1)S(1)}, u32[]{:S(2)}, u32[]{:S(2)}) collective-permute-start(bf16[512,256]{1,0:T(8,128)(2,1)S(1)} %pad_maximum_fusion.2), channel_id=1, source_target_pairs={{0,8},{2,10},{4,12},{6,14},{8,0},{10,2},{12,4},{14,6},{16,24},{18,... | collective-permute-start | bytes 786440 | tf_op jit(solution)/shard_map/ppermute | solution.py:242
  12.6 10.5 %collective-permute-start.4 = (bf16[512,256]{1,0:T(8,128)(2,1)S(1)}, bf16[512,256]{1,0:T(8,128)(2,1)S(1)}, u32[]{:S(2)}, u32[]{:S(2)}) collective-permute-start(bf16[512,256]{1,0:T(8,128)(2,1)S(1)} %pad_maximum_fusion.2), channel_id=1, source_target_pairs={{8,16},{10,18},{12,20},{14,22},{16,8},{18,10},{20,12},{22,14},{9,1... | collective-permute-start | bytes 786440 | tf_op jit(solution)/shard_map/ppermute | solution.py:242
  13.3 9.8 %collective-permute-start.6 = (bf16[512,256]{1,0:T(8,128)(2,1)S(1)}, bf16[512,256]{1,0:T(8,128)(2,1)S(1)}, u32[]{:S(2)}, u32[]{:S(2)}) collective-permute-start(bf16[512,256]{1,0:T(8,128)(2,1)S(1)} %pad_maximum_fusion.3), channel_id=1, source_target_pairs={{0,1},{1,0},{2,3},{3,2},{4,5},{5,4},{6,7},{7,6},{8,9},{9,8},{10,11... | collective-permute-start | bytes 786440 | tf_op jit(solution)/shard_map/ppermute | solution.py:238
  17.9 11.6 %collective-permute-start.3 = (bf16[512,256]{1,0:T(8,128)(2,1)S(1)}, bf16[512,256]{1,0:T(8,128)(2,1)S(1)}, u32[]{:S(2)}, u32[]{:S(2)}) collective-permute-start(bf16[512,256]{1,0:T(8,128)(2,1)S(1)} %slice.111), channel_id=1, source_target_pairs={{0,8},{2,10},{4,12},{6,14},{8,0},{10,2},{12,4},{14,6},{16,24},{18,... | collective-permute-start | bytes 786440 | tf_op jit(solution)/shard_map/ppermute | solution.py:242
  19.8 9.7 %collective-permute-start.5 = (bf16[512,256]{1,0:T(8,128)(2,1)S(1)}, bf16[512,256]{1,0:T(8,128)(2,1)S(1)}, u32[]{:S(2)}, u32[]{:S(2)}) collective-permute-start(bf16[512,256]{1,0:T(8,128)(2,1)S(1)} %slice.111), channel_id=1, source_target_pairs={{8,16},{10,18},{12,20},{14,22},{16,8},{18,10},{20,12},{22,14},{9,1... | collective-permute-start | bytes 786440 | tf_op jit(solution)/shard_map/ppermute | solution.py:242
  20.5 9.0 %collective-permute-start.8 = (bf16[512,256]{1,0:T(8,128)(2,1)S(1)}, bf16[512,256]{1,0:T(8,128)(2,1)S(1)}, u32[]{:S(2)}, u32[]{:S(2)}) collective-permute-start(bf16[512,256]{1,0:T(8,128)(2,1)S(1)} %pad_maximum_fusion.4), channel_id=1, source_target_pairs={{0,5},{1,4},{2,7},{3,6},{4,1},{5,0},{6,3},{7,2},{8,13},{9,12},{10,... | collective-permute-start | bytes 786440 | tf_op jit(solution)/shard_map/ppermute | solution.py:238
  23.0 17.0 %copy-start.2 = (bf16[256,256]{1,0:T(8,128)(2,1)S(1)}, bf16[256,256]{1,0:T(8,128)(2,1)}, u32[]{:S(2)}) copy-start(bf16[256,256]{1,0:T(8,128)(2,1)} %constant.87.clone.table_ref) | copy-start | bytes 393220
  23.1 14.7 %collective-permute-start.10 = (bf16[512,256]{1,0:T(8,128)(2,1)S(1)}, bf16[512,256]{1,0:T(8,128)(2,1)S(1)}, u32[]{:S(2)}, u32[]{:S(2)}) collective-permute-start(bf16[512,256]{1,0:T(8,128)(2,1)S(1)} %collective-permute-done.6.refs_2_), channel_id=1, source_target_pairs={{8,16},{10,18},{12,20},{14,22},{16,8},{18,10},{20,12},{22,14},{9,1... | collective-permute-start | bytes 786440 | tf_op jit(solution)/shard_map/ppermute | solution.py:242
  23.8 14.1 %collective-permute-start.7 = (bf16[512,256]{1,0:T(8,128)(2,1)S(1)}, bf16[512,256]{1,0:T(8,128)(2,1)S(1)}, u32[]{:S(2)}, u32[]{:S(2)}) collective-permute-start(bf16[512,256]{1,0:T(8,128)(2,1)S(1)} %collective-permute-done.6.refs_2_), channel_id=1, source_target_pairs={{0,8},{2,10},{4,12},{6,14},{8,0},{10,2},{12,4},{14,6},{16,24},{18,... | collective-permute-start | bytes 786440 | tf_op jit(solution)/shard_map/ppermute | solution.py:242
  29.5 8.3 %collective-permute-start.11 = (bf16[512,256]{1,0:T(8,128)(2,1)S(1)}, bf16[512,256]{1,0:T(8,128)(2,1)S(1)}, u32[]{:S(2)}, u32[]{:S(2)}) collective-permute-start(bf16[512,256]{1,0:T(8,128)(2,1)S(1)} %collective-permute-done.8.refs_3_), channel_id=1, source_target_pairs={{8,16},{10,18},{12,20},{14,22},{16,8},{18,10},{20,12},{22,14},{9,1... | collective-permute-start | bytes 786440 | tf_op jit(solution)/shard_map/ppermute | solution.py:242
  30.2 9.8 %collective-permute-start.9 = (bf16[512,256]{1,0:T(8,128)(2,1)S(1)}, bf16[512,256]{1,0:T(8,128)(2,1)S(1)}, u32[]{:S(2)}, u32[]{:S(2)}) collective-permute-start(bf16[512,256]{1,0:T(8,128)(2,1)S(1)} %collective-permute-done.8.refs_3_), channel_id=1, source_target_pairs={{0,8},{2,10},{4,12},{6,14},{8,0},{10,2},{12,4},{14,6},{16,24},{18,... | collective-permute-start | bytes 786440 | tf_op jit(solution)/shard_map/ppermute | solution.py:242
  37.8 17.9 %copy-start.4 = (s32[32]{0:T(128)S(1)}, s32[32]{0:T(128)}, u32[]{:S(2)}) copy-start(s32[32]{0:T(128)} %low_ref.1) | copy-start | bytes 388
  37.8 17.9 %copy-start.5 = (s32[32]{0:T(128)S(1)}, s32[32]{0:T(128)}, u32[]{:S(2)}) copy-start(s32[32]{0:T(128)} %high_ref.1) | copy-start | bytes 388

commit v4 on v3

v4 whole, which is shorter than its diff:
```python
import functools
import math

import jax
import jax.numpy as jnp
import numpy as np
from jax import lax
from jax.experimental import pallas as pl
from jax.experimental.pallas import tpu as pltpu
from jax.sharding import PartitionSpec as P

BLOCK = 128
F = 128
LAGS = 128
REACH = 16
NOTE_ROWS = 16
VMEM_LIMIT = 48 * 1024 * 1024
SPECTRA_VMEM = 52 * 1024 * 1024


def fill_forward_table(table_ref):
    length = table_ref.shape[0]
    first = length // 32
    step = 64
    for start in range(0, length, step):
        times = start + lax.broadcasted_iota(jnp.int32, (step, F), 0)
        freqs = first + lax.broadcasted_iota(jnp.int32, (step, F), 1)
        turns = lax.rem(times * freqs, length).astype(jnp.float32) * (1.0 / length)
        half = jnp.minimum(turns, 1.0 - turns)
        angle = 2.0 * math.pi * jnp.minimum(half, 0.5 - half)
        square = angle * angle
        sine, cosine = 1.0, 1.0
        for k in range(6, 0, -1):
            sine = 1.0 - square * sine * (1.0 / (2 * k * (2 * k + 1)))
        for k in range(7, 0, -1):
            cosine = 1.0 - square * cosine * (1.0 / (2 * k * (2 * k - 1)))
        sine = sine * angle
        sine = jnp.where(turns < 0.5, -sine, sine)
        cosine = jnp.where(half <= 0.25, cosine, -cosine)
        table_ref[pl.ds(start, step), pl.ds(0, F)] = cosine.astype(jnp.bfloat16)
        table_ref[pl.ds(start, step), pl.ds(F, F)] = sine.astype(jnp.bfloat16)


def inverse_tables(length, factor):
    first = length // 32
    freqs = (first + np.arange(F, dtype=np.int64))[:, None]
    shifts = (np.arange(LAGS, dtype=np.int64) - LAGS // 2)[None, :]
    phase = 2.0 * math.pi / length * (freqs * shifts % length)
    table = (np.concatenate([np.cos(phase), -np.sin(phase)], axis=0) * factor).astype(np.float32)
    high = table.astype(jnp.bfloat16)
    low = (table - high.astype(np.float32)).astype(jnp.bfloat16)
    return jnp.asarray(np.concatenate([high, low], axis=1))


def encode(values):
    values = values * jnp.abs(values)
    return (values * jnp.abs(values)).astype(jnp.bfloat16)


def spectra_kernel(near, wins, records, out_ref, held, table, sem):
    segments, channels, _ = records.shape
    cut, blocks = out_ref.shape[0], channels // BLOCK
    width = BLOCK // cut
    mine = lax.rem(lax.axis_index("chan"), near) * wins + lax.axis_index("win")
    copies = [
        pltpu.make_async_copy(records.at[s], held.at[s], sem.at[s]) for s in range(segments)
    ]
    for copy in copies:
        copy.start()
    fill_forward_table(table)

    def whitened(s, block):
        rows = held[s, pl.ds(block * BLOCK, BLOCK), :]
        spectra = jnp.dot(rows, table[...], preferred_element_type=jnp.float32)
        real_part, imag_part = spectra[:, :F], spectra[:, F:]
        power = real_part * real_part + imag_part * imag_part
        level = jnp.mean(power, axis=-1, keepdims=True)
        scale = lax.rsqrt(power + 0.1 * level + 1e-06)
        return jnp.concatenate([real_part * scale, imag_part * scale], axis=1)

    together = max(1, 16 // width)
    for s in range(0, segments, together):
        for k in range(together):
            copies[s + k].wait()
        for block in range(blocks):
            values = [whitened(s + k, block) for k in range(together)]
            for part in range(cut):
                tile = [v[part * width : (part + 1) * width] for v in values]
                tile = jnp.concatenate(tile, axis=0) if together > 1 else tile[0]
                spot = pl.ds((block * segments + s) * width, together * width)
                number = jnp.bitwise_xor(mine, part) if cut > 1 else 0
                out_ref[number, spot, :] = tile.astype(jnp.bfloat16)


def whitened_parts(records, near, wins):
    segments, channels, length = records.shape
    blocks, parts = channels // BLOCK, near * wins
    width = BLOCK // parts
    packed = width % 8 == 0
    cut = parts if packed else 1
    rows = blocks * segments * BLOCK // cut
    hbm = pl.BlockSpec(memory_space=pl.ANY)
    out = pl.pallas_call(
        functools.partial(spectra_kernel, near, wins),
        in_specs=[hbm],
        out_specs=pl.BlockSpec(memory_space=pltpu.VMEM),
        out_shape=jax.ShapeDtypeStruct((cut, rows, 2 * F), jnp.bfloat16),
        scratch_shapes=[
            pltpu.VMEM(records.shape, jnp.bfloat16),
            pltpu.VMEM((length, 2 * F), jnp.bfloat16),
            pltpu.SemaphoreType.DMA((segments,)),
        ],
        compiler_params=pltpu.CompilerParams(vmem_limit_bytes=SPECTRA_VMEM),
    )(records)
    if packed:
        return out
    mine = lax.axis_index("chan") % near * wins + lax.axis_index("win")
    split = out.reshape(blocks, segments, parts, width, 2 * F)
    split = split.transpose(2, 0, 1, 3, 4).reshape(parts, rows // parts, 2 * F)
    return jnp.take(split, jnp.bitwise_xor(mine, jnp.arange(parts)), axis=0)


def gather(moves, held, sem):
    copies, spot = [], 0
    for k, (ref, first, count) in enumerate(moves):
        copies.append(
            pltpu.make_async_copy(
                ref.at[pl.ds(first, count)], held.at[pl.ds(spot, count)], sem.at[k]
            )
        )
        spot += count
        copies[-1].start()
    for copy in copies:
        copy.wait()


def add_pairs(near, fold, slots_ref, held, tiles, before, cross):
    slots = (slots_ref.shape[0] - near - 1) // (2 * near + 2)
    together = min(4, slots)

    def one_pair(index):
        first, second = slots_ref[index], slots_ref[near * slots + index]
        spot = pl.ds(pl.multiple_of(index * fold, fold), fold)
        real_sum, imag_sum = None, None
        for tile in tiles:
            a = held[pl.ds(pl.multiple_of(first + tile, 16), 16), :].astype(jnp.float32)
            b = held[pl.ds(pl.multiple_of(second + tile, 16), 16), :].astype(jnp.float32)
            ar, ai, br, bi = a[:, :F], a[:, F:], b[:, :F], b[:, F:]
            real_part, imag_part = ar * br + ai * bi, ar * bi - ai * br
            real_sum = real_part if real_sum is None else real_sum + real_part
            imag_sum = imag_part if imag_sum is None else imag_sum + imag_part
        if fold == 8:
            real_sum = real_sum[:8] + real_sum[8:]
            imag_sum = imag_sum[:8] + imag_sum[8:]
        if before is not None:
            real_sum += before[spot, pl.ds(0, F)]
            imag_sum += before[spot, pl.ds(F, F)]
        cross[spot, pl.ds(0, F)] = real_sum
        cross[spot, pl.ds(F, F)] = imag_sum

    def owner_of(owner, _):
        def some_pairs(step, _):
            for k in range(together):
                one_pair(owner * slots + step * together + k)
            return 0

        count = jnp.clip(slots_ref[2 * near * slots + owner], 0, slots)
        lax.fori_loop(0, lax.div(count + (together - 1), together), some_pairs, 0)
        return 0

    lax.fori_loop(0, near, owner_of, 0)


def first_kernel(near, fold, size, rows, slots_ref, *refs):
    pieces, (cross, held, sem) = refs[:6], refs[6:]
    part = (near - 2) * size
    moves = []
    for plane in range(3):
        moves += [(pieces[plane], 0, 2 * size), (pieces[3 + plane], 0, part)]
    gather(moves, held, sem)
    add_pairs(near, fold, slots_ref, held, list(range(0, rows, 16)), None, cross)


def last_kernel(near, fold, windows, size, rows, slots_ref, before, table, *refs):
    pieces, (out_ref, held, cross, table_ref, sem) = refs[:6], refs[6:]
    table_copy = pltpu.make_async_copy(table, table_ref, sem.at[6])
    table_copy.start()
    part = (near - 2) * size
    moves = []
    for plane in range(3):
        piece, last = pieces[plane], pieces[3 + plane]
        moves += [(piece, part, piece.shape[0] - part), (last, 0, 2 * size)]
    gather(moves, held, sem)
    tiles = [w * near * size + r for w in range(windows) for r in range(0, rows, 16)]
    add_pairs(near, fold, slots_ref, held, tiles, before, cross)
    table_copy.wait()
    mine = lax.rem(lax.axis_index("chan"), near)
    span = cross.shape[0] // near
    for owner in range(near):
        spectrum = cross[pl.ds(owner * span, span), :]
        high = spectrum.astype(jnp.bfloat16)
        low = (spectrum - high.astype(jnp.float32)).astype(jnp.bfloat16)
        left = jnp.dot(high, table_ref[...], preferred_element_type=jnp.float32)
        right = jnp.dot(low, table_ref[:, :LAGS], preferred_element_type=jnp.float32)
        lagged = left[:, :LAGS] + (left[:, LAGS:] + right)
        lagged = lagged if out_ref.dtype == jnp.float32 else encode(lagged)
        out_ref[jnp.bitwise_xor(owner, mine)] = lagged


def stack_kernel(near, width, scale, slots_ref, *refs):
    codes, (out, held, sem) = refs[:-3], refs[-3:]
    share, parts = held.shape[0], codes[0].shape[0]
    slots = (slots_ref.shape[0] - near - 1) // (2 * near + 2)
    limits = 2 * near * slots + near
    start = lax.axis_index("win") * share
    lag_index = lax.broadcasted_iota(jnp.int32, (parts, width, LAGS), 2)
    together = min(4, share)
    copies = []
    for slot in range(share):
        tile = slot * width // 16 * 16
        at = limits + start + slot
        high = jnp.where(start + slot < slots_ref[limits + 2 * slots], slots_ref[at + slots], 0)
        keep = (lag_index >= slots_ref[at]) & (lag_index < high)
        kept = []
        for code in codes:
            values = code[:, pl.ds(tile, 16), :].astype(jnp.float32)
            values = values[:, slot * width - tile : slot * width - tile + width, :]
            root = lax.rsqrt(lax.rsqrt(jnp.abs(values))) * scale
            root = jnp.where(values < 0, -root, root)
            kept.append(jnp.where(keep, root, 0.0))
        kept = jnp.concatenate(kept, axis=1) if len(kept) > 1 else kept[0]
        held[slot] = kept.reshape(BLOCK, LAGS)
        if slot % together == together - 1:
            spot = pl.ds(slot + 1 - together, together)
            copies.append(pltpu.make_async_copy(held.at[spot], out.at[spot], sem.at[len(copies)]))
            copies[-1].start()
    for copy in copies:
        copy.wait()


def per_device(records, block_pairs, lag_low, lag_high, slot_count):
    segments, channels, length = records.shape
    blocks = channels // BLOCK
    chans, wins = lax.axis_size("chan"), lax.axis_size("win")
    both = ("chan", "win")
    near = REACH // blocks
    parts, halves = near * wins, near // 2
    width = BLOCK // parts
    rows = segments * width
    size = blocks * rows
    slots = block_pairs.shape[0]
    share = slots // wins
    group_total = chans // near
    group, member = lax.axis_index("chan") // near, lax.axis_index("chan") % near

    def partner(block, distance):
        return lax.ppermute(block, both, [(i, i ^ distance) for i in range(chans * wins)])

    def along(block, to):
        route = [(q * near + j, to(q) * near + j) for q in range(group_total) for j in range(near)]
        return lax.ppermute(block, "chan", [r for r in route if 0 <= r[1] < chans])

    def even(block):
        return along(block, lambda q: q ^ 1)

    def odd(block):
        return along(block, lambda q: ((q + 1) ^ 1) - 1)

    def after(block, *others):
        return lax.optimization_barrier((block,) + others)[0]

    near_blocks = jnp.clip(block_pairs.T - (group - 1) * REACH, 0, 3 * REACH - 1)
    note = jnp.pad(near_blocks, ((0, NOTE_ROWS - 2), (0, 2 * F - slots)))
    note = jnp.where(jnp.arange(NOTE_ROWS)[:, None] == 2, slot_count[0], note).astype(jnp.bfloat16)

    split = whitened_parts(records, near, wins)
    split = split.reshape(halves, 2, wins, size, 2 * F)
    sent = split[:, 1].reshape(halves * wins * size, 2 * F)
    other = partner(jnp.concatenate([sent, note], axis=0), wins)
    other_note = other[halves * wins * size :]
    other = other[: halves * wins * size].reshape(halves, wins, size, 2 * F)

    order = [(w, h) for w in range(wins) for h in range(halves)]
    own, notes = [], []
    for w, h in order:
        piece = [split[h, 0, w], other[h, w]] + ([note, other_note] if w == 0 else [])
        piece = jnp.concatenate(piece, axis=0)
        if (w, h) == order[-1]:
            piece = after(piece, own[2])
        if w or h:
            piece = partner(piece, h * 2 * wins + w)
        if w == 0:
            notes.append(piece[2 * size :].reshape(2, NOTE_ROWS, 2 * F)[:, :3, :slots])
        own.append(piece[: 2 * size])
    rounds = [own[0], jnp.concatenate(own[1:-1], axis=0), own[-1]]
    planes = []
    for k, sent in enumerate(rounds):
        sent = after(sent, planes[0][0], planes[0][2]) if k == 2 else sent
        planes.append([even(sent), sent, odd(sent)])

    notes = jnp.concatenate(notes, axis=0).astype(jnp.int32)
    level, rest = notes[:, :2] // REACH, notes[:, :2] % REACH
    level = jnp.where(group % 2 == 0, 2 - level, level)
    member_block = (jnp.bitwise_xor(rest // blocks, member), rest % blocks)
    counts = notes[:, 2, 0]

    def first_row(windows):
        row = (level * (windows * near) + member_block[0]) * size + member_block[1] * rows
        row = [row[:, 0].reshape(near * slots), row[:, 1].reshape(near * slots)]
        return jnp.concatenate(row + [counts, lag_low, lag_high, slot_count])

    fold = 16 if width % 16 == 0 else 8
    scale = 2.0 ** math.floor(31 - 0.5 * math.log2(F * segments * wins))
    table = inverse_tables(length, scale / math.sqrt(F * segments * wins))
    hbm = pl.BlockSpec(memory_space=pl.ANY)
    smem = pl.BlockSpec(memory_space=pltpu.SMEM)
    vmem = pl.BlockSpec(memory_space=pltpu.VMEM)
    params = pltpu.CompilerParams(vmem_limit_bytes=VMEM_LIMIT)
    cross = jax.ShapeDtypeStruct((near * slots * fold, 2 * F), jnp.float32)
    table_rows, last_rows = first_row(1), first_row(wins - 1)
    before = pl.pallas_call(
        functools.partial(first_kernel, near, fold, size, rows),
        in_specs=[smem] + [hbm] * 6,
        out_specs=vmem,
        out_shape=cross,
        scratch_shapes=[
            pltpu.VMEM((3 * near * size, 2 * F), jnp.bfloat16),
            pltpu.SemaphoreType.DMA((6,)),
        ],
        compiler_params=params,
    )(table_rows, *planes[0], *planes[1])

    groups = [[q * parts + k for k in range(parts)] for q in range(group_total)]
    lagged = pl.pallas_call(
        functools.partial(last_kernel, near, fold, wins - 1, size, rows),
        in_specs=[smem, vmem, hbm] + [hbm] * 6,
        out_specs=vmem,
        out_shape=jax.ShapeDtypeStruct(
            (near, slots * fold, LAGS), jnp.bfloat16 if fold == width else jnp.float32
        ),
        scratch_shapes=[
            pltpu.VMEM((3 * (wins - 1) * near * size, 2 * F), jnp.bfloat16),
            pltpu.VMEM(cross.shape, jnp.float32),
            pltpu.VMEM(table.shape, table.dtype),
            pltpu.SemaphoreType.DMA((7,)),
        ],
        compiler_params=params,
    )(last_rows, before, table, *planes[1], *planes[2])
    if fold > width:
        lagged = encode(lagged.reshape(near, slots, fold // width, width, LAGS).sum(axis=2))
    lagged = lagged.reshape(parts, share * width, LAGS)
    code = lax.all_to_all(lagged, both, 0, 0, axis_index_groups=groups, tiled=True)

    return pl.pallas_call(
        functools.partial(stack_kernel, near, width, 1.0 / scale),
        in_specs=[smem, vmem],
        out_specs=hbm,
        out_shape=jax.ShapeDtypeStruct((share, BLOCK, LAGS), jnp.float32),
        scratch_shapes=[
            pltpu.VMEM((share, BLOCK, LAGS), jnp.float32),
            pltpu.SemaphoreType.DMA((max(1, share // 4),)),
        ],
        compiler_params=params,
    )(table_rows, code)


def solution(mesh):
    in_specs = (P("win", "chan", None), P("chan", None), P("chan"), P("chan"), P("chan"))
    out_specs = P(("chan", "win"), None, None)
    return jax.shard_map(
        per_device, mesh=mesh, in_specs=in_specs, out_specs=out_specs, check_vma=False
    )
```

time: 57.8 us -> 55.2 us (0.955)
  the two profiles are of different devices: /device:TPU:0 before, /device:TPU:17 now
where the time goes in v4:
time: 55.2 us; the launch traced here: 54.6 us
  starting transfers between devices  15.2 us (28%)
  waiting for transfers between devices  14.8 us (27%)
  blocking collectives  13.8 us (25%)
  Pallas kernels  9.06 us (16%)
  between operations  0.89 us (2%)
    all_to_all x1, blocking collectives, per_device(): lax.all_to_all(lagged, both, 0, 0, axis_index_groups=groups, tiled=True)  13.8 us
    ppermute x6, waiting for transfers between devices, along(): return lax.ppermute(block, 'chan', [r for r in route if 0 <= r[1] < chans])  9.75 us
    ppermute x6, starting transfers between devices, along(): return lax.ppermute(block, 'chan', [r for r in route if 0 <= r[1] < chans])  9.74 us
    ppermute x4, starting transfers between devices, partner(): lax.ppermute(block, both, [(i, i ^ distance) for i in range(chans * wins)])  5.48 us
    ppermute x4, waiting for transfers between devices, partner(): lax.ppermute(block, both, [(i, i ^ distance) for i in range(chans * wins)])  5.04 us
    pallas_call x1, Pallas kernels, per_device(): pl.pallas_call(functools.partial(last_kernel, near, fold, wins - 1, size,...  2.81 us
    pallas_call x1, Pallas kernels, whitened_parts(): pl.pallas_call(functools.partial(spectra_kernel, near, wins), in_specs=[h...  2.74 us
    pallas_call x1, Pallas kernels, per_device(): pl.pallas_call(functools.partial(first_kernel, near, fold, size, rows), i...  1.86 us
  transfers between devices with their start and end apart: 10, of which 7 were waited for; matrix products, arithmetic and copies ran while one was open for 1% of the time, Pallas kernels for 3%

profile of v4, /device:TPU:17, one launch (start us, length us, event | category | flops | bytes accessed | tf_op | source)
XLA Modules:
  0.0 54.6 jit_solution(8058817630948726387)
XLA Ops:
  0.7 0.0 copy-start.1
  0.7 2.7 %shard_map.64 = bf16[8,256,256]{2,1,0:T(8,128)(2,1)S(1)} custom-call(bf16[4,512,512]{2,1,0:T(8,128)(2,1)} %records.1), custom_call_target="tpu_custom_call" | custom-call | tf_op jit(solution)/shard_map/pallas_call | solution.py:103
  3.5 0.0 copy-done.1
  3.5 0.1 select_convert_fusion
  3.6 0.7 %collective-permute-start = (bf16[1040,256]{1,0:T(8,128)(2,1)S(1)}, bf16[1040,256]{1,0:T(8,128)(2,1)S(1)}, u32[]{:S(2)}, u32[]{:S(2)}) collective-permute-start(bf16[1040,256]{1,0:T(8,128)(2,1)S(1)} %pad_maximum_fusion), channel_id=1, source_target_pairs={{0,2},{1,3},{2,0},{3,1},{4,6},{5,7},{6,4},{7,5},{8,10},{9,11},{10,... | collective-permute-start | bytes 1597448 | tf_op jit(solution)/shard_map/ppermute | solution.py:257
  4.4 1.5 %collective-permute-done = bf16[1040,256]{1,0:T(8,128)(2,1)S(1)} collective-permute-done((bf16[1040,256]{1,0:T(8,128)(2,1)S(1)}, bf16[1040,256]{1,0:T(8,128)(2,1)S(1)}, u32[]{:S(2)}, u32[]{:S(2)}) %collective-permute-start) | collective-permute-done | bytes 532512 | tf_op jit(solution)/shard_map/ppermute | solution.py:257
  6.0 1.3 %collective-permute-start.4 = (bf16[512,256]{1,0:T(8,128)(2,1)S(1)}, bf16[512,256]{1,0:T(8,128)(2,1)S(1)}, u32[]{:S(2)}, u32[]{:S(2)}) collective-permute-start(bf16[512,256]{1,0:T(8,128)(2,1)S(1)} %pad_maximum_fusion.4), channel_id=1, source_target_pairs={{0,1},{1,0},{2,3},{3,2},{4,5},{5,4},{6,7},{7,6},{8,9},{9,8},{10,11... | collective-permute-start | bytes 786440 | tf_op jit(solution)/shard_map/ppermute | solution.py:257
  7.3 1.3 %collective-permute-start.1 = (bf16[544,256]{1,0:T(8,128)(2,1)S(1)}, bf16[544,256]{1,0:T(8,128)(2,1)S(1)}, u32[]{:S(2)}, u32[]{:S(2)}) collective-permute-start(bf16[544,256]{1,0:T(8,128)(2,1)S(1)} %pad_maximum_fusion.2), channel_id=1, source_target_pairs={{0,4},{1,5},{2,6},{3,7},{4,0},{5,1},{6,2},{7,3},{8,12},{9,13},{10,... | collective-permute-start | bytes 835592 | tf_op jit(solution)/shard_map/ppermute | solution.py:257
  8.6 1.4 %collective-permute-start.2 = (bf16[512,256]{1,0:T(8,128)(2,1)S(1)}, bf16[512,256]{1,0:T(8,128)(2,1)S(1)}, u32[]{:S(2)}, u32[]{:S(2)}) collective-permute-start(bf16[512,256]{1,0:T(8,128)(2,1)S(1)} %pad_maximum_fusion.3.refs_1_), channel_id=1, source_target_pairs={{0,8},{2,10},{4,12},{6,14},{8,0},{10,2},{12,4},{14,6},{16,24},{18,... | collective-permute-start | bytes 786440 | tf_op jit(solution)/shard_map/ppermute | solution.py:261
  10.0 1.9 %collective-permute-start.3 = (bf16[512,256]{1,0:T(8,128)(2,1)S(1)}, bf16[512,256]{1,0:T(8,128)(2,1)S(1)}, u32[]{:S(2)}, u32[]{:S(2)}) collective-permute-start(bf16[512,256]{1,0:T(8,128)(2,1)S(1)} %pad_maximum_fusion.3.refs_1_), channel_id=1, source_target_pairs={{8,16},{10,18},{12,20},{14,22},{16,8},{18,10},{20,12},{22,14},{9,1... | collective-permute-start | bytes 786440 | tf_op jit(solution)/shard_map/ppermute | solution.py:261
  11.9 0.0 copy-start.2
  11.9 0.0 copy-start.3
  12.0 1.6 %collective-permute-done.4 = bf16[512,256]{1,0:T(8,128)(2,1)S(1)} collective-permute-done((bf16[512,256]{1,0:T(8,128)(2,1)S(1)}, bf16[512,256]{1,0:T(8,128)(2,1)S(1)}, u32[]{:S(2)}, u32[]{:S(2)}) %collective-permute-start.4) | collective-permute-done | bytes 262176 | tf_op jit(solution)/shard_map/ppermute | solution.py:257
  13.6 2.2 %collective-permute-start.7 = (bf16[512,256]{1,0:T(8,128)(2,1)S(1)}, bf16[512,256]{1,0:T(8,128)(2,1)S(1)}, u32[]{:S(2)}, u32[]{:S(2)}) collective-permute-start(bf16[512,256]{1,0:T(8,128)(2,1)S(1)} %pad_maximum_fusion.5), channel_id=1, source_target_pairs={{0,5},{1,4},{2,7},{3,6},{4,1},{5,0},{6,3},{7,2},{8,13},{9,12},{10,... | collective-permute-start | bytes 786440 | tf_op jit(solution)/shard_map/ppermute | solution.py:257
  15.8 0.0 collective-permute-done.1
  15.8 1.4 %collective-permute-start.5 = (bf16[1024,256]{1,0:T(8,128)(2,1)S(1)}, bf16[1024,256]{1,0:T(8,128)(2,1)S(1)}, u32[]{:S(2)}, u32[]{:S(2)}) collective-permute-start(bf16[1024,256]{1,0:T(8,128)(2,1)S(1)} %pad_maximum_fusion.1.refs_4_.refs_1_), channel_id=1, source_target_pairs={{0,8},{2,10},{4,12},{6,14},{8,0},{10,2},{12,4},{14,6},{16,24},{18,... | collective-permute-start | bytes 1572872 | tf_op jit(solution)/shard_map/ppermute | solution.py:261
  17.2 1.9 %collective-permute-start.6 = (bf16[1024,256]{1,0:T(8,128)(2,1)S(1)}, bf16[1024,256]{1,0:T(8,128)(2,1)S(1)}, u32[]{:S(2)}, u32[]{:S(2)}) collective-permute-start(bf16[1024,256]{1,0:T(8,128)(2,1)S(1)} %pad_maximum_fusion.1.refs_4_.refs_1_), channel_id=1, source_target_pairs={{8,16},{10,18},{12,20},{14,22},{16,8},{18,10},{20,12},{22,14},{9,1... | collective-permute-start | bytes 1572872 | tf_op jit(solution)/shard_map/ppermute | solution.py:261
  19.2 0.0 collective-permute-done.2.refs_0_
  19.2 0.0 collective-permute-done.3.refs_2_
  19.2 1.9 %collective-permute-done.7.refs_4_ = bf16[512,256]{1,0:T(8,128)(2,1)S(1)} collective-permute-done((bf16[512,256]{1,0:T(8,128)(2,1)S(1)}, bf16[512,256]{1,0:T(8,128)(2,1)S(1)}, u32[]{:S(2)}, u32[]{:S(2)}) %collective-permute-start.7) | collective-permute-done | bytes 262176 | tf_op jit(solution)/shard_map/ppermute | solution.py:257
  21.1 1.3 %collective-permute-start.8 = (bf16[512,256]{1,0:T(8,128)(2,1)S(1)}, bf16[512,256]{1,0:T(8,128)(2,1)S(1)}, u32[]{:S(2)}, u32[]{:S(2)}) collective-permute-start(bf16[512,256]{1,0:T(8,128)(2,1)S(1)} %collective-permute-done.7.refs_4_), channel_id=1, source_target_pairs={{0,8},{2,10},{4,12},{6,14},{8,0},{10,2},{12,4},{14,6},{16,24},{18,... | collective-permute-start | bytes 786440 | tf_op jit(solution)/shard_map/ppermute | solution.py:261
  22.4 1.9 %collective-permute-start.9 = (bf16[512,256]{1,0:T(8,128)(2,1)S(1)}, bf16[512,256]{1,0:T(8,128)(2,1)S(1)}, u32[]{:S(2)}, u32[]{:S(2)}) collective-permute-start(bf16[512,256]{1,0:T(8,128)(2,1)S(1)} %collective-permute-done.7.refs_4_), channel_id=1, source_target_pairs={{8,16},{10,18},{12,20},{14,22},{16,8},{18,10},{20,12},{22,14},{9,1... | collective-permute-start | bytes 786440 | tf_op jit(solution)/shard_map/ppermute | solution.py:261
  24.3 0.1 reshape_squeeze.12
  24.4 0.1 reshape_squeeze.13
  24.5 0.1 convert_reduce_fusion
  24.6 0.0 copy-done.2
  24.6 0.0 copy-done.3
  24.6 0.1 concatenate.33.slots_ref
  24.7 0.0 copy-start
  24.7 3.1 %collective-permute-done.5.refs_3_.refs_0_ = bf16[1024,256]{1,0:T(8,128)(2,1)S(1)} collective-permute-done((bf16[1024,256]{1,0:T(8,128)(2,1)S(1)}, bf16[1024,256]{1,0:T(8,128)(2,1)S(1)}, u32[]{:S(2)}, u32[]{:S(2)}) %collective-permute-start.5) | collective-permute-done | bytes 524320 | tf_op jit(solution)/shard_map/ppermute | solution.py:261
  27.8 2.9 %collective-permute-done.6.refs_5_.refs_2_ = bf16[1024,256]{1,0:T(8,128)(2,1)S(1)} collective-permute-done((bf16[1024,256]{1,0:T(8,128)(2,1)S(1)}, bf16[1024,256]{1,0:T(8,128)(2,1)S(1)}, u32[]{:S(2)}, u32[]{:S(2)}) %collective-permute-start.6) | collective-permute-done | bytes 524320 | tf_op jit(solution)/shard_map/ppermute | solution.py:261
  30.7 1.9 %shard_map.65.before = f32[2048,256]{1,0:T(8,128)S(1)} custom-call(s32[325]{0:T(512)S(1)} %concatenate.33.slots_ref, bf16[512,256]{1,0:T(8,128)(2,1)S(1)} %collective-permute-done.2.refs_0_, bf16[512,256]{1,0:T(8,128)(2,1)S(1)} %pad_maximum_fusion.3.refs_1_, bf16[512,256]{1,0:T(8,128)(2,1)S(1)} %collective-permute-done.3.refs_2_, ...), custom_call_target="tpu_custom_call" | custom-call | tf_op jit(solution)/shard_map/pallas_call | solution.py:321
  32.6 0.9 %collective-permute-done.8.refs_3_ = bf16[512,256]{1,0:T(8,128)(2,1)S(1)} collective-permute-done((bf16[512,256]{1,0:T(8,128)(2,1)S(1)}, bf16[512,256]{1,0:T(8,128)(2,1)S(1)}, u32[]{:S(2)}, u32[]{:S(2)}) %collective-permute-start.8) | collective-permute-done | bytes 262176 | tf_op jit(solution)/shard_map/ppermute | solution.py:261
  33.5 2.9 %collective-permute-done.9.refs_5_ = bf16[512,256]{1,0:T(8,128)(2,1)S(1)} collective-permute-done((bf16[512,256]{1,0:T(8,128)(2,1)S(1)}, bf16[512,256]{1,0:T(8,128)(2,1)S(1)}, u32[]{:S(2)}, u32[]{:S(2)}) %collective-permute-start.9) | collective-permute-done | bytes 262176 | tf_op jit(solution)/shard_map/ppermute | solution.py:261
  36.4 0.0 copy-done
  36.4 2.8 %shard_map.66 = bf16[4,512,128]{2,1,0:T(8,128)(2,1)S(1)} custom-call(s32[325]{0:T(512)S(1)} %concatenate.33.slots_ref, f32[2048,256]{1,0:T(8,128)S(1)} %shard_map.65.before, bf16[256,256]{1,0:T(8,128)(2,1)S(1)} %copy-done, bf16[1024,256]{1,0:T(8,128)(2,1)S(1)} %collective-permute-done.5.refs_3_.refs_0_, ...), custom_call_target="tpu_custom_call" | custom-call | tf_op jit(solution)/shard_map/pallas_call | solution.py:334
  39.2 13.8 %all_to_all.5.refs_0_ = bf16[8,256,128]{2,1,0:T(8,128)(2,1)S(1)} all-to-all(bf16[8,256,128]{2,1,0:T(8,128)(2,1)S(1)} %bitcast.32), channel_id=1, replica_groups={{0,1,2,3,4,5,6,7},{8,9,10,11,12,13,14,15},{16,17,18,19,20,21,22,23},{24..., dimensions={0} | all-to-all | bytes 1048576 | tf_op jit(solution)/shard_map/all_to_all | solution.py:352
  53.0 1.6 %shard_map.67 = f32[16,128,128]{2,1,0:T(8,128)} custom-call(s32[325]{0:T(512)S(1)} %concatenate.33.slots_ref, bf16[8,256,128]{2,1,0:T(8,128)(2,1)S(1)} %all_to_all.5.refs_0_), custom_call_target="tpu_custom_call" | custom-call | tf_op jit(solution)/shard_map/pallas_call | solution.py:354
  (23 shorter events, 0.4 us)
Async XLA Ops:
  0.7 2.8 %copy-start.1 = (s32[32,2]{0,1:T(2,128)S(1)}, s32[32,2]{0,1:T(2,128)}, u32[]{:S(2)}) copy-start(s32[32,2]{0,1:T(2,128)} %param.7) | copy-start | bytes 772
  3.6 2.3 %collective-permute-start = (bf16[1040,256]{1,0:T(8,128)(2,1)S(1)}, bf16[1040,256]{1,0:T(8,128)(2,1)S(1)}, u32[]{:S(2)}, u32[]{:S(2)}) collective-permute-start(bf16[1040,256]{1,0:T(8,128)(2,1)S(1)} %pad_maximum_fusion), channel_id=1, source_target_pairs={{0,2},{1,3},{2,0},{3,1},{4,6},{5,7},{6,4},{7,5},{8,10},{9,11},{10,... | collective-permute-start | bytes 1597448 | tf_op jit(solution)/shard_map/ppermute | solution.py:257
  6.0 7.6 %collective-permute-start.4 = (bf16[512,256]{1,0:T(8,128)(2,1)S(1)}, bf16[512,256]{1,0:T(8,128)(2,1)S(1)}, u32[]{:S(2)}, u32[]{:S(2)}) collective-permute-start(bf16[512,256]{1,0:T(8,128)(2,1)S(1)} %pad_maximum_fusion.4), channel_id=1, source_target_pairs={{0,1},{1,0},{2,3},{3,2},{4,5},{5,4},{6,7},{7,6},{8,9},{9,8},{10,11... | collective-permute-start | bytes 786440 | tf_op jit(solution)/shard_map/ppermute | solution.py:257
  7.3 8.4 %collective-permute-start.1 = (bf16[544,256]{1,0:T(8,128)(2,1)S(1)}, bf16[544,256]{1,0:T(8,128)(2,1)S(1)}, u32[]{:S(2)}, u32[]{:S(2)}) collective-permute-start(bf16[544,256]{1,0:T(8,128)(2,1)S(1)} %pad_maximum_fusion.2), channel_id=1, source_target_pairs={{0,4},{1,5},{2,6},{3,7},{4,0},{5,1},{6,2},{7,3},{8,12},{9,13},{10,... | collective-permute-start | bytes 835592 | tf_op jit(solution)/shard_map/ppermute | solution.py:257
  8.6 10.5 %collective-permute-start.2 = (bf16[512,256]{1,0:T(8,128)(2,1)S(1)}, bf16[512,256]{1,0:T(8,128)(2,1)S(1)}, u32[]{:S(2)}, u32[]{:S(2)}) collective-permute-start(bf16[512,256]{1,0:T(8,128)(2,1)S(1)} %pad_maximum_fusion.3.refs_1_), channel_id=1, source_target_pairs={{0,8},{2,10},{4,12},{6,14},{8,0},{10,2},{12,4},{14,6},{16,24},{18,... | collective-permute-start | bytes 786440 | tf_op jit(solution)/shard_map/ppermute | solution.py:261
  10.0 9.2 %collective-permute-start.3 = (bf16[512,256]{1,0:T(8,128)(2,1)S(1)}, bf16[512,256]{1,0:T(8,128)(2,1)S(1)}, u32[]{:S(2)}, u32[]{:S(2)}) collective-permute-start(bf16[512,256]{1,0:T(8,128)(2,1)S(1)} %pad_maximum_fusion.3.refs_1_), channel_id=1, source_target_pairs={{8,16},{10,18},{12,20},{14,22},{16,8},{18,10},{20,12},{22,14},{9,1... | collective-permute-start | bytes 786440 | tf_op jit(solution)/shard_map/ppermute | solution.py:261
  11.9 12.7 %copy-start.2 = (s32[32]{0:T(128)S(1)}, s32[32]{0:T(128)}, u32[]{:S(2)}) copy-start(s32[32]{0:T(128)} %param.8) | copy-start | bytes 388
  11.9 12.7 %copy-start.3 = (s32[32]{0:T(128)S(1)}, s32[32]{0:T(128)}, u32[]{:S(2)}) copy-start(s32[32]{0:T(128)} %param.9) | copy-start | bytes 388
  13.6 7.5 %collective-permute-start.7 = (bf16[512,256]{1,0:T(8,128)(2,1)S(1)}, bf16[512,256]{1,0:T(8,128)(2,1)S(1)}, u32[]{:S(2)}, u32[]{:S(2)}) collective-permute-start(bf16[512,256]{1,0:T(8,128)(2,1)S(1)} %pad_maximum_fusion.5), channel_id=1, source_target_pairs={{0,5},{1,4},{2,7},{3,6},{4,1},{5,0},{6,3},{7,2},{8,13},{9,12},{10,... | collective-permute-start | bytes 786440 | tf_op jit(solution)/shard_map/ppermute | solution.py:257
  15.8 12.0 %collective-permute-start.5 = (bf16[1024,256]{1,0:T(8,128)(2,1)S(1)}, bf16[1024,256]{1,0:T(8,128)(2,1)S(1)}, u32[]{:S(2)}, u32[]{:S(2)}) collective-permute-start(bf16[1024,256]{1,0:T(8,128)(2,1)S(1)} %pad_maximum_fusion.1.refs_4_.refs_1_), channel_id=1, source_target_pairs={{0,8},{2,10},{4,12},{6,14},{8,0},{10,2},{12,4},{14,6},{16,24},{18,... | collective-permute-start | bytes 1572872 | tf_op jit(solution)/shard_map/ppermute | solution.py:261
  17.2 13.5 %collective-permute-start.6 = (bf16[1024,256]{1,0:T(8,128)(2,1)S(1)}, bf16[1024,256]{1,0:T(8,128)(2,1)S(1)}, u32[]{:S(2)}, u32[]{:S(2)}) collective-permute-start(bf16[1024,256]{1,0:T(8,128)(2,1)S(1)} %pad_maximum_fusion.1.refs_4_.refs_1_), channel_id=1, source_target_pairs={{8,16},{10,18},{12,20},{14,22},{16,8},{18,10},{20,12},{22,14},{9,1... | collective-permute-start | bytes 1572872 | tf_op jit(solution)/shard_map/ppermute | solution.py:261
  21.1 12.4 %collective-permute-start.8 = (bf16[512,256]{1,0:T(8,128)(2,1)S(1)}, bf16[512,256]{1,0:T(8,128)(2,1)S(1)}, u32[]{:S(2)}, u32[]{:S(2)}) collective-permute-start(bf16[512,256]{1,0:T(8,128)(2,1)S(1)} %collective-permute-done.7.refs_4_), channel_id=1, source_target_pairs={{0,8},{2,10},{4,12},{6,14},{8,0},{10,2},{12,4},{14,6},{16,24},{18,... | collective-permute-start | bytes 786440 | tf_op jit(solution)/shard_map/ppermute | solution.py:261
  22.4 14.0 %collective-permute-start.9 = (bf16[512,256]{1,0:T(8,128)(2,1)S(1)}, bf16[512,256]{1,0:T(8,128)(2,1)S(1)}, u32[]{:S(2)}, u32[]{:S(2)}) collective-permute-start(bf16[512,256]{1,0:T(8,128)(2,1)S(1)} %collective-permute-done.7.refs_4_), channel_id=1, source_target_pairs={{8,16},{10,18},{12,20},{14,22},{16,8},{18,10},{20,12},{22,14},{9,1... | collective-permute-start | bytes 786440 | tf_op jit(solution)/shard_map/ppermute | solution.py:261
  24.7 11.6 %copy-start = (bf16[256,256]{1,0:T(8,128)(2,1)S(1)}, bf16[256,256]{1,0:T(8,128)(2,1)}, u32[]{:S(2)}) copy-start(bf16[256,256]{1,0:T(8,128)(2,1)} %constant.90.clone.table) | copy-start | bytes 393220

commit v5 on v4

--- a/solution.py
+++ b/solution.py
@@ -78,7 +78,7 @@
         scale = lax.rsqrt(power + 0.1 * level + 1e-06)
         return jnp.concatenate([real_part * scale, imag_part * scale], axis=1)
 
-    together = max(1, 16 // width)
+    together = max(2, 16 // width)
     for s in range(0, segments, together):
         for k in range(together):
             copies[s + k].wait()
@@ -120,7 +120,7 @@
     return jnp.take(split, jnp.bitwise_xor(mine, jnp.arange(parts)), axis=0)
 
 
-def gather(moves, held, sem):
+def gather(moves, held, sem, others=()):
     copies, spot = [], 0
     for k, (ref, first, count) in enumerate(moves):
         copies.append(
@@ -130,11 +130,13 @@
         )
         spot += count
         copies[-1].start()
+    for copy in others:
+        copy.start()
     for copy in copies:
         copy.wait()
 
 
-def add_pairs(near, fold, slots_ref, held, tiles, before, cross):
+def add_pairs(near, fold, slots_ref, held, tiles, cross, copies):
     slots = (slots_ref.shape[0] - near - 1) // (2 * near + 2)
     together = min(4, slots)
 
@@ -152,13 +154,16 @@
         if fold == 8:
             real_sum = real_sum[:8] + real_sum[8:]
             imag_sum = imag_sum[:8] + imag_sum[8:]
-        if before is not None:
-            real_sum += before[spot, pl.ds(0, F)]
-            imag_sum += before[spot, pl.ds(F, F)]
+        if copies:
+            real_sum += cross[spot, pl.ds(0, F)]
+            imag_sum += cross[spot, pl.ds(F, F)]
         cross[spot, pl.ds(0, F)] = real_sum
         cross[spot, pl.ds(F, F)] = imag_sum
 
-    def owner_of(owner, _):
+    for owner in range(near):
+        if copies:
+            copies[owner].wait()
+
         def some_pairs(step, _):
             for k in range(together):
                 one_pair(owner * slots + step * together + k)
@@ -166,9 +171,6 @@
 
         count = jnp.clip(slots_ref[2 * near * slots + owner], 0, slots)
         lax.fori_loop(0, lax.div(count + (together - 1), together), some_pairs, 0)
-        return 0
-
-    lax.fori_loop(0, near, owner_of, 0)
 
 
 def first_kernel(near, fold, size, rows, slots_ref, *refs):
@@ -178,24 +180,28 @@
     for plane in range(3):
         moves += [(pieces[plane], 0, 2 * size), (pieces[3 + plane], 0, part)]
     gather(moves, held, sem)
-    add_pairs(near, fold, slots_ref, held, list(range(0, rows, 16)), None, cross)
+    add_pairs(near, fold, slots_ref, held, list(range(0, rows, 16)), cross, [])
 
 
 def last_kernel(near, fold, windows, size, rows, slots_ref, before, table, *refs):
     pieces, (out_ref, held, cross, table_ref, sem) = refs[:6], refs[6:]
     table_copy = pltpu.make_async_copy(table, table_ref, sem.at[6])
     table_copy.start()
+    span = cross.shape[0] // near
+    copies = []
+    for owner in range(near):
+        spot = pl.ds(owner * span, span)
+        copies.append(pltpu.make_async_copy(before.at[spot], cross.at[spot], sem.at[7 + owner]))
     part = (near - 2) * size
     moves = []
     for plane in range(3):
         piece, last = pieces[plane], pieces[3 + plane]
         moves += [(piece, part, piece.shape[0] - part), (last, 0, 2 * size)]
-    gather(moves, held, sem)
+    gather(moves, held, sem, copies)
     tiles = [w * near * size + r for w in range(windows) for r in range(0, rows, 16)]
-    add_pairs(near, fold, slots_ref, held, tiles, before, cross)
+    add_pairs(near, fold, slots_ref, held, tiles, cross, copies)
     table_copy.wait()
     mine = lax.rem(lax.axis_index("chan"), near)
-    span = cross.shape[0] // near
     for owner in range(near):
         spectrum = cross[pl.ds(owner * span, span), :]
         high = spectrum.astype(jnp.bfloat16)
@@ -333,7 +339,7 @@
     groups = [[q * parts + k for k in range(parts)] for q in range(group_total)]
     lagged = pl.pallas_call(
         functools.partial(last_kernel, near, fold, wins - 1, size, rows),
-        in_specs=[smem, vmem, hbm] + [hbm] * 6,
+        in_specs=[smem, hbm, hbm] + [hbm] * 6,
         out_specs=vmem,
         out_shape=jax.ShapeDtypeStruct(
             (near, slots * fold, LAGS), jnp.bfloat16 if fold == width else jnp.float32
@@ -342,7 +348,7 @@
             pltpu.VMEM((3 * (wins - 1) * near * size, 2 * F), jnp.bfloat16),
             pltpu.VMEM(cross.shape, jnp.float32),
             pltpu.VMEM(table.shape, table.dtype),
-            pltpu.SemaphoreType.DMA((7,)),
+            pltpu.SemaphoreType.DMA((7 + near,)),
         ],
         compiler_params=params,
     )(last_rows, before, table, *planes[1], *planes[2])

time: 55.2 us -> 54.9 us (level)
  transfers between devices with their start and end apart: 10 -> 10, of which waited for: 7 -> 7; matrix products, arithmetic and copies ran while one was open for 1% -> 1% of each run, Pallas kernels for 3% -> 4%
where the time goes in v5:
time: 54.9 us; the launch traced here: 54.6 us
  starting transfers between devices  15.2 us (28%)
  waiting for transfers between devices  14.6 us (27%)
  blocking collectives  13.8 us (25%)
  Pallas kernels  9.24 us (17%)
  between operations  0.89 us (2%)
    all_to_all x1, blocking collectives, per_device(): lax.all_to_all(lagged, both, 0, 0, axis_index_groups=groups, tiled=True)  13.8 us
    ppermute x6, starting transfers between devices, along(): return lax.ppermute(block, 'chan', [r for r in route if 0 <= r[1] < chans])  9.74 us
    ppermute x6, waiting for transfers between devices, along(): return lax.ppermute(block, 'chan', [r for r in route if 0 <= r[1] < chans])  9.54 us
    ppermute x4, starting transfers between devices, partner(): lax.ppermute(block, both, [(i, i ^ distance) for i in range(chans * wins)])  5.45 us
    ppermute x4, waiting for transfers between devices, partner(): lax.ppermute(block, both, [(i, i ^ distance) for i in range(chans * wins)])  5.06 us
    pallas_call x1, Pallas kernels, per_device(): pl.pallas_call(functools.partial(last_kernel, near, fold, wins - 1, size,...  3.17 us
    pallas_call x1, Pallas kernels, whitened_parts(): pl.pallas_call(functools.partial(spectra_kernel, near, wins), in_specs=[h...  2.35 us
    pallas_call x1, Pallas kernels, per_device(): pl.pallas_call(functools.partial(first_kernel, near, fold, size, rows), i...  2.07 us
  transfers between devices with their start and end apart: 10, of which 7 were waited for; matrix products, arithmetic and copies ran while one was open for 1% of the time, Pallas kernels for 4%

profile of v5, /device:TPU:17, one launch (start us, length us, event | category | flops | bytes accessed | tf_op | source)
XLA Modules:
  0.0 54.6 jit_solution(12168251067127343468)
XLA Ops:
  0.7 0.0 copy-start.1
  0.7 2.4 %shard_map.64 = bf16[8,256,256]{2,1,0:T(8,128)(2,1)S(1)} custom-call(bf16[4,512,512]{2,1,0:T(8,128)(2,1)} %records.1), custom_call_target="tpu_custom_call" | custom-call | tf_op jit(solution)/shard_map/pallas_call | solution.py:103
  3.1 0.0 copy-done.1
  3.1 0.1 select_convert_fusion
  3.2 0.7 %collective-permute-start = (bf16[1040,256]{1,0:T(8,128)(2,1)S(1)}, bf16[1040,256]{1,0:T(8,128)(2,1)S(1)}, u32[]{:S(2)}, u32[]{:S(2)}) collective-permute-start(bf16[1040,256]{1,0:T(8,128)(2,1)S(1)} %pad_maximum_fusion), channel_id=1, source_target_pairs={{0,2},{1,3},{2,0},{3,1},{4,6},{5,7},{6,4},{7,5},{8,10},{9,11},{10,... | collective-permute-start | bytes 1597448 | tf_op jit(solution)/shard_map/ppermute | solution.py:263
  4.0 1.5 %collective-permute-done = bf16[1040,256]{1,0:T(8,128)(2,1)S(1)} collective-permute-done((bf16[1040,256]{1,0:T(8,128)(2,1)S(1)}, bf16[1040,256]{1,0:T(8,128)(2,1)S(1)}, u32[]{:S(2)}, u32[]{:S(2)}) %collective-permute-start) | collective-permute-done | bytes 532512 | tf_op jit(solution)/shard_map/ppermute | solution.py:263
  5.6 1.3 %collective-permute-start.4 = (bf16[512,256]{1,0:T(8,128)(2,1)S(1)}, bf16[512,256]{1,0:T(8,128)(2,1)S(1)}, u32[]{:S(2)}, u32[]{:S(2)}) collective-permute-start(bf16[512,256]{1,0:T(8,128)(2,1)S(1)} %pad_maximum_fusion.4), channel_id=1, source_target_pairs={{0,1},{1,0},{2,3},{3,2},{4,5},{5,4},{6,7},{7,6},{8,9},{9,8},{10,11... | collective-permute-start | bytes 786440 | tf_op jit(solution)/shard_map/ppermute | solution.py:263
  6.9 1.3 %collective-permute-start.1 = (bf16[544,256]{1,0:T(8,128)(2,1)S(1)}, bf16[544,256]{1,0:T(8,128)(2,1)S(1)}, u32[]{:S(2)}, u32[]{:S(2)}) collective-permute-start(bf16[544,256]{1,0:T(8,128)(2,1)S(1)} %pad_maximum_fusion.2), channel_id=1, source_target_pairs={{0,4},{1,5},{2,6},{3,7},{4,0},{5,1},{6,2},{7,3},{8,12},{9,13},{10,... | collective-permute-start | bytes 835592 | tf_op jit(solution)/shard_map/ppermute | solution.py:263
  8.2 1.4 %collective-permute-start.2 = (bf16[512,256]{1,0:T(8,128)(2,1)S(1)}, bf16[512,256]{1,0:T(8,128)(2,1)S(1)}, u32[]{:S(2)}, u32[]{:S(2)}) collective-permute-start(bf16[512,256]{1,0:T(8,128)(2,1)S(1)} %pad_maximum_fusion.3.refs_1_), channel_id=1, source_target_pairs={{0,8},{2,10},{4,12},{6,14},{8,0},{10,2},{12,4},{14,6},{16,24},{18,... | collective-permute-start | bytes 786440 | tf_op jit(solution)/shard_map/ppermute | solution.py:267
  9.6 1.9 %collective-permute-start.3 = (bf16[512,256]{1,0:T(8,128)(2,1)S(1)}, bf16[512,256]{1,0:T(8,128)(2,1)S(1)}, u32[]{:S(2)}, u32[]{:S(2)}) collective-permute-start(bf16[512,256]{1,0:T(8,128)(2,1)S(1)} %pad_maximum_fusion.3.refs_1_), channel_id=1, source_target_pairs={{8,16},{10,18},{12,20},{14,22},{16,8},{18,10},{20,12},{22,14},{9,1... | collective-permute-start | bytes 786440 | tf_op jit(solution)/shard_map/ppermute | solution.py:267
  11.5 0.0 copy-start.2
  11.5 0.0 copy-start.3
  11.6 1.6 %collective-permute-done.4 = bf16[512,256]{1,0:T(8,128)(2,1)S(1)} collective-permute-done((bf16[512,256]{1,0:T(8,128)(2,1)S(1)}, bf16[512,256]{1,0:T(8,128)(2,1)S(1)}, u32[]{:S(2)}, u32[]{:S(2)}) %collective-permute-start.4) | collective-permute-done | bytes 262176 | tf_op jit(solution)/shard_map/ppermute | solution.py:263
  13.2 2.1 %collective-permute-start.7 = (bf16[512,256]{1,0:T(8,128)(2,1)S(1)}, bf16[512,256]{1,0:T(8,128)(2,1)S(1)}, u32[]{:S(2)}, u32[]{:S(2)}) collective-permute-start(bf16[512,256]{1,0:T(8,128)(2,1)S(1)} %pad_maximum_fusion.5), channel_id=1, source_target_pairs={{0,5},{1,4},{2,7},{3,6},{4,1},{5,0},{6,3},{7,2},{8,13},{9,12},{10,... | collective-permute-start | bytes 786440 | tf_op jit(solution)/shard_map/ppermute | solution.py:263
  15.4 0.0 collective-permute-done.1
  15.4 1.4 %collective-permute-start.5 = (bf16[1024,256]{1,0:T(8,128)(2,1)S(1)}, bf16[1024,256]{1,0:T(8,128)(2,1)S(1)}, u32[]{:S(2)}, u32[]{:S(2)}) collective-permute-start(bf16[1024,256]{1,0:T(8,128)(2,1)S(1)} %pad_maximum_fusion.1.refs_4_.refs_1_), channel_id=1, source_target_pairs={{0,8},{2,10},{4,12},{6,14},{8,0},{10,2},{12,4},{14,6},{16,24},{18,... | collective-permute-start | bytes 1572872 | tf_op jit(solution)/shard_map/ppermute | solution.py:267
  16.8 1.9 %collective-permute-start.6 = (bf16[1024,256]{1,0:T(8,128)(2,1)S(1)}, bf16[1024,256]{1,0:T(8,128)(2,1)S(1)}, u32[]{:S(2)}, u32[]{:S(2)}) collective-permute-start(bf16[1024,256]{1,0:T(8,128)(2,1)S(1)} %pad_maximum_fusion.1.refs_4_.refs_1_), channel_id=1, source_target_pairs={{8,16},{10,18},{12,20},{14,22},{16,8},{18,10},{20,12},{22,14},{9,1... | collective-permute-start | bytes 1572872 | tf_op jit(solution)/shard_map/ppermute | solution.py:267
  18.8 0.0 collective-permute-done.2.refs_0_
  18.8 0.0 collective-permute-done.3.refs_2_
  18.8 1.9 %collective-permute-done.7.refs_4_ = bf16[512,256]{1,0:T(8,128)(2,1)S(1)} collective-permute-done((bf16[512,256]{1,0:T(8,128)(2,1)S(1)}, bf16[512,256]{1,0:T(8,128)(2,1)S(1)}, u32[]{:S(2)}, u32[]{:S(2)}) %collective-permute-start.7) | collective-permute-done | bytes 262176 | tf_op jit(solution)/shard_map/ppermute | solution.py:263
  20.7 1.3 %collective-permute-start.8 = (bf16[512,256]{1,0:T(8,128)(2,1)S(1)}, bf16[512,256]{1,0:T(8,128)(2,1)S(1)}, u32[]{:S(2)}, u32[]{:S(2)}) collective-permute-start(bf16[512,256]{1,0:T(8,128)(2,1)S(1)} %collective-permute-done.7.refs_4_), channel_id=1, source_target_pairs={{0,8},{2,10},{4,12},{6,14},{8,0},{10,2},{12,4},{14,6},{16,24},{18,... | collective-permute-start | bytes 786440 | tf_op jit(solution)/shard_map/ppermute | solution.py:267
  22.0 1.9 %collective-permute-start.9 = (bf16[512,256]{1,0:T(8,128)(2,1)S(1)}, bf16[512,256]{1,0:T(8,128)(2,1)S(1)}, u32[]{:S(2)}, u32[]{:S(2)}) collective-permute-start(bf16[512,256]{1,0:T(8,128)(2,1)S(1)} %collective-permute-done.7.refs_4_), channel_id=1, source_target_pairs={{8,16},{10,18},{12,20},{14,22},{16,8},{18,10},{20,12},{22,14},{9,1... | collective-permute-start | bytes 786440 | tf_op jit(solution)/shard_map/ppermute | solution.py:267
  24.0 0.1 reshape_squeeze.12
  24.0 0.1 reshape_squeeze.13
  24.1 0.1 convert_reduce_fusion
  24.2 0.0 copy-done.2
  24.2 0.0 copy-done.3
  24.3 0.1 concatenate.33.slots_ref
  24.3 0.0 copy-start
  24.3 3.1 %collective-permute-done.5.refs_3_.refs_0_ = bf16[1024,256]{1,0:T(8,128)(2,1)S(1)} collective-permute-done((bf16[1024,256]{1,0:T(8,128)(2,1)S(1)}, bf16[1024,256]{1,0:T(8,128)(2,1)S(1)}, u32[]{:S(2)}, u32[]{:S(2)}) %collective-permute-start.5) | collective-permute-done | bytes 524320 | tf_op jit(solution)/shard_map/ppermute | solution.py:267
  27.4 2.9 %collective-permute-done.6.refs_5_.refs_2_ = bf16[1024,256]{1,0:T(8,128)(2,1)S(1)} collective-permute-done((bf16[1024,256]{1,0:T(8,128)(2,1)S(1)}, bf16[1024,256]{1,0:T(8,128)(2,1)S(1)}, u32[]{:S(2)}, u32[]{:S(2)}) %collective-permute-start.6) | collective-permute-done | bytes 524320 | tf_op jit(solution)/shard_map/ppermute | solution.py:267
  30.3 2.1 %shard_map.65.before = f32[2048,256]{1,0:T(8,128)S(1)} custom-call(s32[325]{0:T(512)S(1)} %concatenate.33.slots_ref, bf16[512,256]{1,0:T(8,128)(2,1)S(1)} %collective-permute-done.2.refs_0_, bf16[512,256]{1,0:T(8,128)(2,1)S(1)} %pad_maximum_fusion.3.refs_1_, bf16[512,256]{1,0:T(8,128)(2,1)S(1)} %collective-permute-done.3.refs_2_, ...), custom_call_target="tpu_custom_call" | custom-call | tf_op jit(solution)/shard_map/pallas_call | solution.py:327
  32.4 0.6 %collective-permute-done.8.refs_3_ = bf16[512,256]{1,0:T(8,128)(2,1)S(1)} collective-permute-done((bf16[512,256]{1,0:T(8,128)(2,1)S(1)}, bf16[512,256]{1,0:T(8,128)(2,1)S(1)}, u32[]{:S(2)}, u32[]{:S(2)}) %collective-permute-start.8) | collective-permute-done | bytes 262176 | tf_op jit(solution)/shard_map/ppermute | solution.py:267
  33.1 2.9 %collective-permute-done.9.refs_5_ = bf16[512,256]{1,0:T(8,128)(2,1)S(1)} collective-permute-done((bf16[512,256]{1,0:T(8,128)(2,1)S(1)}, bf16[512,256]{1,0:T(8,128)(2,1)S(1)}, u32[]{:S(2)}, u32[]{:S(2)}) %collective-permute-start.9) | collective-permute-done | bytes 262176 | tf_op jit(solution)/shard_map/ppermute | solution.py:267
  36.0 0.0 copy-done
  36.0 3.2 %shard_map.66 = bf16[4,512,128]{2,1,0:T(8,128)(2,1)S(1)} custom-call(s32[325]{0:T(512)S(1)} %concatenate.33.slots_ref, f32[2048,256]{1,0:T(8,128)S(1)} %shard_map.65.before, bf16[256,256]{1,0:T(8,128)(2,1)S(1)} %copy-done, bf16[1024,256]{1,0:T(8,128)(2,1)S(1)} %collective-permute-done.5.refs_3_.refs_0_, ...), custom_call_target="tpu_custom_call" | custom-call | tf_op jit(solution)/shard_map/pallas_call | solution.py:340
  39.1 13.8 %all_to_all.5.refs_0_ = bf16[8,256,128]{2,1,0:T(8,128)(2,1)S(1)} all-to-all(bf16[8,256,128]{2,1,0:T(8,128)(2,1)S(1)} %bitcast.32), channel_id=1, replica_groups={{0,1,2,3,4,5,6,7},{8,9,10,11,12,13,14,15},{16,17,18,19,20,21,22,23},{24..., dimensions={0} | all-to-all | bytes 1048576 | tf_op jit(solution)/shard_map/all_to_all | solution.py:358
  52.9 1.6 %shard_map.67 = f32[16,128,128]{2,1,0:T(8,128)} custom-call(s32[325]{0:T(512)S(1)} %concatenate.33.slots_ref, bf16[8,256,128]{2,1,0:T(8,128)(2,1)S(1)} %all_to_all.5.refs_0_), custom_call_target="tpu_custom_call" | custom-call | tf_op jit(solution)/shard_map/pallas_call | solution.py:360
  (23 shorter events, 0.4 us)
Async XLA Ops:
  0.7 2.4 %copy-start.1 = (s32[32,2]{0,1:T(2,128)S(1)}, s32[32,2]{0,1:T(2,128)}, u32[]{:S(2)}) copy-start(s32[32,2]{0,1:T(2,128)} %param.7) | copy-start | bytes 772
  3.2 2.3 %collective-permute-start = (bf16[1040,256]{1,0:T(8,128)(2,1)S(1)}, bf16[1040,256]{1,0:T(8,128)(2,1)S(1)}, u32[]{:S(2)}, u32[]{:S(2)}) collective-permute-start(bf16[1040,256]{1,0:T(8,128)(2,1)S(1)} %pad_maximum_fusion), channel_id=1, source_target_pairs={{0,2},{1,3},{2,0},{3,1},{4,6},{5,7},{6,4},{7,5},{8,10},{9,11},{10,... | collective-permute-start | bytes 1597448 | tf_op jit(solution)/shard_map/ppermute | solution.py:263
  5.6 7.6 %collective-permute-start.4 = (bf16[512,256]{1,0:T(8,128)(2,1)S(1)}, bf16[512,256]{1,0:T(8,128)(2,1)S(1)}, u32[]{:S(2)}, u32[]{:S(2)}) collective-permute-start(bf16[512,256]{1,0:T(8,128)(2,1)S(1)} %pad_maximum_fusion.4), channel_id=1, source_target_pairs={{0,1},{1,0},{2,3},{3,2},{4,5},{5,4},{6,7},{7,6},{8,9},{9,8},{10,11... | collective-permute-start | bytes 786440 | tf_op jit(solution)/shard_map/ppermute | solution.py:263
  6.9 8.4 %collective-permute-start.1 = (bf16[544,256]{1,0:T(8,128)(2,1)S(1)}, bf16[544,256]{1,0:T(8,128)(2,1)S(1)}, u32[]{:S(2)}, u32[]{:S(2)}) collective-permute-start(bf16[544,256]{1,0:T(8,128)(2,1)S(1)} %pad_maximum_fusion.2), channel_id=1, source_target_pairs={{0,4},{1,5},{2,6},{3,7},{4,0},{5,1},{6,2},{7,3},{8,12},{9,13},{10,... | collective-permute-start | bytes 835592 | tf_op jit(solution)/shard_map/ppermute | solution.py:263
  8.2 10.6 %collective-permute-start.2 = (bf16[512,256]{1,0:T(8,128)(2,1)S(1)}, bf16[512,256]{1,0:T(8,128)(2,1)S(1)}, u32[]{:S(2)}, u32[]{:S(2)}) collective-permute-start(bf16[512,256]{1,0:T(8,128)(2,1)S(1)} %pad_maximum_fusion.3.refs_1_), channel_id=1, source_target_pairs={{0,8},{2,10},{4,12},{6,14},{8,0},{10,2},{12,4},{14,6},{16,24},{18,... | collective-permute-start | bytes 786440 | tf_op jit(solution)/shard_map/ppermute | solution.py:267
  9.6 9.2 %collective-permute-start.3 = (bf16[512,256]{1,0:T(8,128)(2,1)S(1)}, bf16[512,256]{1,0:T(8,128)(2,1)S(1)}, u32[]{:S(2)}, u32[]{:S(2)}) collective-permute-start(bf16[512,256]{1,0:T(8,128)(2,1)S(1)} %pad_maximum_fusion.3.refs_1_), channel_id=1, source_target_pairs={{8,16},{10,18},{12,20},{14,22},{16,8},{18,10},{20,12},{22,14},{9,1... | collective-permute-start | bytes 786440 | tf_op jit(solution)/shard_map/ppermute | solution.py:267
  11.5 12.7 %copy-start.2 = (s32[32]{0:T(128)S(1)}, s32[32]{0:T(128)}, u32[]{:S(2)}) copy-start(s32[32]{0:T(128)} %param.8) | copy-start | bytes 388
  11.5 12.7 %copy-start.3 = (s32[32]{0:T(128)S(1)}, s32[32]{0:T(128)}, u32[]{:S(2)}) copy-start(s32[32]{0:T(128)} %param.9) | copy-start | bytes 388
  13.2 7.5 %collective-permute-start.7 = (bf16[512,256]{1,0:T(8,128)(2,1)S(1)}, bf16[512,256]{1,0:T(8,128)(2,1)S(1)}, u32[]{:S(2)}, u32[]{:S(2)}) collective-permute-start(bf16[512,256]{1,0:T(8,128)(2,1)S(1)} %pad_maximum_fusion.5), channel_id=1, source_target_pairs={{0,5},{1,4},{2,7},{3,6},{4,1},{5,0},{6,3},{7,2},{8,13},{9,12},{10,... | collective-permute-start | bytes 786440 | tf_op jit(solution)/shard_map/ppermute | solution.py:263
  15.4 12.0 %collective-permute-start.5 = (bf16[1024,256]{1,0:T(8,128)(2,1)S(1)}, bf16[1024,256]{1,0:T(8,128)(2,1)S(1)}, u32[]{:S(2)}, u32[]{:S(2)}) collective-permute-start(bf16[1024,256]{1,0:T(8,128)(2,1)S(1)} %pad_maximum_fusion.1.refs_4_.refs_1_), channel_id=1, source_target_pairs={{0,8},{2,10},{4,12},{6,14},{8,0},{10,2},{12,4},{14,6},{16,24},{18,... | collective-permute-start | bytes 1572872 | tf_op jit(solution)/shard_map/ppermute | solution.py:267
  16.8 13.5 %collective-permute-start.6 = (bf16[1024,256]{1,0:T(8,128)(2,1)S(1)}, bf16[1024,256]{1,0:T(8,128)(2,1)S(1)}, u32[]{:S(2)}, u32[]{:S(2)}) collective-permute-start(bf16[1024,256]{1,0:T(8,128)(2,1)S(1)} %pad_maximum_fusion.1.refs_4_.refs_1_), channel_id=1, source_target_pairs={{8,16},{10,18},{12,20},{14,22},{16,8},{18,10},{20,12},{22,14},{9,1... | collective-permute-start | bytes 1572872 | tf_op jit(solution)/shard_map/ppermute | solution.py:267
  20.7 12.4 %collective-permute-start.8 = (bf16[512,256]{1,0:T(8,128)(2,1)S(1)}, bf16[512,256]{1,0:T(8,128)(2,1)S(1)}, u32[]{:S(2)}, u32[]{:S(2)}) collective-permute-start(bf16[512,256]{1,0:T(8,128)(2,1)S(1)} %collective-permute-done.7.refs_4_), channel_id=1, source_target_pairs={{0,8},{2,10},{4,12},{6,14},{8,0},{10,2},{12,4},{14,6},{16,24},{18,... | collective-permute-start | bytes 786440 | tf_op jit(solution)/shard_map/ppermute | solution.py:267
  22.0 14.0 %collective-permute-start.9 = (bf16[512,256]{1,0:T(8,128)(2,1)S(1)}, bf16[512,256]{1,0:T(8,128)(2,1)S(1)}, u32[]{:S(2)}, u32[]{:S(2)}) collective-permute-start(bf16[512,256]{1,0:T(8,128)(2,1)S(1)} %collective-permute-done.7.refs_4_), channel_id=1, source_target_pairs={{8,16},{10,18},{12,20},{14,22},{16,8},{18,10},{20,12},{22,14},{9,1... | collective-permute-start | bytes 786440 | tf_op jit(solution)/shard_map/ppermute | solution.py:267
  24.3 11.6 %copy-start = (bf16[256,256]{1,0:T(8,128)(2,1)S(1)}, bf16[256,256]{1,0:T(8,128)(2,1)}, u32[]{:S(2)}) copy-start(bf16[256,256]{1,0:T(8,128)(2,1)} %constant.90.clone.table) | copy-start | bytes 393220

commit v6 on v5

--- a/solution.py
+++ b/solution.py
@@ -183,8 +183,10 @@
     add_pairs(near, fold, slots_ref, held, list(range(0, rows, 16)), cross, [])
 
 
-def last_kernel(near, fold, windows, size, rows, slots_ref, before, table, *refs):
-    pieces, (out_ref, held, cross, table_ref, sem) = refs[:6], refs[6:]
+def last_kernel(near, fold, windows, size, rows, slot_rows, before, table, *refs):
+    pieces, (out_ref, held, cross, table_ref, slots_ref, sem) = refs[:6], refs[6:]
+    slots_copy = pltpu.make_async_copy(slot_rows, slots_ref, sem.at[7 + near])
+    slots_copy.start()
     table_copy = pltpu.make_async_copy(table, table_ref, sem.at[6])
     table_copy.start()
     span = cross.shape[0] // near
@@ -198,6 +200,7 @@
         piece, last = pieces[plane], pieces[3 + plane]
         moves += [(piece, part, piece.shape[0] - part), (last, 0, 2 * size)]
     gather(moves, held, sem, copies)
+    slots_copy.wait()
     tiles = [w * near * size + r for w in range(windows) for r in range(0, rows, 16)]
     add_pairs(near, fold, slots_ref, held, tiles, cross, copies)
     table_copy.wait()
@@ -233,7 +236,7 @@
             values = values[:, slot * width - tile : slot * width - tile + width, :]
             root = lax.rsqrt(lax.rsqrt(jnp.abs(values))) * scale
             root = jnp.where(values < 0, -root, root)
-            kept.append(jnp.where(keep, root, 0.0))
+            kept.append(jnp.where(keep & (values != 0), root, 0.0))
         kept = jnp.concatenate(kept, axis=1) if len(kept) > 1 else kept[0]
         held[slot] = kept.reshape(BLOCK, LAGS)
         if slot % together == together - 1:
@@ -339,7 +342,7 @@
     groups = [[q * parts + k for k in range(parts)] for q in range(group_total)]
     lagged = pl.pallas_call(
         functools.partial(last_kernel, near, fold, wins - 1, size, rows),
-        in_specs=[smem, hbm, hbm] + [hbm] * 6,
+        in_specs=[hbm, hbm, hbm] + [hbm] * 6,
         out_specs=vmem,
         out_shape=jax.ShapeDtypeStruct(
             (near, slots * fold, LAGS), jnp.bfloat16 if fold == width else jnp.float32
@@ -348,7 +351,8 @@
             pltpu.VMEM((3 * (wins - 1) * near * size, 2 * F), jnp.bfloat16),
             pltpu.VMEM(cross.shape, jnp.float32),
             pltpu.VMEM(table.shape, table.dtype),
-            pltpu.SemaphoreType.DMA((7 + near,)),
+            pltpu.SMEM(last_rows.shape, jnp.int32),
+            pltpu.SemaphoreType.DMA((8 + near,)),
         ],
         compiler_params=params,
     )(last_rows, before, table, *planes[1], *planes[2])

time: 54.9 us -> 54 us (0.984)
  Pallas kernels: 9.24 us -> 7.91 us
    pallas_call x1, Pallas kernels: 3.17 us -> 2.27 us  [per_device(): pl.pallas_call(functools.partial(last_kernel, near, fold, wins - 1, size,...]
  transfers between devices with their start and end apart: 10 -> 10, of which waited for: 7 -> 7; matrix products, arithmetic and copies ran while one was open for 1% -> 1% of each run, Pallas kernels for 4% -> 3%
where the time goes in v6:
time: 54 us; the launch traced here: 53.7 us
  starting transfers between devices  15.2 us (28%)
  waiting for transfers between devices  15.1 us (28%)
  blocking collectives  13.8 us (26%)
  Pallas kernels  7.91 us (15%)
  between operations  0.89 us (2%)
    all_to_all x1, blocking collectives, per_device(): lax.all_to_all(lagged, both, 0, 0, axis_index_groups=groups, tiled=True)  13.8 us
    ppermute x6, waiting for transfers between devices, along(): return lax.ppermute(block, 'chan', [r for r in route if 0 <= r[1] < chans])  10 us
    ppermute x6, starting transfers between devices, along(): return lax.ppermute(block, 'chan', [r for r in route if 0 <= r[1] < chans])  9.74 us
    ppermute x4, starting transfers between devices, partner(): lax.ppermute(block, both, [(i, i ^ distance) for i in range(chans * wins)])  5.45 us
    ppermute x4, waiting for transfers between devices, partner(): lax.ppermute(block, both, [(i, i ^ distance) for i in range(chans * wins)])  5.06 us
    pallas_call x1, Pallas kernels, whitened_parts(): pl.pallas_call(functools.partial(spectra_kernel, near, wins), in_specs=[h...  2.35 us
    pallas_call x1, Pallas kernels, per_device(): pl.pallas_call(functools.partial(last_kernel, near, fold, wins - 1, size,...  2.27 us
    pallas_call x1, Pallas kernels, per_device(): pl.pallas_call(functools.partial(stack_kernel, near, width, 1.0 / scale),...  1.69 us
  transfers between devices with their start and end apart: 10, of which 7 were waited for; matrix products, arithmetic and copies ran while one was open for 1% of the time, Pallas kernels for 3%

profile of v6, /device:TPU:17, one launch (start us, length us, event | category | flops | bytes accessed | tf_op | source)
XLA Modules:
  0.0 53.7 jit_solution(3279989956885199605)
XLA Ops:
  0.7 0.0 copy-start.1
  0.7 2.4 %shard_map.64 = bf16[8,256,256]{2,1,0:T(8,128)(2,1)S(1)} custom-call(bf16[4,512,512]{2,1,0:T(8,128)(2,1)} %records.1), custom_call_target="tpu_custom_call" | custom-call | tf_op jit(solution)/shard_map/pallas_call | solution.py:103
  3.1 0.0 copy-done.1
  3.1 0.1 select_convert_fusion
  3.2 0.7 %collective-permute-start = (bf16[1040,256]{1,0:T(8,128)(2,1)S(1)}, bf16[1040,256]{1,0:T(8,128)(2,1)S(1)}, u32[]{:S(2)}, u32[]{:S(2)}) collective-permute-start(bf16[1040,256]{1,0:T(8,128)(2,1)S(1)} %pad_maximum_fusion), channel_id=1, source_target_pairs={{0,2},{1,3},{2,0},{3,1},{4,6},{5,7},{6,4},{7,5},{8,10},{9,11},{10,... | collective-permute-start | bytes 1597448 | tf_op jit(solution)/shard_map/ppermute | solution.py:266
  4.0 1.5 %collective-permute-done = bf16[1040,256]{1,0:T(8,128)(2,1)S(1)} collective-permute-done((bf16[1040,256]{1,0:T(8,128)(2,1)S(1)}, bf16[1040,256]{1,0:T(8,128)(2,1)S(1)}, u32[]{:S(2)}, u32[]{:S(2)}) %collective-permute-start) | collective-permute-done | bytes 532512 | tf_op jit(solution)/shard_map/ppermute | solution.py:266
  5.6 1.3 %collective-permute-start.4 = (bf16[512,256]{1,0:T(8,128)(2,1)S(1)}, bf16[512,256]{1,0:T(8,128)(2,1)S(1)}, u32[]{:S(2)}, u32[]{:S(2)}) collective-permute-start(bf16[512,256]{1,0:T(8,128)(2,1)S(1)} %pad_maximum_fusion.4), channel_id=1, source_target_pairs={{0,1},{1,0},{2,3},{3,2},{4,5},{5,4},{6,7},{7,6},{8,9},{9,8},{10,11... | collective-permute-start | bytes 786440 | tf_op jit(solution)/shard_map/ppermute | solution.py:266
  6.9 1.3 %collective-permute-start.1 = (bf16[544,256]{1,0:T(8,128)(2,1)S(1)}, bf16[544,256]{1,0:T(8,128)(2,1)S(1)}, u32[]{:S(2)}, u32[]{:S(2)}) collective-permute-start(bf16[544,256]{1,0:T(8,128)(2,1)S(1)} %pad_maximum_fusion.2), channel_id=1, source_target_pairs={{0,4},{1,5},{2,6},{3,7},{4,0},{5,1},{6,2},{7,3},{8,12},{9,13},{10,... | collective-permute-start | bytes 835592 | tf_op jit(solution)/shard_map/ppermute | solution.py:266
  8.2 1.4 %collective-permute-start.2 = (bf16[512,256]{1,0:T(8,128)(2,1)S(1)}, bf16[512,256]{1,0:T(8,128)(2,1)S(1)}, u32[]{:S(2)}, u32[]{:S(2)}) collective-permute-start(bf16[512,256]{1,0:T(8,128)(2,1)S(1)} %pad_maximum_fusion.3.refs_1_), channel_id=1, source_target_pairs={{0,8},{2,10},{4,12},{6,14},{8,0},{10,2},{12,4},{14,6},{16,24},{18,... | collective-permute-start | bytes 786440 | tf_op jit(solution)/shard_map/ppermute | solution.py:270
  9.6 1.9 %collective-permute-start.3 = (bf16[512,256]{1,0:T(8,128)(2,1)S(1)}, bf16[512,256]{1,0:T(8,128)(2,1)S(1)}, u32[]{:S(2)}, u32[]{:S(2)}) collective-permute-start(bf16[512,256]{1,0:T(8,128)(2,1)S(1)} %pad_maximum_fusion.3.refs_1_), channel_id=1, source_target_pairs={{8,16},{10,18},{12,20},{14,22},{16,8},{18,10},{20,12},{22,14},{9,1... | collective-permute-start | bytes 786440 | tf_op jit(solution)/shard_map/ppermute | solution.py:270
  11.5 0.0 copy-start.2
  11.5 0.0 copy-start.3
  11.6 1.6 %collective-permute-done.4 = bf16[512,256]{1,0:T(8,128)(2,1)S(1)} collective-permute-done((bf16[512,256]{1,0:T(8,128)(2,1)S(1)}, bf16[512,256]{1,0:T(8,128)(2,1)S(1)}, u32[]{:S(2)}, u32[]{:S(2)}) %collective-permute-start.4) | collective-permute-done | bytes 262176 | tf_op jit(solution)/shard_map/ppermute | solution.py:266
  13.2 2.1 %collective-permute-start.7 = (bf16[512,256]{1,0:T(8,128)(2,1)S(1)}, bf16[512,256]{1,0:T(8,128)(2,1)S(1)}, u32[]{:S(2)}, u32[]{:S(2)}) collective-permute-start(bf16[512,256]{1,0:T(8,128)(2,1)S(1)} %pad_maximum_fusion.5), channel_id=1, source_target_pairs={{0,5},{1,4},{2,7},{3,6},{4,1},{5,0},{6,3},{7,2},{8,13},{9,12},{10,... | collective-permute-start | bytes 786440 | tf_op jit(solution)/shard_map/ppermute | solution.py:266
  15.4 0.0 collective-permute-done.1
  15.4 1.4 %collective-permute-start.5 = (bf16[1024,256]{1,0:T(8,128)(2,1)S(1)}, bf16[1024,256]{1,0:T(8,128)(2,1)S(1)}, u32[]{:S(2)}, u32[]{:S(2)}) collective-permute-start(bf16[1024,256]{1,0:T(8,128)(2,1)S(1)} %pad_maximum_fusion.1.refs_4_.refs_1_), channel_id=1, source_target_pairs={{0,8},{2,10},{4,12},{6,14},{8,0},{10,2},{12,4},{14,6},{16,24},{18,... | collective-permute-start | bytes 1572872 | tf_op jit(solution)/shard_map/ppermute | solution.py:270
  16.8 1.9 %collective-permute-start.6 = (bf16[1024,256]{1,0:T(8,128)(2,1)S(1)}, bf16[1024,256]{1,0:T(8,128)(2,1)S(1)}, u32[]{:S(2)}, u32[]{:S(2)}) collective-permute-start(bf16[1024,256]{1,0:T(8,128)(2,1)S(1)} %pad_maximum_fusion.1.refs_4_.refs_1_), channel_id=1, source_target_pairs={{8,16},{10,18},{12,20},{14,22},{16,8},{18,10},{20,12},{22,14},{9,1... | collective-permute-start | bytes 1572872 | tf_op jit(solution)/shard_map/ppermute | solution.py:270
  18.8 0.0 collective-permute-done.2.refs_0_
  18.8 0.0 collective-permute-done.3.refs_2_
  18.8 1.9 %collective-permute-done.7.refs_4_ = bf16[512,256]{1,0:T(8,128)(2,1)S(1)} collective-permute-done((bf16[512,256]{1,0:T(8,128)(2,1)S(1)}, bf16[512,256]{1,0:T(8,128)(2,1)S(1)}, u32[]{:S(2)}, u32[]{:S(2)}) %collective-permute-start.7) | collective-permute-done | bytes 262176 | tf_op jit(solution)/shard_map/ppermute | solution.py:266
  20.7 1.3 %collective-permute-start.8 = (bf16[512,256]{1,0:T(8,128)(2,1)S(1)}, bf16[512,256]{1,0:T(8,128)(2,1)S(1)}, u32[]{:S(2)}, u32[]{:S(2)}) collective-permute-start(bf16[512,256]{1,0:T(8,128)(2,1)S(1)} %collective-permute-done.7.refs_4_), channel_id=1, source_target_pairs={{0,8},{2,10},{4,12},{6,14},{8,0},{10,2},{12,4},{14,6},{16,24},{18,... | collective-permute-start | bytes 786440 | tf_op jit(solution)/shard_map/ppermute | solution.py:270
  22.0 1.9 %collective-permute-start.9 = (bf16[512,256]{1,0:T(8,128)(2,1)S(1)}, bf16[512,256]{1,0:T(8,128)(2,1)S(1)}, u32[]{:S(2)}, u32[]{:S(2)}) collective-permute-start(bf16[512,256]{1,0:T(8,128)(2,1)S(1)} %collective-permute-done.7.refs_4_), channel_id=1, source_target_pairs={{8,16},{10,18},{12,20},{14,22},{16,8},{18,10},{20,12},{22,14},{9,1... | collective-permute-start | bytes 786440 | tf_op jit(solution)/shard_map/ppermute | solution.py:270
  24.0 0.1 reshape_squeeze.12
  24.0 0.1 reshape_squeeze.13
  24.1 0.1 convert_reduce_fusion
  24.2 0.0 copy-done.2
  24.2 0.0 copy-done.3
  24.3 0.1 concatenate.33.slots_ref.slot_rows
  24.3 0.0 copy-start
  24.3 3.1 %collective-permute-done.5.refs_3_.refs_0_ = bf16[1024,256]{1,0:T(8,128)(2,1)S(1)} collective-permute-done((bf16[1024,256]{1,0:T(8,128)(2,1)S(1)}, bf16[1024,256]{1,0:T(8,128)(2,1)S(1)}, u32[]{:S(2)}, u32[]{:S(2)}) %collective-permute-start.5) | collective-permute-done | bytes 524320 | tf_op jit(solution)/shard_map/ppermute | solution.py:270
  27.4 2.9 %collective-permute-done.6.refs_5_.refs_2_ = bf16[1024,256]{1,0:T(8,128)(2,1)S(1)} collective-permute-done((bf16[1024,256]{1,0:T(8,128)(2,1)S(1)}, bf16[1024,256]{1,0:T(8,128)(2,1)S(1)}, u32[]{:S(2)}, u32[]{:S(2)}) %collective-permute-start.6) | collective-permute-done | bytes 524320 | tf_op jit(solution)/shard_map/ppermute | solution.py:270
  30.3 1.6 %shard_map.65.before = f32[2048,256]{1,0:T(8,128)S(1)} custom-call(s32[325]{0:T(512)S(1)} %concatenate.33.slots_ref.slot_rows, bf16[512,256]{1,0:T(8,128)(2,1)S(1)} %collective-permute-done.2.refs_0_, bf16[512,256]{1,0:T(8,128)(2,1)S(1)} %pad_maximum_fusion.3.refs_1_, bf16[512,256]{1,0:T(8,128)(2,1)S(1)} %collective-permute-done.3.refs_2_, ...), custom_call_target="tpu_custom_call" | custom-call | tf_op jit(solution)/shard_map/pallas_call | solution.py:330
  32.0 1.1 %collective-permute-done.8.refs_3_ = bf16[512,256]{1,0:T(8,128)(2,1)S(1)} collective-permute-done((bf16[512,256]{1,0:T(8,128)(2,1)S(1)}, bf16[512,256]{1,0:T(8,128)(2,1)S(1)}, u32[]{:S(2)}, u32[]{:S(2)}) %collective-permute-start.8) | collective-permute-done | bytes 262176 | tf_op jit(solution)/shard_map/ppermute | solution.py:270
  33.1 2.9 %collective-permute-done.9.refs_5_ = bf16[512,256]{1,0:T(8,128)(2,1)S(1)} collective-permute-done((bf16[512,256]{1,0:T(8,128)(2,1)S(1)}, bf16[512,256]{1,0:T(8,128)(2,1)S(1)}, u32[]{:S(2)}, u32[]{:S(2)}) %collective-permute-start.9) | collective-permute-done | bytes 262176 | tf_op jit(solution)/shard_map/ppermute | solution.py:270
  36.0 0.0 copy-done
  36.0 2.3 %shard_map.66 = bf16[4,512,128]{2,1,0:T(8,128)(2,1)S(1)} custom-call(s32[325]{0:T(512)S(1)} %concatenate.33.slots_ref.slot_rows, f32[2048,256]{1,0:T(8,128)S(1)} %shard_map.65.before, bf16[256,256]{1,0:T(8,128)(2,1)S(1)} %copy-done, bf16[1024,256]{1,0:T(8,128)(2,1)S(1)} %collective-permute-done.5.refs_3_.refs_0_, ...), custom_call_target="tpu_custom_call" | custom-call | tf_op jit(solution)/shard_map/pallas_call | solution.py:343
  38.2 13.8 %all_to_all.5.refs_0_ = bf16[8,256,128]{2,1,0:T(8,128)(2,1)S(1)} all-to-all(bf16[8,256,128]{2,1,0:T(8,128)(2,1)S(1)} %bitcast.32), channel_id=1, replica_groups={{0,1,2,3,4,5,6,7},{8,9,10,11,12,13,14,15},{16,17,18,19,20,21,22,23},{24..., dimensions={0} | all-to-all | bytes 1048576 | tf_op jit(solution)/shard_map/all_to_all | solution.py:362
  52.0 1.7 %shard_map.67 = f32[16,128,128]{2,1,0:T(8,128)} custom-call(s32[325]{0:T(512)S(1)} %concatenate.33.slots_ref.slot_rows, bf16[8,256,128]{2,1,0:T(8,128)(2,1)S(1)} %all_to_all.5.refs_0_), custom_call_target="tpu_custom_call" | custom-call | tf_op jit(solution)/shard_map/pallas_call | solution.py:364
  (23 shorter events, 0.4 us)
Async XLA Ops:
  0.7 2.4 %copy-start.1 = (s32[32,2]{0,1:T(2,128)S(1)}, s32[32,2]{0,1:T(2,128)}, u32[]{:S(2)}) copy-start(s32[32,2]{0,1:T(2,128)} %param.7) | copy-start | bytes 772
  3.2 2.3 %collective-permute-start = (bf16[1040,256]{1,0:T(8,128)(2,1)S(1)}, bf16[1040,256]{1,0:T(8,128)(2,1)S(1)}, u32[]{:S(2)}, u32[]{:S(2)}) collective-permute-start(bf16[1040,256]{1,0:T(8,128)(2,1)S(1)} %pad_maximum_fusion), channel_id=1, source_target_pairs={{0,2},{1,3},{2,0},{3,1},{4,6},{5,7},{6,4},{7,5},{8,10},{9,11},{10,... | collective-permute-start | bytes 1597448 | tf_op jit(solution)/shard_map/ppermute | solution.py:266
  5.6 7.6 %collective-permute-start.4 = (bf16[512,256]{1,0:T(8,128)(2,1)S(1)}, bf16[512,256]{1,0:T(8,128)(2,1)S(1)}, u32[]{:S(2)}, u32[]{:S(2)}) collective-permute-start(bf16[512,256]{1,0:T(8,128)(2,1)S(1)} %pad_maximum_fusion.4), channel_id=1, source_target_pairs={{0,1},{1,0},{2,3},{3,2},{4,5},{5,4},{6,7},{7,6},{8,9},{9,8},{10,11... | collective-permute-start | bytes 786440 | tf_op jit(solution)/shard_map/ppermute | solution.py:266
  6.9 8.4 %collective-permute-start.1 = (bf16[544,256]{1,0:T(8,128)(2,1)S(1)}, bf16[544,256]{1,0:T(8,128)(2,1)S(1)}, u32[]{:S(2)}, u32[]{:S(2)}) collective-permute-start(bf16[544,256]{1,0:T(8,128)(2,1)S(1)} %pad_maximum_fusion.2), channel_id=1, source_target_pairs={{0,4},{1,5},{2,6},{3,7},{4,0},{5,1},{6,2},{7,3},{8,12},{9,13},{10,... | collective-permute-start | bytes 835592 | tf_op jit(solution)/shard_map/ppermute | solution.py:266
  8.2 10.6 %collective-permute-start.2 = (bf16[512,256]{1,0:T(8,128)(2,1)S(1)}, bf16[512,256]{1,0:T(8,128)(2,1)S(1)}, u32[]{:S(2)}, u32[]{:S(2)}) collective-permute-start(bf16[512,256]{1,0:T(8,128)(2,1)S(1)} %pad_maximum_fusion.3.refs_1_), channel_id=1, source_target_pairs={{0,8},{2,10},{4,12},{6,14},{8,0},{10,2},{12,4},{14,6},{16,24},{18,... | collective-permute-start | bytes 786440 | tf_op jit(solution)/shard_map/ppermute | solution.py:270
  9.6 9.2 %collective-permute-start.3 = (bf16[512,256]{1,0:T(8,128)(2,1)S(1)}, bf16[512,256]{1,0:T(8,128)(2,1)S(1)}, u32[]{:S(2)}, u32[]{:S(2)}) collective-permute-start(bf16[512,256]{1,0:T(8,128)(2,1)S(1)} %pad_maximum_fusion.3.refs_1_), channel_id=1, source_target_pairs={{8,16},{10,18},{12,20},{14,22},{16,8},{18,10},{20,12},{22,14},{9,1... | collective-permute-start | bytes 786440 | tf_op jit(solution)/shard_map/ppermute | solution.py:270
  11.5 12.7 %copy-start.2 = (s32[32]{0:T(128)S(1)}, s32[32]{0:T(128)}, u32[]{:S(2)}) copy-start(s32[32]{0:T(128)} %param.8) | copy-start | bytes 388
  11.5 12.7 %copy-start.3 = (s32[32]{0:T(128)S(1)}, s32[32]{0:T(128)}, u32[]{:S(2)}) copy-start(s32[32]{0:T(128)} %param.9) | copy-start | bytes 388
  13.2 7.5 %collective-permute-start.7 = (bf16[512,256]{1,0:T(8,128)(2,1)S(1)}, bf16[512,256]{1,0:T(8,128)(2,1)S(1)}, u32[]{:S(2)}, u32[]{:S(2)}) collective-permute-start(bf16[512,256]{1,0:T(8,128)(2,1)S(1)} %pad_maximum_fusion.5), channel_id=1, source_target_pairs={{0,5},{1,4},{2,7},{3,6},{4,1},{5,0},{6,3},{7,2},{8,13},{9,12},{10,... | collective-permute-start | bytes 786440 | tf_op jit(solution)/shard_map/ppermute | solution.py:266
  15.4 12.0 %collective-permute-start.5 = (bf16[1024,256]{1,0:T(8,128)(2,1)S(1)}, bf16[1024,256]{1,0:T(8,128)(2,1)S(1)}, u32[]{:S(2)}, u32[]{:S(2)}) collective-permute-start(bf16[1024,256]{1,0:T(8,128)(2,1)S(1)} %pad_maximum_fusion.1.refs_4_.refs_1_), channel_id=1, source_target_pairs={{0,8},{2,10},{4,12},{6,14},{8,0},{10,2},{12,4},{14,6},{16,24},{18,... | collective-permute-start | bytes 1572872 | tf_op jit(solution)/shard_map/ppermute | solution.py:270
  16.8 13.5 %collective-permute-start.6 = (bf16[1024,256]{1,0:T(8,128)(2,1)S(1)}, bf16[1024,256]{1,0:T(8,128)(2,1)S(1)}, u32[]{:S(2)}, u32[]{:S(2)}) collective-permute-start(bf16[1024,256]{1,0:T(8,128)(2,1)S(1)} %pad_maximum_fusion.1.refs_4_.refs_1_), channel_id=1, source_target_pairs={{8,16},{10,18},{12,20},{14,22},{16,8},{18,10},{20,12},{22,14},{9,1... | collective-permute-start | bytes 1572872 | tf_op jit(solution)/shard_map/ppermute | solution.py:270
  20.7 12.4 %collective-permute-start.8 = (bf16[512,256]{1,0:T(8,128)(2,1)S(1)}, bf16[512,256]{1,0:T(8,128)(2,1)S(1)}, u32[]{:S(2)}, u32[]{:S(2)}) collective-permute-start(bf16[512,256]{1,0:T(8,128)(2,1)S(1)} %collective-permute-done.7.refs_4_), channel_id=1, source_target_pairs={{0,8},{2,10},{4,12},{6,14},{8,0},{10,2},{12,4},{14,6},{16,24},{18,... | collective-permute-start | bytes 786440 | tf_op jit(solution)/shard_map/ppermute | solution.py:270
  22.0 14.0 %collective-permute-start.9 = (bf16[512,256]{1,0:T(8,128)(2,1)S(1)}, bf16[512,256]{1,0:T(8,128)(2,1)S(1)}, u32[]{:S(2)}, u32[]{:S(2)}) collective-permute-start(bf16[512,256]{1,0:T(8,128)(2,1)S(1)} %collective-permute-done.7.refs_4_), channel_id=1, source_target_pairs={{8,16},{10,18},{12,20},{14,22},{16,8},{18,10},{20,12},{22,14},{9,1... | collective-permute-start | bytes 786440 | tf_op jit(solution)/shard_map/ppermute | solution.py:270
  24.3 11.6 %copy-start = (bf16[256,256]{1,0:T(8,128)(2,1)S(1)}, bf16[256,256]{1,0:T(8,128)(2,1)}, u32[]{:S(2)}) copy-start(bf16[256,256]{1,0:T(8,128)(2,1)} %constant.90.clone.table) | copy-start | bytes 393220

commit v7 on v6

--- a/solution.py
+++ b/solution.py
@@ -138,7 +138,7 @@
 
 def add_pairs(near, fold, slots_ref, held, tiles, cross, copies):
     slots = (slots_ref.shape[0] - near - 1) // (2 * near + 2)
-    together = min(4, slots)
+    together = min(8, slots)
 
     def one_pair(index):
         first, second = slots_ref[index], slots_ref[near * slots + index]

time: 54 us -> 54.4 us (level)
  no operation moved by 1% of the time
where the time goes in v7:
time: 54.4 us; the launch traced here: 53.8 us
  starting transfers between devices  15.2 us (28%)
  waiting for transfers between devices  15 us (28%)
  blocking collectives  13.8 us (25%)
  Pallas kernels  8.03 us (15%)
  between operations  0.89 us (2%)
    all_to_all x1, blocking collectives, per_device(): lax.all_to_all(lagged, both, 0, 0, axis_index_groups=groups, tiled=True)  13.8 us
    ppermute x6, waiting for transfers between devices, along(): return lax.ppermute(block, 'chan', [r for r in route if 0 <= r[1] < chans])  9.94 us
    ppermute x6, starting transfers between devices, along(): return lax.ppermute(block, 'chan', [r for r in route if 0 <= r[1] < chans])  9.74 us
    ppermute x4, starting transfers between devices, partner(): lax.ppermute(block, both, [(i, i ^ distance) for i in range(chans * wins)])  5.45 us
    ppermute x4, waiting for transfers between devices, partner(): lax.ppermute(block, both, [(i, i ^ distance) for i in range(chans * wins)])  5.06 us
    pallas_call x1, Pallas kernels, whitened_parts(): pl.pallas_call(functools.partial(spectra_kernel, near, wins), in_specs=[h...  2.35 us
    pallas_call x1, Pallas kernels, per_device(): pl.pallas_call(functools.partial(last_kernel, near, fold, wins - 1, size,...  2.32 us
    pallas_call x1, Pallas kernels, per_device(): pl.pallas_call(functools.partial(stack_kernel, near, width, 1.0 / scale),...  1.69 us
  transfers between devices with their start and end apart: 10, of which 7 were waited for; matrix products, arithmetic and copies ran while one was open for 1% of the time, Pallas kernels for 3%

profile of v7, /device:TPU:17, one launch (start us, length us, event | category | flops | bytes accessed | tf_op | source)
XLA Modules:
  0.0 53.8 jit_solution(2401474887685685724)
XLA Ops:
  0.7 0.0 copy-start.1
  0.7 2.4 %shard_map.64 = bf16[8,256,256]{2,1,0:T(8,128)(2,1)S(1)} custom-call(bf16[4,512,512]{2,1,0:T(8,128)(2,1)} %records.1), custom_call_target="tpu_custom_call" | custom-call | tf_op jit(solution)/shard_map/pallas_call | solution.py:103
  3.1 0.0 copy-done.1
  3.1 0.1 select_convert_fusion
  3.2 0.7 %collective-permute-start = (bf16[1040,256]{1,0:T(8,128)(2,1)S(1)}, bf16[1040,256]{1,0:T(8,128)(2,1)S(1)}, u32[]{:S(2)}, u32[]{:S(2)}) collective-permute-start(bf16[1040,256]{1,0:T(8,128)(2,1)S(1)} %pad_maximum_fusion), channel_id=1, source_target_pairs={{0,2},{1,3},{2,0},{3,1},{4,6},{5,7},{6,4},{7,5},{8,10},{9,11},{10,... | collective-permute-start | bytes 1597448 | tf_op jit(solution)/shard_map/ppermute | solution.py:266
  4.0 1.5 %collective-permute-done = bf16[1040,256]{1,0:T(8,128)(2,1)S(1)} collective-permute-done((bf16[1040,256]{1,0:T(8,128)(2,1)S(1)}, bf16[1040,256]{1,0:T(8,128)(2,1)S(1)}, u32[]{:S(2)}, u32[]{:S(2)}) %collective-permute-start) | collective-permute-done | bytes 532512 | tf_op jit(solution)/shard_map/ppermute | solution.py:266
  5.6 1.3 %collective-permute-start.4 = (bf16[512,256]{1,0:T(8,128)(2,1)S(1)}, bf16[512,256]{1,0:T(8,128)(2,1)S(1)}, u32[]{:S(2)}, u32[]{:S(2)}) collective-permute-start(bf16[512,256]{1,0:T(8,128)(2,1)S(1)} %pad_maximum_fusion.4), channel_id=1, source_target_pairs={{0,1},{1,0},{2,3},{3,2},{4,5},{5,4},{6,7},{7,6},{8,9},{9,8},{10,11... | collective-permute-start | bytes 786440 | tf_op jit(solution)/shard_map/ppermute | solution.py:266
  6.9 1.3 %collective-permute-start.1 = (bf16[544,256]{1,0:T(8,128)(2,1)S(1)}, bf16[544,256]{1,0:T(8,128)(2,1)S(1)}, u32[]{:S(2)}, u32[]{:S(2)}) collective-permute-start(bf16[544,256]{1,0:T(8,128)(2,1)S(1)} %pad_maximum_fusion.2), channel_id=1, source_target_pairs={{0,4},{1,5},{2,6},{3,7},{4,0},{5,1},{6,2},{7,3},{8,12},{9,13},{10,... | collective-permute-start | bytes 835592 | tf_op jit(solution)/shard_map/ppermute | solution.py:266
  8.2 1.4 %collective-permute-start.2 = (bf16[512,256]{1,0:T(8,128)(2,1)S(1)}, bf16[512,256]{1,0:T(8,128)(2,1)S(1)}, u32[]{:S(2)}, u32[]{:S(2)}) collective-permute-start(bf16[512,256]{1,0:T(8,128)(2,1)S(1)} %pad_maximum_fusion.3.refs_1_), channel_id=1, source_target_pairs={{0,8},{2,10},{4,12},{6,14},{8,0},{10,2},{12,4},{14,6},{16,24},{18,... | collective-permute-start | bytes 786440 | tf_op jit(solution)/shard_map/ppermute | solution.py:270
  9.6 1.9 %collective-permute-start.3 = (bf16[512,256]{1,0:T(8,128)(2,1)S(1)}, bf16[512,256]{1,0:T(8,128)(2,1)S(1)}, u32[]{:S(2)}, u32[]{:S(2)}) collective-permute-start(bf16[512,256]{1,0:T(8,128)(2,1)S(1)} %pad_maximum_fusion.3.refs_1_), channel_id=1, source_target_pairs={{8,16},{10,18},{12,20},{14,22},{16,8},{18,10},{20,12},{22,14},{9,1... | collective-permute-start | bytes 786440 | tf_op jit(solution)/shard_map/ppermute | solution.py:270
  11.5 0.0 copy-start.2
  11.5 0.0 copy-start.3
  11.6 1.6 %collective-permute-done.4 = bf16[512,256]{1,0:T(8,128)(2,1)S(1)} collective-permute-done((bf16[512,256]{1,0:T(8,128)(2,1)S(1)}, bf16[512,256]{1,0:T(8,128)(2,1)S(1)}, u32[]{:S(2)}, u32[]{:S(2)}) %collective-permute-start.4) | collective-permute-done | bytes 262176 | tf_op jit(solution)/shard_map/ppermute | solution.py:266
  13.2 2.1 %collective-permute-start.7 = (bf16[512,256]{1,0:T(8,128)(2,1)S(1)}, bf16[512,256]{1,0:T(8,128)(2,1)S(1)}, u32[]{:S(2)}, u32[]{:S(2)}) collective-permute-start(bf16[512,256]{1,0:T(8,128)(2,1)S(1)} %pad_maximum_fusion.5), channel_id=1, source_target_pairs={{0,5},{1,4},{2,7},{3,6},{4,1},{5,0},{6,3},{7,2},{8,13},{9,12},{10,... | collective-permute-start | bytes 786440 | tf_op jit(solution)/shard_map/ppermute | solution.py:266
  15.4 0.0 collective-permute-done.1
  15.4 1.4 %collective-permute-start.5 = (bf16[1024,256]{1,0:T(8,128)(2,1)S(1)}, bf16[1024,256]{1,0:T(8,128)(2,1)S(1)}, u32[]{:S(2)}, u32[]{:S(2)}) collective-permute-start(bf16[1024,256]{1,0:T(8,128)(2,1)S(1)} %pad_maximum_fusion.1.refs_4_.refs_1_), channel_id=1, source_target_pairs={{0,8},{2,10},{4,12},{6,14},{8,0},{10,2},{12,4},{14,6},{16,24},{18,... | collective-permute-start | bytes 1572872 | tf_op jit(solution)/shard_map/ppermute | solution.py:270
  16.8 1.9 %collective-permute-start.6 = (bf16[1024,256]{1,0:T(8,128)(2,1)S(1)}, bf16[1024,256]{1,0:T(8,128)(2,1)S(1)}, u32[]{:S(2)}, u32[]{:S(2)}) collective-permute-start(bf16[1024,256]{1,0:T(8,128)(2,1)S(1)} %pad_maximum_fusion.1.refs_4_.refs_1_), channel_id=1, source_target_pairs={{8,16},{10,18},{12,20},{14,22},{16,8},{18,10},{20,12},{22,14},{9,1... | collective-permute-start | bytes 1572872 | tf_op jit(solution)/shard_map/ppermute | solution.py:270
  18.8 0.0 collective-permute-done.2.refs_0_
  18.8 0.0 collective-permute-done.3.refs_2_
  18.8 1.9 %collective-permute-done.7.refs_4_ = bf16[512,256]{1,0:T(8,128)(2,1)S(1)} collective-permute-done((bf16[512,256]{1,0:T(8,128)(2,1)S(1)}, bf16[512,256]{1,0:T(8,128)(2,1)S(1)}, u32[]{:S(2)}, u32[]{:S(2)}) %collective-permute-start.7) | collective-permute-done | bytes 262176 | tf_op jit(solution)/shard_map/ppermute | solution.py:266
  20.7 1.3 %collective-permute-start.8 = (bf16[512,256]{1,0:T(8,128)(2,1)S(1)}, bf16[512,256]{1,0:T(8,128)(2,1)S(1)}, u32[]{:S(2)}, u32[]{:S(2)}) collective-permute-start(bf16[512,256]{1,0:T(8,128)(2,1)S(1)} %collective-permute-done.7.refs_4_), channel_id=1, source_target_pairs={{0,8},{2,10},{4,12},{6,14},{8,0},{10,2},{12,4},{14,6},{16,24},{18,... | collective-permute-start | bytes 786440 | tf_op jit(solution)/shard_map/ppermute | solution.py:270
  22.0 1.9 %collective-permute-start.9 = (bf16[512,256]{1,0:T(8,128)(2,1)S(1)}, bf16[512,256]{1,0:T(8,128)(2,1)S(1)}, u32[]{:S(2)}, u32[]{:S(2)}) collective-permute-start(bf16[512,256]{1,0:T(8,128)(2,1)S(1)} %collective-permute-done.7.refs_4_), channel_id=1, source_target_pairs={{8,16},{10,18},{12,20},{14,22},{16,8},{18,10},{20,12},{22,14},{9,1... | collective-permute-start | bytes 786440 | tf_op jit(solution)/shard_map/ppermute | solution.py:270
  24.0 0.1 reshape_squeeze.12
  24.0 0.1 reshape_squeeze.13
  24.1 0.1 convert_reduce_fusion
  24.2 0.0 copy-done.2
  24.2 0.0 copy-done.3
  24.3 0.1 concatenate.33.slots_ref.slot_rows
  24.3 0.0 copy-start
  24.3 3.1 %collective-permute-done.5.refs_3_.refs_0_ = bf16[1024,256]{1,0:T(8,128)(2,1)S(1)} collective-permute-done((bf16[1024,256]{1,0:T(8,128)(2,1)S(1)}, bf16[1024,256]{1,0:T(8,128)(2,1)S(1)}, u32[]{:S(2)}, u32[]{:S(2)}) %collective-permute-start.5) | collective-permute-done | bytes 524320 | tf_op jit(solution)/shard_map/ppermute | solution.py:270
  27.4 2.9 %collective-permute-done.6.refs_5_.refs_2_ = bf16[1024,256]{1,0:T(8,128)(2,1)S(1)} collective-permute-done((bf16[1024,256]{1,0:T(8,128)(2,1)S(1)}, bf16[1024,256]{1,0:T(8,128)(2,1)S(1)}, u32[]{:S(2)}, u32[]{:S(2)}) %collective-permute-start.6) | collective-permute-done | bytes 524320 | tf_op jit(solution)/shard_map/ppermute | solution.py:270
  30.3 1.7 %shard_map.65.before = f32[2048,256]{1,0:T(8,128)S(1)} custom-call(s32[325]{0:T(512)S(1)} %concatenate.33.slots_ref.slot_rows, bf16[512,256]{1,0:T(8,128)(2,1)S(1)} %collective-permute-done.2.refs_0_, bf16[512,256]{1,0:T(8,128)(2,1)S(1)} %pad_maximum_fusion.3.refs_1_, bf16[512,256]{1,0:T(8,128)(2,1)S(1)} %collective-permute-done.3.refs_2_, ...), custom_call_target="tpu_custom_call" | custom-call | tf_op jit(solution)/shard_map/pallas_call | solution.py:330
  32.0 1.0 %collective-permute-done.8.refs_3_ = bf16[512,256]{1,0:T(8,128)(2,1)S(1)} collective-permute-done((bf16[512,256]{1,0:T(8,128)(2,1)S(1)}, bf16[512,256]{1,0:T(8,128)(2,1)S(1)}, u32[]{:S(2)}, u32[]{:S(2)}) %collective-permute-start.8) | collective-permute-done | bytes 262176 | tf_op jit(solution)/shard_map/ppermute | solution.py:270
  33.1 2.9 %collective-permute-done.9.refs_5_ = bf16[512,256]{1,0:T(8,128)(2,1)S(1)} collective-permute-done((bf16[512,256]{1,0:T(8,128)(2,1)S(1)}, bf16[512,256]{1,0:T(8,128)(2,1)S(1)}, u32[]{:S(2)}, u32[]{:S(2)}) %collective-permute-start.9) | collective-permute-done | bytes 262176 | tf_op jit(solution)/shard_map/ppermute | solution.py:270
  36.0 0.0 copy-done
  36.0 2.3 %shard_map.66 = bf16[4,512,128]{2,1,0:T(8,128)(2,1)S(1)} custom-call(s32[325]{0:T(512)S(1)} %concatenate.33.slots_ref.slot_rows, f32[2048,256]{1,0:T(8,128)S(1)} %shard_map.65.before, bf16[256,256]{1,0:T(8,128)(2,1)S(1)} %copy-done, bf16[1024,256]{1,0:T(8,128)(2,1)S(1)} %collective-permute-done.5.refs_3_.refs_0_, ...), custom_call_target="tpu_custom_call" | custom-call | tf_op jit(solution)/shard_map/pallas_call | solution.py:343
  38.3 13.8 %all_to_all.5.refs_0_ = bf16[8,256,128]{2,1,0:T(8,128)(2,1)S(1)} all-to-all(bf16[8,256,128]{2,1,0:T(8,128)(2,1)S(1)} %bitcast.32), channel_id=1, replica_groups={{0,1,2,3,4,5,6,7},{8,9,10,11,12,13,14,15},{16,17,18,19,20,21,22,23},{24..., dimensions={0} | all-to-all | bytes 1048576 | tf_op jit(solution)/shard_map/all_to_all | solution.py:362
  52.1 1.7 %shard_map.67 = f32[16,128,128]{2,1,0:T(8,128)} custom-call(s32[325]{0:T(512)S(1)} %concatenate.33.slots_ref.slot_rows, bf16[8,256,128]{2,1,0:T(8,128)(2,1)S(1)} %all_to_all.5.refs_0_), custom_call_target="tpu_custom_call" | custom-call | tf_op jit(solution)/shard_map/pallas_call | solution.py:364
  (23 shorter events, 0.4 us)
Async XLA Ops:
  0.7 2.4 %copy-start.1 = (s32[32,2]{0,1:T(2,128)S(1)}, s32[32,2]{0,1:T(2,128)}, u32[]{:S(2)}) copy-start(s32[32,2]{0,1:T(2,128)} %param.7) | copy-start | bytes 772
  3.2 2.3 %collective-permute-start = (bf16[1040,256]{1,0:T(8,128)(2,1)S(1)}, bf16[1040,256]{1,0:T(8,128)(2,1)S(1)}, u32[]{:S(2)}, u32[]{:S(2)}) collective-permute-start(bf16[1040,256]{1,0:T(8,128)(2,1)S(1)} %pad_maximum_fusion), channel_id=1, source_target_pairs={{0,2},{1,3},{2,0},{3,1},{4,6},{5,7},{6,4},{7,5},{8,10},{9,11},{10,... | collective-permute-start | bytes 1597448 | tf_op jit(solution)/shard_map/ppermute | solution.py:266
  5.6 7.6 %collective-permute-start.4 = (bf16[512,256]{1,0:T(8,128)(2,1)S(1)}, bf16[512,256]{1,0:T(8,128)(2,1)S(1)}, u32[]{:S(2)}, u32[]{:S(2)}) collective-permute-start(bf16[512,256]{1,0:T(8,128)(2,1)S(1)} %pad_maximum_fusion.4), channel_id=1, source_target_pairs={{0,1},{1,0},{2,3},{3,2},{4,5},{5,4},{6,7},{7,6},{8,9},{9,8},{10,11... | collective-permute-start | bytes 786440 | tf_op jit(solution)/shard_map/ppermute | solution.py:266
  6.9 8.4 %collective-permute-start.1 = (bf16[544,256]{1,0:T(8,128)(2,1)S(1)}, bf16[544,256]{1,0:T(8,128)(2,1)S(1)}, u32[]{:S(2)}, u32[]{:S(2)}) collective-permute-start(bf16[544,256]{1,0:T(8,128)(2,1)S(1)} %pad_maximum_fusion.2), channel_id=1, source_target_pairs={{0,4},{1,5},{2,6},{3,7},{4,0},{5,1},{6,2},{7,3},{8,12},{9,13},{10,... | collective-permute-start | bytes 835592 | tf_op jit(solution)/shard_map/ppermute | solution.py:266
  8.2 10.6 %collective-permute-start.2 = (bf16[512,256]{1,0:T(8,128)(2,1)S(1)}, bf16[512,256]{1,0:T(8,128)(2,1)S(1)}, u32[]{:S(2)}, u32[]{:S(2)}) collective-permute-start(bf16[512,256]{1,0:T(8,128)(2,1)S(1)} %pad_maximum_fusion.3.refs_1_), channel_id=1, source_target_pairs={{0,8},{2,10},{4,12},{6,14},{8,0},{10,2},{12,4},{14,6},{16,24},{18,... | collective-permute-start | bytes 786440 | tf_op jit(solution)/shard_map/ppermute | solution.py:270
  9.6 9.2 %collective-permute-start.3 = (bf16[512,256]{1,0:T(8,128)(2,1)S(1)}, bf16[512,256]{1,0:T(8,128)(2,1)S(1)}, u32[]{:S(2)}, u32[]{:S(2)}) collective-permute-start(bf16[512,256]{1,0:T(8,128)(2,1)S(1)} %pad_maximum_fusion.3.refs_1_), channel_id=1, source_target_pairs={{8,16},{10,18},{12,20},{14,22},{16,8},{18,10},{20,12},{22,14},{9,1... | collective-permute-start | bytes 786440 | tf_op jit(solution)/shard_map/ppermute | solution.py:270
  11.5 12.7 %copy-start.2 = (s32[32]{0:T(128)S(1)}, s32[32]{0:T(128)}, u32[]{:S(2)}) copy-start(s32[32]{0:T(128)} %param.8) | copy-start | bytes 388
  11.5 12.7 %copy-start.3 = (s32[32]{0:T(128)S(1)}, s32[32]{0:T(128)}, u32[]{:S(2)}) copy-start(s32[32]{0:T(128)} %param.9) | copy-start | bytes 388
  13.2 7.5 %collective-permute-start.7 = (bf16[512,256]{1,0:T(8,128)(2,1)S(1)}, bf16[512,256]{1,0:T(8,128)(2,1)S(1)}, u32[]{:S(2)}, u32[]{:S(2)}) collective-permute-start(bf16[512,256]{1,0:T(8,128)(2,1)S(1)} %pad_maximum_fusion.5), channel_id=1, source_target_pairs={{0,5},{1,4},{2,7},{3,6},{4,1},{5,0},{6,3},{7,2},{8,13},{9,12},{10,... | collective-permute-start | bytes 786440 | tf_op jit(solution)/shard_map/ppermute | solution.py:266
  15.4 12.0 %collective-permute-start.5 = (bf16[1024,256]{1,0:T(8,128)(2,1)S(1)}, bf16[1024,256]{1,0:T(8,128)(2,1)S(1)}, u32[]{:S(2)}, u32[]{:S(2)}) collective-permute-start(bf16[1024,256]{1,0:T(8,128)(2,1)S(1)} %pad_maximum_fusion.1.refs_4_.refs_1_), channel_id=1, source_target_pairs={{0,8},{2,10},{4,12},{6,14},{8,0},{10,2},{12,4},{14,6},{16,24},{18,... | collective-permute-start | bytes 1572872 | tf_op jit(solution)/shard_map/ppermute | solution.py:270
  16.8 13.5 %collective-permute-start.6 = (bf16[1024,256]{1,0:T(8,128)(2,1)S(1)}, bf16[1024,256]{1,0:T(8,128)(2,1)S(1)}, u32[]{:S(2)}, u32[]{:S(2)}) collective-permute-start(bf16[1024,256]{1,0:T(8,128)(2,1)S(1)} %pad_maximum_fusion.1.refs_4_.refs_1_), channel_id=1, source_target_pairs={{8,16},{10,18},{12,20},{14,22},{16,8},{18,10},{20,12},{22,14},{9,1... | collective-permute-start | bytes 1572872 | tf_op jit(solution)/shard_map/ppermute | solution.py:270
  20.7 12.4 %collective-permute-start.8 = (bf16[512,256]{1,0:T(8,128)(2,1)S(1)}, bf16[512,256]{1,0:T(8,128)(2,1)S(1)}, u32[]{:S(2)}, u32[]{:S(2)}) collective-permute-start(bf16[512,256]{1,0:T(8,128)(2,1)S(1)} %collective-permute-done.7.refs_4_), channel_id=1, source_target_pairs={{0,8},{2,10},{4,12},{6,14},{8,0},{10,2},{12,4},{14,6},{16,24},{18,... | collective-permute-start | bytes 786440 | tf_op jit(solution)/shard_map/ppermute | solution.py:270
  22.0 14.0 %collective-permute-start.9 = (bf16[512,256]{1,0:T(8,128)(2,1)S(1)}, bf16[512,256]{1,0:T(8,128)(2,1)S(1)}, u32[]{:S(2)}, u32[]{:S(2)}) collective-permute-start(bf16[512,256]{1,0:T(8,128)(2,1)S(1)} %collective-permute-done.7.refs_4_), channel_id=1, source_target_pairs={{8,16},{10,18},{12,20},{14,22},{16,8},{18,10},{20,12},{22,14},{9,1... | collective-permute-start | bytes 786440 | tf_op jit(solution)/shard_map/ppermute | solution.py:270
  24.3 11.6 %copy-start = (bf16[256,256]{1,0:T(8,128)(2,1)S(1)}, bf16[256,256]{1,0:T(8,128)(2,1)}, u32[]{:S(2)}) copy-start(bf16[256,256]{1,0:T(8,128)(2,1)} %constant.90.clone.table) | copy-start | bytes 393220

commit v8 on v7

--- a/solution.py
+++ b/solution.py
@@ -78,6 +78,12 @@
         scale = lax.rsqrt(power + 0.1 * level + 1e-06)
         return jnp.concatenate([real_part * scale, imag_part * scale], axis=1)
 
+    halves = near // 2
+
+    def place(number):
+        half, core, win = number // (2 * wins), number // wins % 2, number % wins
+        return (core * halves + half) * wins + win
+
     together = max(2, 16 // width)
     for s in range(0, segments, together):
         for k in range(together):
@@ -88,7 +94,7 @@
                 tile = [v[part * width : (part + 1) * width] for v in values]
                 tile = jnp.concatenate(tile, axis=0) if together > 1 else tile[0]
                 spot = pl.ds((block * segments + s) * width, together * width)
-                number = jnp.bitwise_xor(mine, part) if cut > 1 else 0
+                number = place(jnp.bitwise_xor(mine, part)) if cut > 1 else 0
                 out_ref[number, spot, :] = tile.astype(jnp.bfloat16)
 
 
@@ -117,7 +123,9 @@
     mine = lax.axis_index("chan") % near * wins + lax.axis_index("win")
     split = out.reshape(blocks, segments, parts, width, 2 * F)
     split = split.transpose(2, 0, 1, 3, 4).reshape(parts, rows // parts, 2 * F)
-    return jnp.take(split, jnp.bitwise_xor(mine, jnp.arange(parts)), axis=0)
+    split = jnp.take(split, jnp.bitwise_xor(mine, jnp.arange(parts)), axis=0)
+    split = split.reshape(near // 2, 2, wins * rows // parts, 2 * F).transpose(1, 0, 2, 3)
+    return split.reshape(parts, rows // parts, 2 * F)
 
 
 def gather(moves, held, sem, others=()):
@@ -283,8 +291,8 @@
     note = jnp.where(jnp.arange(NOTE_ROWS)[:, None] == 2, slot_count[0], note).astype(jnp.bfloat16)
 
     split = whitened_parts(records, near, wins)
-    split = split.reshape(halves, 2, wins, size, 2 * F)
-    sent = split[:, 1].reshape(halves * wins * size, 2 * F)
+    split = split.reshape(2, halves, wins, size, 2 * F)
+    sent = split[1].reshape(halves * wins * size, 2 * F)
     other = partner(jnp.concatenate([sent, note], axis=0), wins)
     other_note = other[halves * wins * size :]
     other = other[: halves * wins * size].reshape(halves, wins, size, 2 * F)
@@ -292,7 +300,7 @@
     order = [(w, h) for w in range(wins) for h in range(halves)]
     own, notes = [], []
     for w, h in order:
-        piece = [split[h, 0, w], other[h, w]] + ([note, other_note] if w == 0 else [])
+        piece = [split[0, h, w], other[h, w]] + ([note, other_note] if w == 0 else [])
         piece = jnp.concatenate(piece, axis=0)
         if (w, h) == order[-1]:
             piece = after(piece, own[2])

time: 54.4 us -> 54.6 us (level)
  transfers between devices with their start and end apart: 10 -> 10, of which waited for: 7 -> 7; matrix products, arithmetic and copies ran while one was open for 1% -> 1% of each run, Pallas kernels for 3% -> 4%
where the time goes in v8:
time: 54.6 us; the launch traced here: 54 us
  starting transfers between devices  15.2 us (28%)
  waiting for transfers between devices  14.8 us (27%)
  blocking collectives  13.8 us (25%)
  Pallas kernels  8.48 us (16%)
  between operations  0.89 us (2%)
    all_to_all x1, blocking collectives, per_device(): lax.all_to_all(lagged, both, 0, 0, axis_index_groups=groups, tiled=True)  13.8 us
    ppermute x6, starting transfers between devices, along(): return lax.ppermute(block, 'chan', [r for r in route if 0 <= r[1] < chans])  9.74 us
    ppermute x6, waiting for transfers between devices, along(): return lax.ppermute(block, 'chan', [r for r in route if 0 <= r[1] < chans])  9.72 us
    ppermute x4, starting transfers between devices, partner(): lax.ppermute(block, both, [(i, i ^ distance) for i in range(chans * wins)])  5.45 us
    ppermute x4, waiting for transfers between devices, partner(): lax.ppermute(block, both, [(i, i ^ distance) for i in range(chans * wins)])  5.06 us
    pallas_call x1, Pallas kernels, per_device(): pl.pallas_call(functools.partial(last_kernel, near, fold, wins - 1, size,...  2.54 us
    pallas_call x1, Pallas kernels, whitened_parts(): pl.pallas_call(functools.partial(spectra_kernel, near, wins), in_specs=[h...  2.35 us
    pallas_call x1, Pallas kernels, per_device(): pl.pallas_call(functools.partial(first_kernel, near, fold, size, rows), i...  1.9 us
  transfers between devices with their start and end apart: 10, of which 7 were waited for; matrix products, arithmetic and copies ran while one was open for 1% of the time, Pallas kernels for 4%

profile of v8, /device:TPU:17, one launch (start us, length us, event | category | flops | bytes accessed | tf_op | source)
XLA Modules:
  0.0 54.0 jit_solution(18413504266730256920)
XLA Ops:
  0.7 0.0 copy-start.1
  0.7 2.4 %shard_map.64 = bf16[8,256,256]{2,1,0:T(8,128)(2,1)S(1)} custom-call(bf16[4,512,512]{2,1,0:T(8,128)(2,1)} %records.1), custom_call_target="tpu_custom_call" | custom-call | tf_op jit(solution)/shard_map/pallas_call | solution.py:109
  3.1 0.0 copy-done.1
  3.1 0.1 select_convert_fusion
  3.2 0.7 %collective-permute-start = (bf16[1040,256]{1,0:T(8,128)(2,1)S(1)}, bf16[1040,256]{1,0:T(8,128)(2,1)S(1)}, u32[]{:S(2)}, u32[]{:S(2)}) collective-permute-start(bf16[1040,256]{1,0:T(8,128)(2,1)S(1)} %pad_maximum_fusion), channel_id=1, source_target_pairs={{0,2},{1,3},{2,0},{3,1},{4,6},{5,7},{6,4},{7,5},{8,10},{9,11},{10,... | collective-permute-start | bytes 1597448 | tf_op jit(solution)/shard_map/ppermute | solution.py:274
  4.0 1.5 %collective-permute-done = bf16[1040,256]{1,0:T(8,128)(2,1)S(1)} collective-permute-done((bf16[1040,256]{1,0:T(8,128)(2,1)S(1)}, bf16[1040,256]{1,0:T(8,128)(2,1)S(1)}, u32[]{:S(2)}, u32[]{:S(2)}) %collective-permute-start) | collective-permute-done | bytes 532512 | tf_op jit(solution)/shard_map/ppermute | solution.py:274
  5.6 1.3 %collective-permute-start.4 = (bf16[512,256]{1,0:T(8,128)(2,1)S(1)}, bf16[512,256]{1,0:T(8,128)(2,1)S(1)}, u32[]{:S(2)}, u32[]{:S(2)}) collective-permute-start(bf16[512,256]{1,0:T(8,128)(2,1)S(1)} %pad_maximum_fusion.4), channel_id=1, source_target_pairs={{0,1},{1,0},{2,3},{3,2},{4,5},{5,4},{6,7},{7,6},{8,9},{9,8},{10,11... | collective-permute-start | bytes 786440 | tf_op jit(solution)/shard_map/ppermute | solution.py:274
  6.9 1.3 %collective-permute-start.1 = (bf16[544,256]{1,0:T(8,128)(2,1)S(1)}, bf16[544,256]{1,0:T(8,128)(2,1)S(1)}, u32[]{:S(2)}, u32[]{:S(2)}) collective-permute-start(bf16[544,256]{1,0:T(8,128)(2,1)S(1)} %pad_maximum_fusion.2), channel_id=1, source_target_pairs={{0,4},{1,5},{2,6},{3,7},{4,0},{5,1},{6,2},{7,3},{8,12},{9,13},{10,... | collective-permute-start | bytes 835592 | tf_op jit(solution)/shard_map/ppermute | solution.py:274
  8.2 1.4 %collective-permute-start.2 = (bf16[512,256]{1,0:T(8,128)(2,1)S(1)}, bf16[512,256]{1,0:T(8,128)(2,1)S(1)}, u32[]{:S(2)}, u32[]{:S(2)}) collective-permute-start(bf16[512,256]{1,0:T(8,128)(2,1)S(1)} %pad_maximum_fusion.3.refs_1_), channel_id=1, source_target_pairs={{0,8},{2,10},{4,12},{6,14},{8,0},{10,2},{12,4},{14,6},{16,24},{18,... | collective-permute-start | bytes 786440 | tf_op jit(solution)/shard_map/ppermute | solution.py:278
  9.6 1.9 %collective-permute-start.3 = (bf16[512,256]{1,0:T(8,128)(2,1)S(1)}, bf16[512,256]{1,0:T(8,128)(2,1)S(1)}, u32[]{:S(2)}, u32[]{:S(2)}) collective-permute-start(bf16[512,256]{1,0:T(8,128)(2,1)S(1)} %pad_maximum_fusion.3.refs_1_), channel_id=1, source_target_pairs={{8,16},{10,18},{12,20},{14,22},{16,8},{18,10},{20,12},{22,14},{9,1... | collective-permute-start | bytes 786440 | tf_op jit(solution)/shard_map/ppermute | solution.py:278
  11.5 0.0 copy-start.2
  11.5 0.0 copy-start.3
  11.6 1.6 %collective-permute-done.4 = bf16[512,256]{1,0:T(8,128)(2,1)S(1)} collective-permute-done((bf16[512,256]{1,0:T(8,128)(2,1)S(1)}, bf16[512,256]{1,0:T(8,128)(2,1)S(1)}, u32[]{:S(2)}, u32[]{:S(2)}) %collective-permute-start.4) | collective-permute-done | bytes 262176 | tf_op jit(solution)/shard_map/ppermute | solution.py:274
  13.2 2.1 %collective-permute-start.7 = (bf16[512,256]{1,0:T(8,128)(2,1)S(1)}, bf16[512,256]{1,0:T(8,128)(2,1)S(1)}, u32[]{:S(2)}, u32[]{:S(2)}) collective-permute-start(bf16[512,256]{1,0:T(8,128)(2,1)S(1)} %pad_maximum_fusion.5), channel_id=1, source_target_pairs={{0,5},{1,4},{2,7},{3,6},{4,1},{5,0},{6,3},{7,2},{8,13},{9,12},{10,... | collective-permute-start | bytes 786440 | tf_op jit(solution)/shard_map/ppermute | solution.py:274
  15.4 0.0 collective-permute-done.1
  15.4 1.4 %collective-permute-start.5 = (bf16[1024,256]{1,0:T(8,128)(2,1)S(1)}, bf16[1024,256]{1,0:T(8,128)(2,1)S(1)}, u32[]{:S(2)}, u32[]{:S(2)}) collective-permute-start(bf16[1024,256]{1,0:T(8,128)(2,1)S(1)} %pad_maximum_fusion.1.refs_4_.refs_1_), channel_id=1, source_target_pairs={{0,8},{2,10},{4,12},{6,14},{8,0},{10,2},{12,4},{14,6},{16,24},{18,... | collective-permute-start | bytes 1572872 | tf_op jit(solution)/shard_map/ppermute | solution.py:278
  16.8 1.9 %collective-permute-start.6 = (bf16[1024,256]{1,0:T(8,128)(2,1)S(1)}, bf16[1024,256]{1,0:T(8,128)(2,1)S(1)}, u32[]{:S(2)}, u32[]{:S(2)}) collective-permute-start(bf16[1024,256]{1,0:T(8,128)(2,1)S(1)} %pad_maximum_fusion.1.refs_4_.refs_1_), channel_id=1, source_target_pairs={{8,16},{10,18},{12,20},{14,22},{16,8},{18,10},{20,12},{22,14},{9,1... | collective-permute-start | bytes 1572872 | tf_op jit(solution)/shard_map/ppermute | solution.py:278
  18.8 0.0 collective-permute-done.2.refs_0_
  18.8 0.0 collective-permute-done.3.refs_2_
  18.8 1.9 %collective-permute-done.7.refs_4_ = bf16[512,256]{1,0:T(8,128)(2,1)S(1)} collective-permute-done((bf16[512,256]{1,0:T(8,128)(2,1)S(1)}, bf16[512,256]{1,0:T(8,128)(2,1)S(1)}, u32[]{:S(2)}, u32[]{:S(2)}) %collective-permute-start.7) | collective-permute-done | bytes 262176 | tf_op jit(solution)/shard_map/ppermute | solution.py:274
  20.7 1.3 %collective-permute-start.8 = (bf16[512,256]{1,0:T(8,128)(2,1)S(1)}, bf16[512,256]{1,0:T(8,128)(2,1)S(1)}, u32[]{:S(2)}, u32[]{:S(2)}) collective-permute-start(bf16[512,256]{1,0:T(8,128)(2,1)S(1)} %collective-permute-done.7.refs_4_), channel_id=1, source_target_pairs={{0,8},{2,10},{4,12},{6,14},{8,0},{10,2},{12,4},{14,6},{16,24},{18,... | collective-permute-start | bytes 786440 | tf_op jit(solution)/shard_map/ppermute | solution.py:278
  22.0 1.9 %collective-permute-start.9 = (bf16[512,256]{1,0:T(8,128)(2,1)S(1)}, bf16[512,256]{1,0:T(8,128)(2,1)S(1)}, u32[]{:S(2)}, u32[]{:S(2)}) collective-permute-start(bf16[512,256]{1,0:T(8,128)(2,1)S(1)} %collective-permute-done.7.refs_4_), channel_id=1, source_target_pairs={{8,16},{10,18},{12,20},{14,22},{16,8},{18,10},{20,12},{22,14},{9,1... | collective-permute-start | bytes 786440 | tf_op jit(solution)/shard_map/ppermute | solution.py:278
  24.0 0.1 reshape_squeeze.12
  24.0 0.1 reshape_squeeze.13
  24.1 0.1 convert_reduce_fusion
  24.2 0.0 copy-done.2
  24.2 0.0 copy-done.3
  24.3 0.1 concatenate.33.slots_ref.slot_rows
  24.3 0.0 copy-start
  24.3 3.1 %collective-permute-done.5.refs_3_.refs_0_ = bf16[1024,256]{1,0:T(8,128)(2,1)S(1)} collective-permute-done((bf16[1024,256]{1,0:T(8,128)(2,1)S(1)}, bf16[1024,256]{1,0:T(8,128)(2,1)S(1)}, u32[]{:S(2)}, u32[]{:S(2)}) %collective-permute-start.5) | collective-permute-done | bytes 524320 | tf_op jit(solution)/shard_map/ppermute | solution.py:278
  27.4 2.9 %collective-permute-done.6.refs_5_.refs_2_ = bf16[1024,256]{1,0:T(8,128)(2,1)S(1)} collective-permute-done((bf16[1024,256]{1,0:T(8,128)(2,1)S(1)}, bf16[1024,256]{1,0:T(8,128)(2,1)S(1)}, u32[]{:S(2)}, u32[]{:S(2)}) %collective-permute-start.6) | collective-permute-done | bytes 524320 | tf_op jit(solution)/shard_map/ppermute | solution.py:278
  30.3 1.9 %shard_map.65.before = f32[2048,256]{1,0:T(8,128)S(1)} custom-call(s32[325]{0:T(512)S(1)} %concatenate.33.slots_ref.slot_rows, bf16[512,256]{1,0:T(8,128)(2,1)S(1)} %collective-permute-done.2.refs_0_, bf16[512,256]{1,0:T(8,128)(2,1)S(1)} %pad_maximum_fusion.3.refs_1_, bf16[512,256]{1,0:T(8,128)(2,1)S(1)} %collective-permute-done.3.refs_2_, ...), custom_call_target="tpu_custom_call" | custom-call | tf_op jit(solution)/shard_map/pallas_call | solution.py:338
  32.3 0.8 %collective-permute-done.8.refs_3_ = bf16[512,256]{1,0:T(8,128)(2,1)S(1)} collective-permute-done((bf16[512,256]{1,0:T(8,128)(2,1)S(1)}, bf16[512,256]{1,0:T(8,128)(2,1)S(1)}, u32[]{:S(2)}, u32[]{:S(2)}) %collective-permute-start.8) | collective-permute-done | bytes 262176 | tf_op jit(solution)/shard_map/ppermute | solution.py:278
  33.1 2.9 %collective-permute-done.9.refs_5_ = bf16[512,256]{1,0:T(8,128)(2,1)S(1)} collective-permute-done((bf16[512,256]{1,0:T(8,128)(2,1)S(1)}, bf16[512,256]{1,0:T(8,128)(2,1)S(1)}, u32[]{:S(2)}, u32[]{:S(2)}) %collective-permute-start.9) | collective-permute-done | bytes 262176 | tf_op jit(solution)/shard_map/ppermute | solution.py:278
  36.0 0.0 copy-done
  36.0 2.5 %shard_map.66 = bf16[4,512,128]{2,1,0:T(8,128)(2,1)S(1)} custom-call(s32[325]{0:T(512)S(1)} %concatenate.33.slots_ref.slot_rows, f32[2048,256]{1,0:T(8,128)S(1)} %shard_map.65.before, bf16[256,256]{1,0:T(8,128)(2,1)S(1)} %copy-done, bf16[1024,256]{1,0:T(8,128)(2,1)S(1)} %collective-permute-done.5.refs_3_.refs_0_, ...), custom_call_target="tpu_custom_call" | custom-call | tf_op jit(solution)/shard_map/pallas_call | solution.py:351
  38.5 13.8 %all_to_all.5.refs_0_ = bf16[8,256,128]{2,1,0:T(8,128)(2,1)S(1)} all-to-all(bf16[8,256,128]{2,1,0:T(8,128)(2,1)S(1)} %bitcast.31), channel_id=1, replica_groups={{0,1,2,3,4,5,6,7},{8,9,10,11,12,13,14,15},{16,17,18,19,20,21,22,23},{24..., dimensions={0} | all-to-all | bytes 1048576 | tf_op jit(solution)/shard_map/all_to_all | solution.py:370
  52.3 1.7 %shard_map.67 = f32[16,128,128]{2,1,0:T(8,128)} custom-call(s32[325]{0:T(512)S(1)} %concatenate.33.slots_ref.slot_rows, bf16[8,256,128]{2,1,0:T(8,128)(2,1)S(1)} %all_to_all.5.refs_0_), custom_call_target="tpu_custom_call" | custom-call | tf_op jit(solution)/shard_map/pallas_call | solution.py:372
  (23 shorter events, 0.4 us)
Async XLA Ops:
  0.7 2.4 %copy-start.1 = (s32[32,2]{0,1:T(2,128)S(1)}, s32[32,2]{0,1:T(2,128)}, u32[]{:S(2)}) copy-start(s32[32,2]{0,1:T(2,128)} %param.7) | copy-start | bytes 772
  3.2 2.3 %collective-permute-start = (bf16[1040,256]{1,0:T(8,128)(2,1)S(1)}, bf16[1040,256]{1,0:T(8,128)(2,1)S(1)}, u32[]{:S(2)}, u32[]{:S(2)}) collective-permute-start(bf16[1040,256]{1,0:T(8,128)(2,1)S(1)} %pad_maximum_fusion), channel_id=1, source_target_pairs={{0,2},{1,3},{2,0},{3,1},{4,6},{5,7},{6,4},{7,5},{8,10},{9,11},{10,... | collective-permute-start | bytes 1597448 | tf_op jit(solution)/shard_map/ppermute | solution.py:274
  5.6 7.6 %collective-permute-start.4 = (bf16[512,256]{1,0:T(8,128)(2,1)S(1)}, bf16[512,256]{1,0:T(8,128)(2,1)S(1)}, u32[]{:S(2)}, u32[]{:S(2)}) collective-permute-start(bf16[512,256]{1,0:T(8,128)(2,1)S(1)} %pad_maximum_fusion.4), channel_id=1, source_target_pairs={{0,1},{1,0},{2,3},{3,2},{4,5},{5,4},{6,7},{7,6},{8,9},{9,8},{10,11... | collective-permute-start | bytes 786440 | tf_op jit(solution)/shard_map/ppermute | solution.py:274
  6.9 8.4 %collective-permute-start.1 = (bf16[544,256]{1,0:T(8,128)(2,1)S(1)}, bf16[544,256]{1,0:T(8,128)(2,1)S(1)}, u32[]{:S(2)}, u32[]{:S(2)}) collective-permute-start(bf16[544,256]{1,0:T(8,128)(2,1)S(1)} %pad_maximum_fusion.2), channel_id=1, source_target_pairs={{0,4},{1,5},{2,6},{3,7},{4,0},{5,1},{6,2},{7,3},{8,12},{9,13},{10,... | collective-permute-start | bytes 835592 | tf_op jit(solution)/shard_map/ppermute | solution.py:274
  8.2 10.6 %collective-permute-start.2 = (bf16[512,256]{1,0:T(8,128)(2,1)S(1)}, bf16[512,256]{1,0:T(8,128)(2,1)S(1)}, u32[]{:S(2)}, u32[]{:S(2)}) collective-permute-start(bf16[512,256]{1,0:T(8,128)(2,1)S(1)} %pad_maximum_fusion.3.refs_1_), channel_id=1, source_target_pairs={{0,8},{2,10},{4,12},{6,14},{8,0},{10,2},{12,4},{14,6},{16,24},{18,... | collective-permute-start | bytes 786440 | tf_op jit(solution)/shard_map/ppermute | solution.py:278
  9.6 9.2 %collective-permute-start.3 = (bf16[512,256]{1,0:T(8,128)(2,1)S(1)}, bf16[512,256]{1,0:T(8,128)(2,1)S(1)}, u32[]{:S(2)}, u32[]{:S(2)}) collective-permute-start(bf16[512,256]{1,0:T(8,128)(2,1)S(1)} %pad_maximum_fusion.3.refs_1_), channel_id=1, source_target_pairs={{8,16},{10,18},{12,20},{14,22},{16,8},{18,10},{20,12},{22,14},{9,1... | collective-permute-start | bytes 786440 | tf_op jit(solution)/shard_map/ppermute | solution.py:278
  11.5 12.7 %copy-start.2 = (s32[32]{0:T(128)S(1)}, s32[32]{0:T(128)}, u32[]{:S(2)}) copy-start(s32[32]{0:T(128)} %param.8) | copy-start | bytes 388
  11.5 12.7 %copy-start.3 = (s32[32]{0:T(128)S(1)}, s32[32]{0:T(128)}, u32[]{:S(2)}) copy-start(s32[32]{0:T(128)} %param.9) | copy-start | bytes 388
  13.2 7.5 %collective-permute-start.7 = (bf16[512,256]{1,0:T(8,128)(2,1)S(1)}, bf16[512,256]{1,0:T(8,128)(2,1)S(1)}, u32[]{:S(2)}, u32[]{:S(2)}) collective-permute-start(bf16[512,256]{1,0:T(8,128)(2,1)S(1)} %pad_maximum_fusion.5), channel_id=1, source_target_pairs={{0,5},{1,4},{2,7},{3,6},{4,1},{5,0},{6,3},{7,2},{8,13},{9,12},{10,... | collective-permute-start | bytes 786440 | tf_op jit(solution)/shard_map/ppermute | solution.py:274
  15.4 12.0 %collective-permute-start.5 = (bf16[1024,256]{1,0:T(8,128)(2,1)S(1)}, bf16[1024,256]{1,0:T(8,128)(2,1)S(1)}, u32[]{:S(2)}, u32[]{:S(2)}) collective-permute-start(bf16[1024,256]{1,0:T(8,128)(2,1)S(1)} %pad_maximum_fusion.1.refs_4_.refs_1_), channel_id=1, source_target_pairs={{0,8},{2,10},{4,12},{6,14},{8,0},{10,2},{12,4},{14,6},{16,24},{18,... | collective-permute-start | bytes 1572872 | tf_op jit(solution)/shard_map/ppermute | solution.py:278
  16.8 13.5 %collective-permute-start.6 = (bf16[1024,256]{1,0:T(8,128)(2,1)S(1)}, bf16[1024,256]{1,0:T(8,128)(2,1)S(1)}, u32[]{:S(2)}, u32[]{:S(2)}) collective-permute-start(bf16[1024,256]{1,0:T(8,128)(2,1)S(1)} %pad_maximum_fusion.1.refs_4_.refs_1_), channel_id=1, source_target_pairs={{8,16},{10,18},{12,20},{14,22},{16,8},{18,10},{20,12},{22,14},{9,1... | collective-permute-start | bytes 1572872 | tf_op jit(solution)/shard_map/ppermute | solution.py:278
  20.7 12.4 %collective-permute-start.8 = (bf16[512,256]{1,0:T(8,128)(2,1)S(1)}, bf16[512,256]{1,0:T(8,128)(2,1)S(1)}, u32[]{:S(2)}, u32[]{:S(2)}) collective-permute-start(bf16[512,256]{1,0:T(8,128)(2,1)S(1)} %collective-permute-done.7.refs_4_), channel_id=1, source_target_pairs={{0,8},{2,10},{4,12},{6,14},{8,0},{10,2},{12,4},{14,6},{16,24},{18,... | collective-permute-start | bytes 786440 | tf_op jit(solution)/shard_map/ppermute | solution.py:278
  22.0 14.0 %collective-permute-start.9 = (bf16[512,256]{1,0:T(8,128)(2,1)S(1)}, bf16[512,256]{1,0:T(8,128)(2,1)S(1)}, u32[]{:S(2)}, u32[]{:S(2)}) collective-permute-start(bf16[512,256]{1,0:T(8,128)(2,1)S(1)} %collective-permute-done.7.refs_4_), channel_id=1, source_target_pairs={{8,16},{10,18},{12,20},{14,22},{16,8},{18,10},{20,12},{22,14},{9,1... | collective-permute-start | bytes 786440 | tf_op jit(solution)/shard_map/ppermute | solution.py:278
  24.3 11.6 %copy-start = (bf16[256,256]{1,0:T(8,128)(2,1)S(1)}, bf16[256,256]{1,0:T(8,128)(2,1)}, u32[]{:S(2)}) copy-start(bf16[256,256]{1,0:T(8,128)(2,1)} %constant.90.clone.table) | copy-start | bytes 393220
